TPU v7x, 256 devices: a whole 4x4x8 slice. The times are simulated.
256 devices in a mesh: gx: 16 (over x_hi, y, core), gy: 16 (over z, x_lo).
Axes of the slice: x: 4 (x_hi: 2, x_lo: 2; x = x_hi * 2 + x_lo), y: 4, z: 8, core: 2. Of those that a mesh axis runs over, the one named last changes fastest.
Arguments:
- fields: bfloat16 [256, 512, 256], P('gx', 'gy'), may hold values from -6 to 6
- w_down: bfloat16 [3, 3, 3, 32, 32], replicated, may hold values from -0.21875 to 0.21875
- w_pool: bfloat16 [2, 2, 2, 32, 64], replicated, may hold values from -0.375 to 0.375
- w_mid: bfloat16 [3, 3, 3, 64, 64], replicated, may hold values from -0.15625 to 0.15625
- w_unpool: bfloat16 [2, 2, 2, 64, 32], replicated, may hold values from -0.75 to 0.75
- w_up: bfloat16 [3, 3, 3, 32, 32], replicated, may hold values from -0.21875 to 0.21875
- cotangent: bfloat16 [256, 512, 256], P('gx', 'gy'), may hold values from -6 to 6
Outputs:
- output: bfloat16 [256, 512, 256], P('gx', 'gy')
- grad_fields: bfloat16 [256, 512, 256], P('gx', 'gy')
- grad_down: float32 [3, 3, 3, 32, 32], replicated
- grad_pool: float32 [2, 2, 2, 32, 64], replicated
- grad_mid: float32 [3, 3, 3, 64, 64], replicated
- grad_unpool: float32 [2, 2, 2, 64, 32], replicated
- grad_up: float32 [3, 3, 3, 32, 32], replicated
All inputs are finite; a program needn't handle non-finite values.
Results may differ from a plain program's by a relative error of at most 0.0071.
Values may be sent and summed in bfloat16 or wider, within the bound.
No kernel may reach another device: no remote copies, remote signals or barrier semaphores. Data moves between devices by JAX's collectives and lax.ppermute only.
A program may use at most 128 MiB of HBM per device.

v0:
```python
import math

import jax
import jax.numpy as jnp
from jax import lax
from jax.sharding import PartitionSpec as P


def padded_2(block, sides, width):
    for axis, dim in sides:
        count = lax.axis_size(axis)
        forward = [(i, i + 1) for i in range(count - 1)]
        forward.append((count - 1, 0))
        backward = [(target, source) for source, target in forward]
        low = lax.ppermute(
            lax.slice_in_dim(block, block.shape[dim] - width, None, axis=dim), axis, forward
        )
        high = lax.ppermute(lax.slice_in_dim(block, 0, width, axis=dim), axis, backward)
        block = jnp.concatenate([low, block, high], axis=dim)
    return block


def in_one(arrays, axis):
    ends = [0]
    for a in arrays:
        ends.append(ends[-1] + a.size)
    so_far = lax.psum(jnp.concatenate([a.ravel() for a in arrays]), axis)
    return tuple((so_far[b:e].reshape(a.shape) for a, b, e in zip(arrays, ends, ends[1:])))


def dsilu(value):
    sig = jax.nn.sigmoid(value)
    return sig * (1.0 + value * (1.0 - sig))


def plane_shifts(planes):
    return jnp.stack([jnp.eye(planes, k=1 - kk, dtype=jnp.float32) for kk in range(3)])


def band_matrix(weight, planes):
    shifts = plane_shifts(planes)
    band = jnp.einsum("kpz,abkco->abpczo", shifts, weight.astype(jnp.float32))
    return band.reshape(9 * planes * weight.shape[3], planes * weight.shape[4]).astype(jnp.bfloat16)


def band_to_weight(dband, planes, cin, cout):
    shifts = plane_shifts(planes)
    return jnp.einsum("kpz,abpczo->abkco", shifts, dband.reshape(3, 3, planes, cin, planes, cout))


def flipped(weight):
    return jnp.transpose(weight[::-1, ::-1, ::-1], (0, 1, 2, 4, 3))


def fine_rim(field):
    return padded_2(field, (("gx", 0), ("gy", 1)), 1)


def coarse_rim(field):
    return padded_2(field, (("gx", 0), ("gy", 1)), 1)


def columns(padded):
    xs = padded.shape[0] - 2
    ys = padded.shape[1] - 2
    cols = jnp.concatenate(
        [padded[aa : aa + xs, bb : bb + ys, :] for aa in range(3) for bb in range(3)], axis=2
    )
    return cols.reshape(xs * ys, -1)


def conv_padded(padded, band):
    xs = padded.shape[0] - 2
    ys = padded.shape[1] - 2
    return jnp.dot(columns(padded), band, preferred_element_type=jnp.float32).reshape(xs, ys, -1)


def weight_grad(padded, dout, planes, cin, cout):
    flat = dout.reshape(-1, dout.shape[2])
    dband = lax.dot_general(
        columns(padded), flat, (((0,), (0,)), ((), ())), preferred_element_type=jnp.float32
    )
    return band_to_weight(dband, planes, cin, cout)


def split_fine(field):
    xs, ys, width = field.shape
    parts = field.reshape(xs // 2, 2, ys // 2, 2, width).transpose(0, 2, 1, 3, 4)
    return parts.reshape(xs // 2 * (ys // 2), 4 * width)


def merge_fine(flat, xs, ys):
    width = flat.shape[1] // 4
    return (
        flat.reshape(xs // 2, ys // 2, 2, 2, width).transpose(0, 2, 1, 3, 4).reshape(xs, ys, width)
    )


def pool_matrix(weight, half):
    eye = jnp.eye(half, dtype=jnp.float32)
    mat = jnp.einsum("yz,ijlco->ijylczo", eye, weight.astype(jnp.float32))
    return mat.reshape(-1, half * weight.shape[4]).astype(jnp.bfloat16)


def unpool_matrix(weight, half):
    eye = jnp.eye(half, dtype=jnp.float32)
    mat = jnp.einsum("yz,ijlof->yoijzlf", eye, weight.astype(jnp.float32))
    return mat.reshape(half * weight.shape[3], -1).astype(jnp.bfloat16)


def per_device(fields, w_down, w_pool, w_mid, w_unpool, w_up, cotangent):
    cf = w_down.shape[3]
    cc = w_mid.shape[3]
    xs, ys = (fields.shape[0], fields.shape[1])
    width = fields.shape[2]
    planes = width // cf
    half = planes // 2
    pmat = pool_matrix(w_pool, half)
    umat = unpool_matrix(w_unpool, half)
    joined = padded_2(jnp.concatenate((fields, cotangent), axis=2), (("gx", 0), ("gy", 1)), 1)
    fields_pad = joined[:, :, :width]
    cot_pad = joined[:, :, width:]
    pre_down = conv_padded(fields_pad, band_matrix(w_down, planes))
    hidden = jax.nn.silu(pre_down).astype(jnp.bfloat16)
    hidden_parts = split_fine(hidden)
    pre_pool = jnp.dot(hidden_parts, pmat, preferred_element_type=jnp.float32).reshape(
        xs // 2, ys // 2, -1
    )
    coarse = jax.nn.silu(pre_pool).astype(jnp.bfloat16)
    coarse_pad = coarse_rim(coarse)
    pre_mid = conv_padded(coarse_pad, band_matrix(w_mid, half))
    middle = (coarse.astype(jnp.float32) + jax.nn.silu(pre_mid)).astype(jnp.bfloat16)
    middle_flat = middle.reshape(-1, middle.shape[2])
    lifted = jnp.dot(middle_flat, umat, preferred_element_type=jnp.float32)
    pre_up = hidden.astype(jnp.float32) + merge_fine(lifted, xs, ys)
    skip = jax.nn.silu(pre_up).astype(jnp.bfloat16)
    skip_pad = fine_rim(skip)
    output = (fields.astype(jnp.float32) + conv_padded(skip_pad, band_matrix(w_up, planes))).astype(
        jnp.bfloat16
    )
    d_up = (conv_padded(cot_pad, band_matrix(flipped(w_up), planes)) * dsilu(pre_up)).astype(
        jnp.bfloat16
    )
    d_up_parts = split_fine(d_up)
    d_middle = lax.dot_general(
        d_up_parts, umat, (((1,), (1,)), ((), ())), preferred_element_type=jnp.float32
    )
    d_middle = d_middle.reshape(xs // 2, ys // 2, -1)
    d_mid = (d_middle * dsilu(pre_mid)).astype(jnp.bfloat16)
    d_coarse = d_middle + conv_padded(coarse_rim(d_mid), band_matrix(flipped(w_mid), half))
    d_pool = (d_coarse * dsilu(pre_pool)).astype(jnp.bfloat16)
    d_pool_flat = d_pool.reshape(-1, d_pool.shape[2])
    back = lax.dot_general(
        d_pool_flat, pmat, (((1,), (1,)), ((), ())), preferred_element_type=jnp.float32
    )
    d_hidden = d_up.astype(jnp.float32) + merge_fine(back, xs, ys)
    d_down = (d_hidden * dsilu(pre_down)).astype(jnp.bfloat16)
    grad_fields = (
        cotangent.astype(jnp.float32)
        + conv_padded(fine_rim(d_down), band_matrix(flipped(w_down), planes))
    ).astype(jnp.bfloat16)
    part_up = weight_grad(skip_pad, cotangent, planes, cf, cf)
    part_mid = weight_grad(coarse_pad, d_mid, half, cc, cc)
    part_down = weight_grad(fields_pad, d_down, planes, cf, cf)
    eye = jnp.eye(half, dtype=jnp.float32)
    d_umat = lax.dot_general(
        middle_flat, d_up_parts, (((0,), (0,)), ((), ())), preferred_element_type=jnp.float32
    )
    part_unpool = jnp.einsum("yz,yoijzlf->ijlof", eye, d_umat.reshape(half, cc, 2, 2, half, 2, cf))
    d_pmat = lax.dot_general(
        hidden_parts, d_pool_flat, (((0,), (0,)), ((), ())), preferred_element_type=jnp.float32
    )
    part_pool = jnp.einsum("yz,ijylczo->ijlco", eye, d_pmat.reshape(2, 2, half, 2, cf, half, cc))
    summed = in_one((part_down, part_pool, part_mid, part_unpool, part_up), ("gx", "gy"))
    scale = 1.0 / math.sqrt(xs * ys * planes * lax.axis_size("gx") * lax.axis_size("gy"))
    grad_down = summed[0] * scale
    grad_pool = summed[1] * scale
    grad_mid = summed[2] * scale
    grad_unpool = summed[3] * scale
    grad_up = summed[4] * scale
    return (output, grad_fields, grad_down, grad_pool, grad_mid, grad_unpool, grad_up)


def solution(mesh):
    placed = (P("gx", "gy", None), P(), P(), P(), P(), P(), P("gx", "gy", None))
    return jax.shard_map(
        per_device,
        mesh=mesh,
        in_specs=placed,
        out_specs=(P("gx", "gy", None), P("gx", "gy", None), P(), P(), P(), P(), P()),
        check_vma=False,
    )
```

profile of v0, /device:TPU:1, one launch (start us, length us, event | category | flops | bytes accessed | tf_op | source)
XLA Modules:
  0.0 483.6 jit_solution(3323634900499420828)
XLA Ops:
  9.8 2.7 collective-permute-start
  14.9 4.5 convert_bitcast_fusion.3
  19.4 3.7 convert_bitcast_fusion.2
  25.3 3.7 convert_bitcast_fusion.1
  34.2 3.6 convert_bitcast_fusion
  38.8 5.6 %collective-permute-start.3 = (bf16[18,1,512]{2,1,0:T(2,128)(2,1)S(1)}, bf16[18,1,512]{2,1,0:T(2,128)(2,1)S(1)}, u32[]{:S(2)}, u32[]{:S(2)}) collective-permute-start(bf16[18,1,512]{2,1,0:T(2,128)(2,1)S(1)} %get-tuple-element.39), channel_id=1, source_target_pairs={{1,0},{2,1},{3,2},{4,3},{5,4},{6,5},{7,6},{8,7},{9,8},{10,9},{11,1... | collective-permute-start | bytes 55304 | tf_op jit(solution)/shard_map/ppermute | solution.py:18
  45.9 5.0 %copy.61 = bf16[3,3,8,32,8,32]{5,4,3,2,1,0:T(8,128)(2,1)} copy(bf16[3,3,8,32,8,32]{5,4,3,1,0,2:T(8,128)(2,1)} %convert_bitcast_fusion.3) | data formatting | bytes 2359296 | tf_op jit(solution)/shard_map/convert_element_type | solution.py:43
  50.9 6.6 %reshape.315 = bf16[2304,256,1]{1,0,2:T(8,128)(2,1)} reshape(bf16[3,3,8,32,8,32]{5,4,3,2,1,0:T(8,128)(2,1)} %copy.61) | data formatting | bytes 2359296 | tf_op jit(solution)/shard_map/convert_element_type | solution.py:43
  57.5 2.7 reshape.316
  80.8 3.9 collective-permute-start.7
  89.1 4.6 reshape.319
  95.2 5.0 %copy.70 = bf16[3,3,8,32,8,32]{5,4,3,2,1,0:T(8,128)(2,1)} copy(bf16[3,3,8,32,8,32]{5,4,3,1,0,2:T(8,128)(2,1)} %convert_bitcast_fusion.1) | data formatting | bytes 2359296 | tf_op jit(solution)/shard_map/convert_element_type | solution.py:43
  100.2 6.7 %reshape.325 = bf16[2304,256,1]{1,0,2:T(8,128)(2,1)} reshape(bf16[3,3,8,32,8,32]{5,4,3,2,1,0:T(8,128)(2,1)} %copy.70) | data formatting | bytes 2359296 | tf_op jit(solution)/shard_map/convert_element_type | solution.py:43
  109.4 4.6 reshape.328
  115.0 5.1 %copy.77 = bf16[3,3,8,32,8,32]{5,4,3,2,1,0:T(8,128)(2,1)} copy(bf16[3,3,8,32,8,32]{5,4,3,1,0,2:T(8,128)(2,1)} %convert_bitcast_fusion) | data formatting | bytes 2359296 | tf_op jit(solution)/shard_map/convert_element_type | solution.py:43
  120.1 6.6 %reshape.332 = bf16[2304,256,1]{1,0,2:T(8,128)(2,1)} reshape(bf16[3,3,8,32,8,32]{5,4,3,2,1,0:T(8,128)(2,1)} %copy.77) | data formatting | bytes 2359296 | tf_op jit(solution)/shard_map/convert_element_type | solution.py:43
  126.7 5.1 %copy.68 = bf16[3,3,8,32,8,32]{5,4,3,2,1,0:T(8,128)(2,1)} copy(bf16[3,3,8,32,8,32]{5,4,3,1,0,2:T(8,128)(2,1)} %convert_bitcast_fusion.2) | data formatting | bytes 2359296 | tf_op jit(solution)/shard_map/convert_element_type | solution.py:43
  131.8 6.7 %reshape.323 = bf16[2304,256,1]{1,0,2:T(8,128)(2,1)} reshape(bf16[3,3,8,32,8,32]{5,4,3,2,1,0:T(8,128)(2,1)} %copy.68) | data formatting | bytes 2359296 | tf_op jit(solution)/shard_map/convert_element_type | solution.py:43
  138.9 2.6 copy.78
  144.8 2.8 fusion.18
  150.9 3.5 fusion.8
  154.4 5.9 %collective-permute-start.13 = (bf16[1,16,256]{2,1,0:T(8,128)(2,1)S(1)}, bf16[1,16,256]{2,1,0:T(8,128)(2,1)S(1)}, u32[]{:S(2)}, u32[]{:S(2)}) collective-permute-start(bf16[1,16,256]{2,1,0:T(8,128)(2,1)S(1)} %get-tuple-element.68), channel_id=1, source_target_pairs={{16,0},{32,16},{48,32},{64,48},{80,64},{96,80},{112,96},{128,112},... | collective-permute-start | bytes 24584 | tf_op jit(solution)/shard_map/ppermute | solution.py:18
  161.5 3.6 collective-permute-start.15
  168.3 6.4 %collective-permute-start.9 = (bf16[1,32,256]{2,1,0:T(8,128)(2,1)}, bf16[1,32,256]{2,1,0:T(8,128)(2,1)}, u32[]{:S(2)}, u32[]{:S(2)}) collective-permute-start(bf16[1,32,256]{2,1,0:T(8,128)(2,1)} %get-tuple-element.58), channel_id=1, source_target_pairs={{16,0},{32,16},{48,32},{64,48},{80,64},{96,80},{112,96},{128,112},... | collective-permute-start | bytes 49160 | tf_op jit(solution)/shard_map/ppermute | solution.py:18
  183.7 2.8 fusion.59
  188.3 5.4 %collective-permute-start.17 = (bf16[1,32,256]{2,1,0:T(8,128)(2,1)S(1)}, bf16[1,32,256]{2,1,0:T(8,128)(2,1)S(1)}, u32[]{:S(2)}, u32[]{:S(2)}) collective-permute-start(bf16[1,32,256]{2,1,0:T(8,128)(2,1)S(1)} %copy-done.27), channel_id=1, source_target_pairs={{16,0},{32,16},{48,32},{64,48},{80,64},{96,80},{112,96},{128,112},... | collective-permute-start | bytes 49160 | tf_op jit(solution)/shard_map/ppermute | solution.py:18
  194.6 3.8 collective-permute-start.11
  202.5 2.5 copy.91
  205.0 4.5 fusion.62
  213.7 3.6 collective-permute-start.19
  217.4 2.8 fusion.17
  223.1 245.7 %all-reduce.2.cloned.1.call-done = f32[198656]{0:T(1024)} async-done(((f32[198656]{0:T(1024)}), f32[198656]{0:T(1024)}) %all-reduce.2.cloned.1.call-update) | async-done | bytes 794640 | tf_op jit(solution)/shard_map/psum | solution.py:27
  (246 shorter events, 85.7 us)
Async XLA Ops:
  7.2 461.6 %all-reduce.2.cloned.1.call-start = ((), (), s32[]{:S(2)}) async-start(), calls=%async_computation | async-start | bytes 1589248 | tf_op jit(solution)/shard_map/psum | solution.py:27
  9.8 28.1 %collective-permute-start = (bf16[1,32,512]{2,1,0:T(8,128)(2,1)}, bf16[1,32,512]{2,1,0:T(8,128)(2,1)S(1)}, u32[]{:S(2)}, u32[]{:S(2)}) collective-permute-start(bf16[1,32,512]{2,1,0:T(8,128)(2,1)} %get-tuple-element.45), channel_id=1, source_target_pairs={{0,16},{16,32},{32,48},{48,64},{64,80},{80,96},{96,112},{112,128},... | collective-permute-start | bytes 98312 | tf_op jit(solution)/shard_map/ppermute | solution.py:15
  12.5 25.5 %collective-permute-start.1 = (bf16[1,32,512]{2,1,0:T(8,128)(2,1)}, bf16[1,32,512]{2,1,0:T(8,128)(2,1)S(1)}, u32[]{:S(2)}, u32[]{:S(2)}) collective-permute-start(bf16[1,32,512]{2,1,0:T(8,128)(2,1)} %get-tuple-element.46), channel_id=1, source_target_pairs={{16,0},{32,16},{48,32},{64,48},{80,64},{96,80},{112,96},{128,112},... | collective-permute-start | bytes 98312 | tf_op jit(solution)/shard_map/ppermute | solution.py:18
  38.0 22.9 %collective-permute-start.2 = (bf16[18,1,512]{2,1,0:T(2,128)(2,1)S(1)}, bf16[18,1,512]{2,1,0:T(2,128)(2,1)S(1)}, u32[]{:S(2)}, u32[]{:S(2)}) collective-permute-start(bf16[18,1,512]{2,1,0:T(2,128)(2,1)S(1)} %get-tuple-element.40), channel_id=1, source_target_pairs={{0,1},{1,2},{2,3},{3,4},{4,5},{5,6},{6,7},{7,8},{8,9},{9,10},{10,1... | collective-permute-start | bytes 55304 | tf_op jit(solution)/shard_map/ppermute | solution.py:15
  38.8 22.2 %collective-permute-start.3 = (bf16[18,1,512]{2,1,0:T(2,128)(2,1)S(1)}, bf16[18,1,512]{2,1,0:T(2,128)(2,1)S(1)}, u32[]{:S(2)}, u32[]{:S(2)}) collective-permute-start(bf16[18,1,512]{2,1,0:T(2,128)(2,1)S(1)} %get-tuple-element.39), channel_id=1, source_target_pairs={{1,0},{2,1},{3,2},{4,3},{5,4},{6,5},{7,6},{8,7},{9,8},{10,9},{11,1... | collective-permute-start | bytes 55304 | tf_op jit(solution)/shard_map/ppermute | solution.py:18
  50.9 9.4 %copy-start.25 = (bf16[2,2,2,64,32]{3,4,2,1,0:T(8,128)(2,1)S(1)}, bf16[2,2,2,64,32]{3,4,2,1,0:T(8,128)(2,1)}, u32[]{:S(2)}) copy-start(bf16[2,2,2,64,32]{3,4,2,1,0:T(8,128)(2,1)} %param.11) | copy-start | bytes 98308
  66.2 19.0 %copy-start = (bf16[2,2,4,2,32,4,64]{6,5,4,3,2,1,0:T(4,128)(2,1)S(1)}, bf16[2,2,4,2,32,4,64]{6,5,4,3,2,1,0:T(4,128)(2,1)}, u32[]{:S(2)}) copy-start(bf16[2,2,4,2,32,4,64]{6,5,4,3,2,1,0:T(4,128)(2,1)} %fusion.22) | copy-start | bytes 1572868
  73.7 6.9 %collective-permute-start.4 = (bf16[1,16,256]{2,1,0:T(8,128)(2,1)S(1)}, bf16[1,16,256]{2,1,0:T(8,128)(2,1)S(1)}, u32[]{:S(2)}, u32[]{:S(2)}) collective-permute-start(bf16[1,16,256]{2,1,0:T(8,128)(2,1)S(1)} %get-tuple-element.69), channel_id=1, source_target_pairs={{0,16},{16,32},{32,48},{48,64},{64,80},{80,96},{96,112},{112,128},... | collective-permute-start | bytes 24584 | tf_op jit(solution)/shard_map/ppermute | solution.py:15
  75.7 4.9 %collective-permute-start.5 = (bf16[1,16,256]{2,1,0:T(8,128)(2,1)S(1)}, bf16[1,16,256]{2,1,0:T(8,128)(2,1)S(1)}, u32[]{:S(2)}, u32[]{:S(2)}) collective-permute-start(bf16[1,16,256]{2,1,0:T(8,128)(2,1)S(1)} %get-tuple-element.70), channel_id=1, source_target_pairs={{16,0},{32,16},{48,32},{64,48},{80,64},{96,80},{112,96},{128,112},... | collective-permute-start | bytes 24584 | tf_op jit(solution)/shard_map/ppermute | solution.py:18
  80.7 60.9 %collective-permute-start.6 = (bf16[10,1,256]{2,1,0:T(2,128)(2,1)S(1)}, bf16[10,1,256]{2,1,0:T(2,128)(2,1)S(1)}, u32[]{:S(2)}, u32[]{:S(2)}) collective-permute-start(bf16[10,1,256]{2,1,0:T(2,128)(2,1)S(1)} %get-tuple-element.66), channel_id=1, source_target_pairs={{0,1},{1,2},{2,3},{3,4},{4,5},{5,6},{6,7},{7,8},{8,9},{9,10},{10,1... | collective-permute-start | bytes 15368 | tf_op jit(solution)/shard_map/ppermute | solution.py:15
  80.8 60.8 %collective-permute-start.7 = (bf16[10,1,256]{2,1,0:T(2,128)(2,1)S(1)}, bf16[10,1,256]{2,1,0:T(2,128)(2,1)S(1)}, u32[]{:S(2)}, u32[]{:S(2)}) collective-permute-start(bf16[10,1,256]{2,1,0:T(2,128)(2,1)S(1)} %get-tuple-element.65), channel_id=1, source_target_pairs={{1,0},{2,1},{3,2},{4,3},{5,4},{6,5},{7,6},{8,7},{9,8},{10,9},{11,1... | collective-permute-start | bytes 15368 | tf_op jit(solution)/shard_map/ppermute | solution.py:18
  100.2 6.7 %copy-start.1 = (bf16[3,3,4,64,4,64]{5,4,3,1,0,2:T(4,128)(2,1)S(1)}, bf16[3,3,4,64,4,64]{5,4,3,1,0,2:T(4,128)(2,1)}, u32[]{:S(2)}) copy-start(bf16[3,3,4,64,4,64]{5,4,3,1,0,2:T(4,128)(2,1)} %convert_bitcast_fusion.4) | copy-start | bytes 3538948
  109.4 4.7 copy-start.9
  131.8 6.8 %copy-start.7 = (bf16[8,2,16,2,256]{4,3,1,2,0:T(2,128)(2,1)S(1)}, bf16[8,2,16,2,256]{4,3,1,2,0:T(2,128)(2,1)}, u32[]{:S(2)}) copy-start(bf16[8,2,16,2,256]{4,3,1,2,0:T(2,128)(2,1)} %copy.155) | copy-start | bytes 786436
  131.8 7.1 %copy-start.4 = (bf16[16,32,2304]{2,1,0:T(8,128)(2,1)S(1)}, bf16[16,32,2304]{2,1,0:T(8,128)(2,1)}, u32[]{:S(2)}) copy-start(bf16[16,32,2304]{2,1,0:T(8,128)(2,1)} %copy-done.3) | copy-start | bytes 7077892
  154.4 7.0 %collective-permute-start.12 = (bf16[1,16,256]{2,1,0:T(8,128)(2,1)S(1)}, bf16[1,16,256]{2,1,0:T(8,128)(2,1)S(1)}, u32[]{:S(2)}, u32[]{:S(2)}) collective-permute-start(bf16[1,16,256]{2,1,0:T(8,128)(2,1)S(1)} %get-tuple-element.67), channel_id=1, source_target_pairs={{0,16},{16,32},{32,48},{48,64},{64,80},{80,96},{96,112},{112,128},... | collective-permute-start | bytes 24584 | tf_op jit(solution)/shard_map/ppermute | solution.py:15
  154.4 7.0 %collective-permute-start.13 = (bf16[1,16,256]{2,1,0:T(8,128)(2,1)S(1)}, bf16[1,16,256]{2,1,0:T(8,128)(2,1)S(1)}, u32[]{:S(2)}, u32[]{:S(2)}) collective-permute-start(bf16[1,16,256]{2,1,0:T(8,128)(2,1)S(1)} %get-tuple-element.68), channel_id=1, source_target_pairs={{16,0},{32,16},{48,32},{64,48},{80,64},{96,80},{112,96},{128,112},... | collective-permute-start | bytes 24584 | tf_op jit(solution)/shard_map/ppermute | solution.py:18
  161.4 13.2 %collective-permute-start.14 = (bf16[10,1,256]{2,1,0:T(2,128)(2,1)S(1)}, bf16[10,1,256]{2,1,0:T(2,128)(2,1)S(1)}, u32[]{:S(2)}, u32[]{:S(2)}) collective-permute-start(bf16[10,1,256]{2,1,0:T(2,128)(2,1)S(1)} %get-tuple-element.62), channel_id=1, source_target_pairs={{0,1},{1,2},{2,3},{3,4},{4,5},{5,6},{6,7},{7,8},{8,9},{9,10},{10,1... | collective-permute-start | bytes 15368 | tf_op jit(solution)/shard_map/ppermute | solution.py:15
  161.5 13.1 %collective-permute-start.15 = (bf16[10,1,256]{2,1,0:T(2,128)(2,1)S(1)}, bf16[10,1,256]{2,1,0:T(2,128)(2,1)S(1)}, u32[]{:S(2)}, u32[]{:S(2)}) collective-permute-start(bf16[10,1,256]{2,1,0:T(2,128)(2,1)S(1)} %get-tuple-element.61), channel_id=1, source_target_pairs={{1,0},{2,1},{3,2},{4,3},{5,4},{6,5},{7,6},{8,7},{9,8},{10,9},{11,1... | collective-permute-start | bytes 15368 | tf_op jit(solution)/shard_map/ppermute | solution.py:18
  165.8 9.1 %copy-start.14 = (bf16[2304,256,1]{1,0,2:T(8,128)(2,1)S(1)}, bf16[2304,256,1]{1,0,2:T(8,128)(2,1)}, u32[]{:S(2)}) copy-start(bf16[2304,256,1]{1,0,2:T(8,128)(2,1)} %reshape.328) | copy-start | bytes 3538948
  165.8 9.1 %copy-start.30 = (f32[8,16,256]{2,1,0:T(8,128)S(1)}, f32[8,16,256]{2,1,0:T(8,128)}, u32[]{:S(2)}) copy-start(f32[8,16,256]{2,1,0:T(8,128)} %get-tuple-element.74) | copy-start | bytes 393220
  168.3 25.5 %collective-permute-start.8 = (bf16[1,32,256]{2,1,0:T(8,128)(2,1)}, bf16[1,32,256]{2,1,0:T(8,128)(2,1)}, u32[]{:S(2)}, u32[]{:S(2)}) collective-permute-start(bf16[1,32,256]{2,1,0:T(8,128)(2,1)} %get-tuple-element.57), channel_id=1, source_target_pairs={{0,16},{16,32},{32,48},{48,64},{64,80},{80,96},{96,112},{112,128},... | collective-permute-start | bytes 49160 | tf_op jit(solution)/shard_map/ppermute | solution.py:15
  168.3 25.5 %collective-permute-start.9 = (bf16[1,32,256]{2,1,0:T(8,128)(2,1)}, bf16[1,32,256]{2,1,0:T(8,128)(2,1)}, u32[]{:S(2)}, u32[]{:S(2)}) collective-permute-start(bf16[1,32,256]{2,1,0:T(8,128)(2,1)} %get-tuple-element.58), channel_id=1, source_target_pairs={{16,0},{32,16},{48,32},{64,48},{80,64},{96,80},{112,96},{128,112},... | collective-permute-start | bytes 49160 | tf_op jit(solution)/shard_map/ppermute | solution.py:18
  178.1 5.6 %copy-start.6 = (bf16[512,2304]{0,1:T(8,128)(2,1)S(1)}, bf16[512,2304]{0,1:T(8,128)(2,1)}, u32[]{:S(2)}) copy-start(bf16[512,2304]{0,1:T(8,128)(2,1)} %copy.78) | copy-start | bytes 7077892
  186.5 7.2 %copy-start.12 = (f32[110592]{0:T(1024)S(1)}, f32[110592]{0:T(1024)}, u32[]{:S(2)}) copy-start(f32[110592]{0:T(1024)} %reshape.306) | copy-start | bytes 1327108
  188.2 25.4 %collective-permute-start.16 = (bf16[1,32,256]{2,1,0:T(8,128)(2,1)S(1)}, bf16[1,32,256]{2,1,0:T(8,128)(2,1)S(1)}, u32[]{:S(2)}, u32[]{:S(2)}) collective-permute-start(bf16[1,32,256]{2,1,0:T(8,128)(2,1)S(1)} %copy-done.28), channel_id=1, source_target_pairs={{0,16},{16,32},{32,48},{48,64},{64,80},{80,96},{96,112},{112,128},... | collective-permute-start | bytes 49160 | tf_op jit(solution)/shard_map/ppermute | solution.py:15
  188.3 25.3 %collective-permute-start.17 = (bf16[1,32,256]{2,1,0:T(8,128)(2,1)S(1)}, bf16[1,32,256]{2,1,0:T(8,128)(2,1)S(1)}, u32[]{:S(2)}, u32[]{:S(2)}) collective-permute-start(bf16[1,32,256]{2,1,0:T(8,128)(2,1)S(1)} %copy-done.27), channel_id=1, source_target_pairs={{16,0},{32,16},{48,32},{64,48},{80,64},{96,80},{112,96},{128,112},... | collective-permute-start | bytes 49160 | tf_op jit(solution)/shard_map/ppermute | solution.py:18
  194.5 5.1 %collective-permute-start.10 = (bf16[18,1,256]{2,1,0:T(2,128)(2,1)S(1)}, bf16[18,1,256]{2,1,0:T(2,128)(2,1)S(1)}, u32[]{:S(2)}, u32[]{:S(2)}) collective-permute-start(bf16[18,1,256]{2,1,0:T(2,128)(2,1)S(1)} %get-tuple-element.54), channel_id=1, source_target_pairs={{0,1},{1,2},{2,3},{3,4},{4,5},{5,6},{6,7},{7,8},{8,9},{9,10},{10,1... | collective-permute-start | bytes 27656 | tf_op jit(solution)/shard_map/ppermute | solution.py:15
  194.6 5.0 %collective-permute-start.11 = (bf16[18,1,256]{2,1,0:T(2,128)(2,1)S(1)}, bf16[18,1,256]{2,1,0:T(2,128)(2,1)S(1)}, u32[]{:S(2)}, u32[]{:S(2)}) collective-permute-start(bf16[18,1,256]{2,1,0:T(2,128)(2,1)S(1)} %get-tuple-element.53), channel_id=1, source_target_pairs={{1,0},{2,1},{3,2},{4,3},{5,4},{6,5},{7,6},{8,7},{9,8},{10,9},{11,1... | collective-permute-start | bytes 27656 | tf_op jit(solution)/shard_map/ppermute | solution.py:18
  210.9 6.4 %copy-start.18 = (bf16[16,32,256]{2,1,0:T(8,128)(2,1)S(1)}, bf16[16,32,256]{2,1,0:T(8,128)(2,1)}, u32[]{:S(2)}) copy-start(bf16[16,32,256]{2,1,0:T(8,128)(2,1)} %param.7) | copy-start | bytes 786436
  213.6 6.5 %collective-permute-start.18 = (bf16[18,1,256]{2,1,0:T(2,128)(2,1)S(1)}, bf16[18,1,256]{2,1,0:T(2,128)(2,1)S(1)}, u32[]{:S(2)}, u32[]{:S(2)}) collective-permute-start(bf16[18,1,256]{2,1,0:T(2,128)(2,1)S(1)} %get-tuple-element.50), channel_id=1, source_target_pairs={{0,1},{1,2},{2,3},{3,4},{4,5},{5,6},{6,7},{7,8},{8,9},{9,10},{10,1... | collective-permute-start | bytes 27656 | tf_op jit(solution)/shard_map/ppermute | solution.py:15
  213.7 6.4 %collective-permute-start.19 = (bf16[18,1,256]{2,1,0:T(2,128)(2,1)S(1)}, bf16[18,1,256]{2,1,0:T(2,128)(2,1)S(1)}, u32[]{:S(2)}, u32[]{:S(2)}) collective-permute-start(bf16[18,1,256]{2,1,0:T(2,128)(2,1)S(1)} %get-tuple-element.49), channel_id=1, source_target_pairs={{1,0},{2,1},{3,2},{4,3},{5,4},{6,5},{7,6},{8,7},{9,8},{10,9},{11,1... | collective-permute-start | bytes 27656 | tf_op jit(solution)/shard_map/ppermute | solution.py:18
  (20 other events, 48.8 us)
Sparse Core Ops, SparseCore 0:
  213.7 255.0 all-reduce.1
where the time goes:
time: 491 us; the launch traced here: 484 us
  waiting for transfers between devices  247 us (50%)
  local copies, waits for them, and re-layouts  109 us (22%)
  matrix products  50.3 us (10%)
  starting transfers between devices  47.1 us (10%)
  between operations  15.5 us (3%)
  other arithmetic  14.3 us (3%)
    psum x1, waiting for transfers between devices, in_one(): so_far = lax.psum(jnp.concatenate([a.ravel() for a in arrays]), axis)  246 us
    convert_element_type x12, local copies, waits for them, and re-layouts, band_matrix(): band.reshape(9 * planes * weight.shape[3], planes * weight.shape[4])  61 us
    ppermute x10, starting transfers between devices, padded_2(): lax.ppermute(lax.slice_in_dim(block, 0, width, axis=dim), axis, backward)  41.2 us
    dot_general x6, matrix products, band_matrix(): band = jnp.einsum('kpz,abkco->abpczo', shifts, weight.astype(jnp.float32))  18.8 us
    dot_general x6, matrix products, conv_padded(): jnp.dot(columns(padded), band, preferred_element_type=jnp.float32)  11.6 us
  transfers between devices with their start and end apart: 21, of which 2 were waited for; matrix products, arithmetic and copies ran while one was open for 28% of the time, Pallas kernels for 0%

commit v1 on v0

v1 whole, which is shorter than its diff:
```python
import functools
import math

import jax
import jax.numpy as jnp
from jax import lax
from jax.experimental import pallas as pl
from jax.experimental.pallas import tpu as pltpu
from jax.sharding import PartitionSpec as P

BF = jnp.bfloat16
F32 = jnp.float32
NN = (((1,), (0,)), ((), ()))
NT = (((1,), (1,)), ((), ()))

HF = 7
HC = 5
EX, EY = 32, 48
CX, CY = 16, 32
BX, BY = 16, 32
W = 256
TILES = 50


def dot(a, b, dims=NN):
    return lax.dot_general(a, b, dims, preferred_element_type=F32)


def rounded(v):
    return v.astype(BF).astype(F32)


def loop(n, body):
    def step(i, carry):
        body(i)
        return carry

    lax.fori_loop(0, n, step, 0)


def repeat_matrix(rows, cols, period, first):
    r = lax.broadcasted_iota(jnp.int32, (rows, cols), 0)
    c = lax.broadcasted_iota(jnp.int32, (rows, cols), 1)
    return (lax.rem(c, period) == r + first).astype(F32).astype(BF)


def bands_kernel(wd, wp, wm, wu, wup, bd, pm, bm, um, bu, wide, wide_mid):
    def band(w, out, wide, ch):
        planes = W // ch
        wide[...] = dot(w[...], repeat_matrix(ch, W, ch, 0))
        group = lax.broadcasted_iota(jnp.int32, (ch, W), 1) // ch

        def tap(t):
            base = pl.multiple_of(t * 3 * ch, ch)
            t0 = wide[pl.ds(base, ch), :]
            t1 = wide[pl.ds(base + ch, ch), :]
            t2 = wide[pl.ds(base + 2 * ch, ch), :]
            for p in range(planes):
                rows = jnp.where(group == p, t1, 0.0)
                if p + 1 < planes:
                    rows = jnp.where(group == p + 1, t0, rows)
                if p > 0:
                    rows = jnp.where(group == p - 1, t2, rows)
                out[pl.ds(pl.multiple_of(t * W + p * ch, ch), ch), :] = rows.astype(BF)

        loop(9, tap)

    band(wd, bd, wide, 32)
    band(wup, bu, wide, 32)
    band(wm, bm, wide_mid, 64)
    group = lax.broadcasted_iota(jnp.int32, (64, W), 1) // 64
    same = repeat_matrix(64, W, 64, 0)
    low = repeat_matrix(32, W, 64, 0)
    high = repeat_matrix(32, W, 64, 32)
    for q in range(4):
        pool = dot(wp[q], same)
        unpool = dot(wu[2 * q], low) + dot(wu[2 * q + 1], high)
        for y in range(4):
            rows = slice(q * W + y * 64, q * W + y * 64 + 64)
            pm[rows, :] = jnp.where(group == y, pool, 0.0).astype(BF)
            um[rows, :] = jnp.where(group == y, unpool, 0.0).astype(BF)


def build_bands(w_down, w_pool, w_mid, w_unpool, w_up):
    wide = jax.ShapeDtypeStruct((9 * W, W), BF)
    four = jax.ShapeDtypeStruct((4 * W, W), BF)
    return pl.pallas_call(
        bands_kernel,
        out_shape=(wide, four, wide, four, wide),
        scratch_shapes=[pltpu.VMEM((27 * 32, W), F32), pltpu.VMEM((27 * 64, W), F32)],
        compiler_params=pltpu.CompilerParams(vmem_limit_bytes=24 * 1024 * 1024),
        cost_estimate=pl.CostEstimate(flops=2 * 10**9, bytes_accessed=8 * 10**6, transcendentals=0),
        name="bands",
    )(
        w_down.reshape(27 * 32, 32),
        w_pool.reshape(4, 64, 64),
        w_mid.reshape(27 * 64, 64),
        w_unpool.reshape(8, 64, 32),
        w_up.reshape(27 * 32, 32),
    )


def get_row(src, row):
    if len(src.shape) == 3:
        return src[row]
    return jnp.concatenate([src[0, row], src[1, row]], axis=1)


def get_rows(src, rows):
    return jnp.concatenate([src[0, rows], src[1, rows]], axis=2)


def put_rows(dst, rows, value):
    dst[0, rows] = value[..., 0:128]
    dst[1, rows] = value[..., 128:256]


def get_every_second(src, row, first, count):
    at = pl.ds(first, count, stride=2)
    return jnp.concatenate([src[0, row, at, :], src[1, row, at, :]], axis=1)


def put_every_second(dst, row, first, value):
    at = pl.ds(first, value.shape[0], stride=2)
    dst[0, row, at, :] = value[:, 0:128]
    dst[1, row, at, :] = value[:, 128:256]


def taps_to_lanes(src, row, out, at, lo, size):
    v = get_row(src, row)
    n = v.shape[0]
    out[at, :, 0:W] = pltpu.roll(v, 1, 0)[lo : lo + size].astype(BF)
    out[at, :, W : 2 * W] = v[lo : lo + size].astype(BF)
    out[at, :, 2 * W : 3 * W] = pltpu.roll(v, n - 1, 0)[lo : lo + size].astype(BF)


def conv_rows(v3, first, rows, band):
    total = None
    for a in range(3):
        piece = v3[pl.ds(first + a, rows)]
        piece = piece.reshape(rows * piece.shape[1], 3 * W)
        part = dot(piece, band[a * 3 * W : (a + 1) * 3 * W, :])
        total = part if total is None else total + part
    return total


def conv_t_rows(v3, first, rows, band):
    total = None
    for a in range(3):
        piece = v3[pl.ds(first + a, rows)]
        piece = piece.reshape(rows * piece.shape[1], 3 * W)
        for b in range(3):
            tap = (2 - a) * 3 + (2 - b)
            part = dot(piece[:, b * W : (b + 1) * W], band[tap * W : (tap + 1) * W, :], NT)
            total = part if total is None else total + part
    return total


def pick(d, lanes, shift, ch, width):
    group = lax.broadcasted_iota(jnp.int32, (ch, 128), 1) // ch
    p0 = (lanes % width) // ch
    out = jnp.zeros((ch, 128), F32)
    for g in range(128 // ch):
        z = p0 + g - shift
        if 0 <= z < W // ch:
            out = jnp.where(group == g, d[z * ch : (z + 1) * ch, lanes : lanes + 128], out)
    return out


def put_split(value, hi, lo, row, lanes):
    top = value.astype(BF)
    hi[row : row + value.shape[0], lanes : lanes + 128] = top
    lo[row : row + value.shape[0], lanes : lanes + 128] = (value - top.astype(F32)).astype(BF)


def conv_weight_terms(dout_t, v3, rows, ch, hi, lo, dsc):
    units = 27 * ch
    pad = hi.shape[0] - units
    hi[units:, :] = jnp.zeros((pad, W), BF)
    lo[units:, :] = jnp.zeros((pad, W), BF)
    for a in range(3):
        piece = v3[a : a + rows]
        piece = piece.reshape(rows * piece.shape[1], 3 * W)
        dsc[...] = dot(dout_t, piece)
        for b in range(3):
            for k in range(3):
                unit = (a * 3 + b) * 3 + k
                for t in range(2):
                    value = pick(dsc, b * W + t * 128, k - 1, ch, W)
                    put_split(value, hi, lo, unit * ch, t * 128)


def main_kernel(
    fc, cc, xlo, xhi, ylo, yhi, clo, chi, bd, pm, bm, um, bu,
    out, gf, terms,
    fe, ce, hid, ds_down, skp, ds_up, dup, ddn,
    v3f, v3c, v3fl, v3s, v3d,
    parts, co, mid, ds_pool, ds_mid, dmid, v3m, v3dm, v3ml, local,
    hi, lo, him, lom, dsc,
):
    def gather(dst, count, center, off_x, off_y):
        def own(i):
            dst[8 + i, 0:8] = ylo[off_y + i].astype(F32)
            dst[8 + i, 8:40] = center[i].astype(F32)
            dst[8 + i, 40:48] = yhi[off_y + i].astype(F32)

        loop(BX, own)

        def edge(i):
            dst[8 - count + i, 0:8] = clo[off_x + i].astype(F32)
            dst[8 - count + i, 8:40] = xlo[off_x + i].astype(F32)
            dst[8 - count + i, 40:48] = chi[off_x + i].astype(F32)
            dst[24 + i, 0:8] = clo[HF + HC + off_x + i].astype(F32)
            dst[24 + i, 8:40] = xhi[off_x + i].astype(F32)
            dst[24 + i, 40:48] = chi[HF + HC + off_x + i].astype(F32)

        loop(count, edge)

    gather(fe, HF, fc, 0, 0)
    gather(ce, HC, cc, HF, BX)

    loop(30, lambda i: taps_to_lanes(fe, 1 + i, v3f, i, 0, EY))
    loop(18, lambda i: taps_to_lanes(fe, 7 + i, v3fl, i, 8, BY))
    zero = jnp.zeros((2, EY, W), F32)
    put_rows(hid, slice(0, 2), zero)
    put_rows(hid, slice(30, 32), zero)

    def down(i):
        pre = conv_rows(v3f, 4 * i, 4, bd)
        sig = jax.nn.sigmoid(pre)
        at = pl.ds(2 + 4 * i, 4)
        put_rows(hid, at, rounded(pre * sig).reshape(4, EY, W))
        put_rows(ds_down, at, (sig * (1.0 + pre * (1.0 - sig))).reshape(4, EY, W))

    loop(7, down)

    pad = jnp.zeros((CY - EY // 2, W), F32)

    def to_parts(src, x):
        for i in range(2):
            for j in range(2):
                half = get_every_second(src, 2 * x + i, j, EY // 2)
                parts[2 * i + j, x] = jnp.concatenate([half, pad], axis=0).astype(BF)

    loop(CX, lambda x: to_parts(hid, x))

    def pool(i):
        pre = None
        for q in range(4):
            piece = parts[q, pl.ds(4 * i, 4)].reshape(4 * CY, W)
            part = dot(piece, pm[q * W : (q + 1) * W, :])
            pre = part if pre is None else pre + part
        sig = jax.nn.sigmoid(pre)
        co[pl.ds(4 * i, 4)] = rounded(pre * sig).reshape(4, CY, W)
        ds_pool[pl.ds(4 * i, 4)] = (sig * (1.0 + pre * (1.0 - sig))).reshape(4, CY, W)

    loop(4, pool)

    loop(14, lambda i: taps_to_lanes(co, 1 + i, v3m, i, 0, CY))

    def middle(i):
        pre = conv_rows(v3m, 4 * i, 4, bm)
        sig = jax.nn.sigmoid(pre)
        own = co[pl.ds(2 + 4 * i, 4)].reshape(4 * CY, W)
        mid[pl.ds(2 + 4 * i, 4)] = (own + pre * sig).astype(BF).reshape(4, CY, W)
        ds_mid[pl.ds(2 + 4 * i, 4)] = (sig * (1.0 + pre * (1.0 - sig))).reshape(4, CY, W)

    loop(3, middle)

    def up(x):
        m = mid[pl.ds(2 + 2 * x, 2)].reshape(2 * CY, W)
        for i in range(2):
            for j in range(2):
                q = 2 * i + j
                lifted = dot(m, um[q * W : (q + 1) * W, :])
                for r in range(2):
                    row = 2 * (2 + 2 * x + r) + i
                    own = get_every_second(hid, row, j, EY // 2)
                    pre = own + lifted[r * CY : r * CY + EY // 2]
                    sig = jax.nn.sigmoid(pre)
                    put_every_second(skp, row, j, rounded(pre * sig))
                    put_every_second(ds_up, row, j, sig * (1.0 + pre * (1.0 - sig)))

    loop(6, up)

    loop(18, lambda i: taps_to_lanes(skp, 7 + i, v3s, i, 8, BY))

    def output(i):
        total = conv_rows(v3s, 4 * i, 4, bu).reshape(4, BY, W)
        out[pl.ds(4 * i, 4)] = (fc[pl.ds(4 * i, 4)].astype(F32) + total).astype(BF)

    loop(4, output)

    loop(26, lambda i: taps_to_lanes(ce, 3 + i, v3c, i, 0, EY))

    def d_up(i):
        total = conv_t_rows(v3c, 4 * i, 4, bu)
        at = pl.ds(4 + 4 * i, 4)
        put_rows(dup, at, rounded(total.reshape(4, EY, W) * get_rows(ds_up, at)))

    loop(6, d_up)

    cot_t = cc[...].reshape(BX * BY, W).astype(F32).T.astype(BF)
    fold = repeat_matrix(32, W, 32, 0)
    fold_mid = repeat_matrix(64, W, 64, 0)

    def fold_to(matrix, hi, lo, tile, count):
        total = dot(matrix, hi[...], NT) + dot(matrix, lo[...], NT)
        for t in range(count):
            rows = matrix.shape[0]
            terms[(tile * 32 + t * rows) : (tile * 32 + (t + 1) * rows), :] = total[
                :, t * 128 : (t + 1) * 128
            ]

    conv_weight_terms(cot_t, v3s, BX, 32, hi, lo, dsc)
    fold_to(fold, hi, lo, 7, 7)

    def own_parts(src, x):
        for i in range(2):
            for j in range(2):
                half = get_every_second(src, 8 + 2 * x + i, 8 + j, BY // 2)
                local[2 * i + j, x] = half.astype(BF)

    loop(8, lambda x: own_parts(dup, x))
    mid_t = mid[4:12].astype(F32)[:, 0:24][:, 4:20].reshape(128, W).T.astype(BF)

    def plain_terms(left, q, row):
        d = dot(left, local[q].reshape(128, W))
        for t in range(2):
            group = lax.broadcasted_iota(jnp.int32, (64, 128), 1) // 64
            low = d[(2 * t) * 64 : (2 * t + 1) * 64, t * 128 : (t + 1) * 128]
            high = d[(2 * t + 1) * 64 : (2 * t + 2) * 64, t * 128 : (t + 1) * 128]
            put_split(jnp.where(group == 0, low, high), him, lom, row, t * 128)

    for q in range(4):
        plain_terms(mid_t, q, 64 * q)
    fold_cols = (him[0:256, :], lom[0:256, :])
    unpool = dot(fold_cols[0], fold_mid, NT) + dot(fold_cols[1], fold_mid, NT)
    for q in range(4):
        half = (q % 2) * 64
        rows = slice(46 * 32 + (q // 2) * 64, 46 * 32 + (q // 2 + 1) * 64)
        terms[rows, half : half + 64] = unpool[q * 64 : (q + 1) * 64, :]

    loop(12, lambda x: to_parts(dup, 2 + x))

    def d_middle(i):
        total = None
        at = pl.ds(2 + 4 * i, 4)
        for q in range(4):
            piece = parts[q, at].reshape(4 * CY, W)
            part = dot(piece, um[q * W : (q + 1) * W, :], NT)
            total = part if total is None else total + part
        dmid[at] = rounded(total * ds_mid[at].reshape(4 * CY, W)).reshape(4, CY, W)
        ds_mid[at] = total.reshape(4, CY, W)

    loop(3, d_middle)

    loop(12, lambda i: taps_to_lanes(dmid, 2 + i, v3dm, i, 0, CY))

    def coarse_local(i):
        v = co[3 + i]
        for b in range(3):
            v3ml[i, :, b * W : (b + 1) * W] = v[3 + b : 19 + b].astype(BF)

    loop(10, coarse_local)
    dmid_t = dmid[4:12][:, 4:20].reshape(128, W).T.astype(BF)
    conv_weight_terms(dmid_t, v3ml, 8, 64, him, lom, dsc)
    fold_to(fold_mid, him, lom, 14, 14)

    def d_pool(i):
        at = pl.ds(3 + 2 * i, 2)
        total = conv_t_rows(v3dm, 2 * i, 2, bm).reshape(2, CY, W)
        ds_pool[at] = rounded((ds_mid[at] + total) * ds_pool[at])

    loop(5, d_pool)

    def d_down(i):
        dp = ds_pool[pl.ds(3 + 2 * i, 2)].reshape(2 * CY, W).astype(BF)
        for a in range(2):
            for j in range(2):
                q = 2 * a + j
                back = dot(dp, pm[q * W : (q + 1) * W, :], NT)
                for r in range(2):
                    row = 2 * (3 + 2 * i + r) + a
                    own = get_every_second(dup, row, j, EY // 2)
                    d_hidden = own + back[r * CY : r * CY + EY // 2]
                    slope = get_every_second(ds_down, row, j, EY // 2)
                    put_every_second(ddn, row, j, rounded(d_hidden * slope))

    loop(5, d_down)

    loop(18, lambda i: taps_to_lanes(ddn, 7 + i, v3d, i, 8, BY))

    down_t = get_rows(ddn, slice(8, 24))[:, 8:40].reshape(BX * BY, W).T.astype(BF)
    conv_weight_terms(down_t, v3fl, BX, 32, hi, lo, dsc)
    fold_to(fold, hi, lo, 0, 7)

    loop(8, lambda x: own_parts(hid, x))
    pool_t = ds_pool[4:12][:, 4:20].reshape(128, W).T.astype(BF)
    for q in range(4):
        plain_terms(pool_t, q, 64 * q)
    pooled = dot(fold_mid, him[0:256, :], NT) + dot(fold_mid, lom[0:256, :], NT)
    for t in range(2):
        terms[42 * 32 + t * 64 : 42 * 32 + (t + 1) * 64, :] = pooled[:, t * 128 : (t + 1) * 128]
    rest = terms.shape[0] - TILES * 32
    if rest > 0:
        terms[TILES * 32 :, :] = jnp.zeros((rest, 128), F32)

    def grad_fields(i):
        total = conv_t_rows(v3d, 4 * i, 4, bd).reshape(4, BY, W)
        gf[pl.ds(4 * i, 4)] = (cc[pl.ds(4 * i, 4)].astype(F32) + total).astype(BF)

    loop(4, grad_fields)


def main_call(fields, cot, halos, bands, term_rows):
    block = jax.ShapeDtypeStruct((BX, BY, W), BF)
    fine = pltpu.VMEM((EX, EY, W), F32)
    split = pltpu.VMEM((2, EX, EY, 128), F32)
    coarse = pltpu.VMEM((CX, CY, W), F32)
    return pl.pallas_call(
        main_kernel,
        out_shape=(block, block, jax.ShapeDtypeStruct((term_rows, 128), F32)),
        scratch_shapes=[fine] * 2
        + [split] * 6
        + [
            pltpu.VMEM((30, EY, 3 * W), BF),
            pltpu.VMEM((26, EY, 3 * W), BF),
            pltpu.VMEM((18, BY, 3 * W), BF),
            pltpu.VMEM((18, BY, 3 * W), BF),
            pltpu.VMEM((18, BY, 3 * W), BF),
            pltpu.VMEM((4, CX, CY, W), BF),
            coarse,
            pltpu.VMEM((CX, CY, W), BF),
            coarse,
            coarse,
            coarse,
            pltpu.VMEM((14, CY, 3 * W), BF),
            pltpu.VMEM((12, CY, 3 * W), BF),
            pltpu.VMEM((10, 16, 3 * W), BF),
            pltpu.VMEM((4, 8, 16, W), BF),
            pltpu.VMEM((28 * 32, W), BF),
            pltpu.VMEM((28 * 32, W), BF),
            pltpu.VMEM((28 * 64, W), BF),
            pltpu.VMEM((28 * 64, W), BF),
            pltpu.VMEM((W, 3 * W), F32),
        ],
        compiler_params=pltpu.CompilerParams(vmem_limit_bytes=52 * 1024 * 1024),
        cost_estimate=pl.CostEstimate(flops=10**10, bytes_accessed=10**7, transcendentals=10**6),
        name="network",
    )(fields, cot, *halos, *bands)


def unpack_kernel(terms, down, pool, mid, unpool, up):
    for u in range(27):
        row, lane = (u // 4) * 32, (u % 4) * 32
        down[u] = terms[row : row + 32, lane : lane + 32]
        up[u] = terms[224 + row : 224 + row + 32, lane : lane + 32]
        row, lane = 14 * 32 + (u // 2) * 64, (u % 2) * 64
        mid[u] = terms[row : row + 64, lane : lane + 64]
    for q in range(4):
        row, lane = 42 * 32 + (q // 2) * 64, (q % 2) * 64
        pool[q] = terms[row : row + 64, lane : lane + 64]
        for l in range(2):
            row, lane = 46 * 32 + (q // 2) * 64, (q % 2) * 64 + l * 32
            unpool[2 * q + l] = terms[row : row + 64, lane : lane + 32]


def unpack(terms):
    shape = lambda *s: jax.ShapeDtypeStruct(s, F32)
    return pl.pallas_call(
        unpack_kernel,
        out_shape=(
            shape(27, 32, 32), shape(4, 64, 64), shape(27, 64, 64), shape(8, 64, 32),
            shape(27, 32, 32),
        ),
        name="unpack",
    )(terms)


def ring(axis, step):
    n = lax.axis_size(axis)
    return [(i, (i + step) % n) for i in range(n)]


def exchange(fields, cot):
    def columns(a, b, lo):
        return jnp.concatenate([a[:, lo : lo + 8], b[:, lo : lo + 8]], axis=0)

    last = jnp.concatenate([fields[BX - HF :], cot[BX - HC :]], axis=0)
    first = jnp.concatenate([fields[:HF], cot[:HC]], axis=0)
    xlo = lax.ppermute(last, "gx", ring("gx", 1))
    xhi = lax.ppermute(first, "gx", ring("gx", -1))
    ylo = lax.ppermute(columns(fields, cot, BY - 8), "gy", ring("gy", 1))
    yhi = lax.ppermute(columns(fields, cot, 0), "gy", ring("gy", -1))
    clo = lax.ppermute(columns(xlo, xhi, BY - 8), "gy", ring("gy", 1))
    chi = lax.ppermute(columns(xlo, xhi, 0), "gy", ring("gy", -1))
    return (xlo, xhi, ylo, yhi, clo, chi)


def reduce_groups(nx, ny):
    flat = lambda x, y: x * ny + y
    near = [[flat(x, 2 * z + e) for x in range(nx) for e in range(2)] for z in range(ny // 2)]
    far = [[flat(x, 2 * z + e) for z in range(ny // 2)] for x in range(nx) for e in range(2)]
    return near, far


def per_device(fields, w_down, w_pool, w_mid, w_unpool, w_up, cotangent):
    nx, ny = lax.axis_size("gx"), lax.axis_size("gy")
    near, far = reduce_groups(nx, ny)
    n1, n2 = len(near[0]), len(far[0])
    rows = -(-TILES * 32 // (8 * n1)) * 8
    bands = build_bands(w_down, w_pool, w_mid, w_unpool, w_up)
    halos = exchange(fields, cotangent)
    output, grad_fields, terms = main_call(fields, cotangent, halos, bands, n1 * rows)
    swap = functools.partial(
        lax.all_to_all, axis_name=("gx", "gy"), split_axis=0, concat_axis=0, tiled=True
    )
    part = jnp.sum(swap(terms.reshape(n1, rows, 128), axis_index_groups=near), axis=0)
    part = swap(jnp.broadcast_to(part, (n2, rows, 128)), axis_index_groups=far)
    cells = fields.shape[0] * fields.shape[1] * 8 * nx * ny
    part = jnp.sum(part, axis=0) * (1.0 / math.sqrt(cells))
    whole = swap(jnp.broadcast_to(part, (n1, rows, 128)), axis_index_groups=near)
    down, pool, mid, unpool, up = unpack(whole.reshape(n1 * rows, 128))
    return (
        output,
        grad_fields,
        down.reshape(w_down.shape),
        pool.reshape(w_pool.shape),
        mid.reshape(w_mid.shape),
        unpool.reshape(w_unpool.shape),
        up.reshape(w_up.shape),
    )


def solution(mesh):
    placed = (P("gx", "gy", None), P(), P(), P(), P(), P(), P("gx", "gy", None))
    return jax.shard_map(
        per_device,
        mesh=mesh,
        in_specs=placed,
        out_specs=(P("gx", "gy", None), P("gx", "gy", None), P(), P(), P(), P(), P()),
        check_vma=False,
    )
```

time: 491 us -> 119 us (0.24); the launches traced: 484 us -> 118 us
  waiting for transfers between devices: 247 us -> 0.02 us
  local copies, waits for them, and re-layouts: 109 us -> 7.87 us
  blocking collectives: 0 us -> 60.5 us
  matrix products: 50.3 us -> 0 us
  Pallas kernels: 0 us -> 34.5 us
  starting transfers between devices: 47.1 us -> 14.6 us
  between operations: 15.5 us -> 0.83 us
  other arithmetic: 14.3 us -> 0.18 us
    psum x1 -> x0, waiting for transfers between devices: 246 us -> none  [in_one(): so_far = lax.psum(jnp.concatenate([a.ravel() for a in arrays]), axis)]
    convert_element_type x15 -> x0, local copies, waits for them, and re-layouts: 66.7 us -> none  [the longest x12 61 us: band_matrix(): band.reshape(9 * planes * weight.shape[3], planes * weight.shape[4])]
    all_to_all x0 -> x3, blocking collectives: none -> 60.5 us  [the longest x1 26.9 us: per_device(): swap(terms.reshape(n1, rows, 128), axis_index_groups=near)]
    dot_general x25 -> x0, matrix products: 50.3 us -> none  [the longest x6 18.8 us: band_matrix(): band = jnp.einsum('kpz,abkco->abpczo', shifts, weight.astype(jnp.float32))]
    pallas_call x0 -> x3, Pallas kernels: none -> 34.5 us  [the longest x1 29.3 us: main_call(): pl.pallas_call(main_kernel, out_shape=(block, block, jax.ShapeDtypeStruct...]
    ppermute x20 -> x6, starting transfers between devices: 47.1 us -> 14.6 us  [the longest x1 5.39 us: exchange(): yhi = lax.ppermute(columns(fields, cot, 0), 'gy', ring('gy', -1))]
    reshape x20 -> x0, local copies, waits for them, and re-layouts: 15.2 us -> none  [the longest x3 5.46 us: columns(): return cols.reshape(xs * ys, -1)]
    transpose x11 -> x0, local copies, waits for them, and re-layouts: 9.39 us -> none  [the longest x6 5.46 us: flipped(): return jnp.transpose(weight[::-1, ::-1, ::-1], (0, 1, 2, 4, 3))]
  transfers between devices with their start and end apart: 21 -> 6, of which waited for: 2 -> 0; matrix products, arithmetic and copies ran while one was open for 28% -> 0% of each run, Pallas kernels for 0% -> 2%
where the time goes in v1:
time: 119 us; the launch traced here: 118 us
  blocking collectives  60.5 us (51%)
  Pallas kernels  34.5 us (29%)
  starting transfers between devices  14.6 us (12%)
  local copies, waits for them, and re-layouts  7.87 us (7%)
    pallas_call x1, Pallas kernels, main_call(): pl.pallas_call(main_kernel, out_shape=(block, block, jax.ShapeDtypeStruct...  29.3 us
    all_to_all x1, blocking collectives, per_device(): swap(terms.reshape(n1, rows, 128), axis_index_groups=near)  26.9 us
    all_to_all x1, blocking collectives, per_device(): swap(jnp.broadcast_to(part, (n1, rows, 128)), axis_index_groups=near)  22.1 us
    all_to_all x1, blocking collectives, per_device(): part = swap(jnp.broadcast_to(part, (n2, rows, 128)), axis_index_groups=far)  11.4 us
    unnamed x24, local copies, waits for them, and re-layouts  5.76 us
    ppermute x1, starting transfers between devices, exchange(): yhi = lax.ppermute(columns(fields, cot, 0), 'gy', ring('gy', -1))  5.39 us
    ppermute x1, starting transfers between devices, exchange(): chi = lax.ppermute(columns(xlo, xhi, 0), 'gy', ring('gy', -1))  5.01 us
    pallas_call x1, Pallas kernels, unpack(): pl.pallas_call(unpack_kernel, out_shape=(shape(27, 32, 32), shape(4, 64,...  2.85 us
  transfers between devices with their start and end apart: 6, of which 0 were waited for; matrix products, arithmetic and copies ran while one was open for 0% of the time, Pallas kernels for 2%

profile of v1, /device:TPU:1, one launch (start us, length us, event | category | flops | bytes accessed | tf_op | source)
XLA Modules:
  0.0 118.5 jit_solution(6016400077811432562)
XLA Ops:
  0.6 0.0 copy-start
  0.7 1.0 fusion.3
  1.7 0.0 copy-start.10
  1.7 1.0 fusion.2
  2.7 2.8 %collective-permute-start = (bf16[12,32,256]{2,1,0:T(8,128)(2,1)S(1)}, bf16[12,32,256]{2,1,0:T(8,128)(2,1)S(1)}, u32[]{:S(2)}, u32[]{:S(2)}) collective-permute-start(bf16[12,32,256]{2,1,0:T(8,128)(2,1)S(1)} %pad_maximum_fusion), channel_id=1, source_target_pairs={{0,16},{16,32},{32,48},{48,64},{64,80},{80,96},{96,112},{112,128},... | collective-permute-start | bytes 589832 | tf_op jit(solution)/shard_map/ppermute | solution.py:492
  5.5 0.7 collective-permute-start.1
  6.2 0.0 copy-done.1
  6.2 0.7 collective-permute-start.2
  7.0 5.4 %collective-permute-start.3 = (bf16[32,8,256]{2,1,0:T(8,128)(2,1)S(1)}, bf16[32,8,256]{2,1,0:T(8,128)(2,1)S(1)}, u32[]{:S(2)}, u32[]{:S(2)}) collective-permute-start(bf16[32,8,256]{2,1,0:T(8,128)(2,1)S(1)} %pad_maximum_fusion.3), channel_id=1, source_target_pairs={{0,15},{1,0},{2,1},{3,2},{4,3},{5,4},{6,5},{7,6},{8,7},{9,8},{10,9... | collective-permute-start | bytes 393224 | tf_op jit(solution)/shard_map/ppermute | solution.py:495
  12.4 0.1 copy.16
  12.5 0.0 collective-permute-done.xlo
  12.5 0.0 collective-permute-done.1.xhi
  12.6 0.1 collective-permute-start.4
  12.7 5.0 %collective-permute-start.5 = (bf16[24,8,256]{2,1,0:T(8,128)(2,1)S(1)}, bf16[24,8,256]{2,1,0:T(8,128)(2,1)S(1)}, u32[]{:S(2)}, u32[]{:S(2)}) collective-permute-start(bf16[24,8,256]{2,1,0:T(8,128)(2,1)S(1)} %pad_maximum_fusion.5), channel_id=1, source_target_pairs={{0,15},{1,0},{2,1},{3,2},{4,3},{5,4},{6,5},{7,6},{8,7},{9,8},{10,9... | collective-permute-start | bytes 294920 | tf_op jit(solution)/shard_map/ppermute | solution.py:497
  17.7 0.0 copy-done.5
  17.7 2.3 %bands.1 = (bf16[2304,256]{1,0:T(8,128)(2,1)S(1)}, bf16[1024,256]{1,0:T(8,128)(2,1)S(1)}, bf16[2304,256]{1,0:T(8,128)(2,1)S(1)}, bf16[1024,256]{1,0:T(8,128)(2,1)S(1)}, bf16[2304,256]{1,0:T(8,128)(2,1)S(1)}) custom-call(bf16[864,32]{1,0:T(8,128)(2,1)S(1)} %bitcast.14, bf16[4,64,64]{2,1,0:T(8,128)(2,1)S(1)} %bitcast.16, bf16[1728,64]{1,0:T(8,128)(2,1)S(1)} %bitcast.13, ...), custom_call_target="tpu_custom_call" | custom-call | flops 2000000000 | bytes 8000000 | tf_op jit(solution)/shard_map/bands/pallas_call | solution.py:87
  20.1 1.0 copy-done.6
  21.1 1.0 copy-done.7
  22.1 1.0 copy-done.8
  23.2 0.8 copy-done.9
  23.9 0.0 collective-permute-done.2.ylo
  24.0 0.0 collective-permute-done.3.yhi
  24.0 0.0 collective-permute-done.4.clo
  24.0 0.0 collective-permute-done.5.chi
  24.0 29.3 %network.1 = (bf16[16,32,256]{2,1,0:T(8,128)(2,1)}, bf16[16,32,256]{2,1,0:T(8,128)(2,1)}, f32[1792,128]{1,0:T(8,128)}) custom-call(bf16[16,32,256]{2,1,0:T(8,128)(2,1)S(1)} %copy-done, bf16[16,32,256]{2,1,0:T(8,128)(2,1)S(1)} %copy-done.1, bf16[12,32,256]{2,1,0:T(8,128)(2,1)S(1)} %collective-permute-done.xlo, ...), custom_call_target="tpu_custom_call" | custom-call | flops 10000000000 | bytes 10000000 | tf_op jit(solution)/shard_map/network/pallas_call | solution.py:421
  53.2 26.9 %all_to_all.15 = f32[32,56,128]{2,1,0:T(8,128)S(1)} all-to-all(f32[32,56,128]{2,1,0:T(8,128)} %bitcast.18), channel_id=1, replica_groups={{0,1,16,17,32,33,48,49,64,65,80,81,96,97,112,113,128,129,144,145,160,16..., dimensions={0} | all-to-all | bytes 1835008 | tf_op jit(solution)/shard_map/all_to_all | solution.py:519
  80.2 0.1 reduce_sum.18
  80.3 11.4 %all_to_all.16 = f32[8,56,128]{2,1,0:T(8,128)S(1)} all-to-all(f32[8,56,128]{2,1,0:T(8,128)S(1)} %broadcast_in_dim.6), channel_id=1, replica_groups={{0,2,4,6,8,10,12,14},{1,3,5,7,9,11,13,15},{16,18,20,22,24,26,28,30},{17..., dimensions={0} | all-to-all | bytes 458752 | tf_op jit(solution)/shard_map/all_to_all | solution.py:520
  91.7 0.1 broadcast_in_dim.7
  91.8 22.1 %all_to_all.17 = f32[32,56,128]{2,1,0:T(8,128)} all-to-all(f32[32,56,128]{2,1,0:T(8,128)S(1)} %broadcast_in_dim.7), channel_id=1, replica_groups={{0,1,16,17,32,33,48,49,64,65,80,81,96,97,112,113,128,129,144,145,160,16..., dimensions={0} | all-to-all | bytes 1835008 | tf_op jit(solution)/shard_map/all_to_all | solution.py:523
  113.9 2.9 %unpack.1 = (f32[27,32,32]{2,1,0:T(8,128)}, f32[4,64,64]{2,1,0:T(8,128)}, f32[27,64,64]{2,1,0:T(8,128)}, f32[8,64,32]{2,1,0:T(8,128)}, f32[27,32,32]{2,1,0:T(8,128)}) custom-call(f32[1792,128]{1,0:T(8,128)} %bitcast.17), custom_call_target="tpu_custom_call" | custom-call | tf_op jit(solution)/shard_map/unpack/pallas_call | solution.py:471
  116.8 1.7 %copy.17 = f32[2,2,2,64,32]{3,4,2,1,0:T(8,128)} copy(f32[2,2,2,64,32]{4,3,2,1,0:T(8,128)} %bitcast.19) | data formatting | bytes 131072
  (26 shorter events, 0.2 us)
Async XLA Ops:
  0.6 5.6 %copy-start.1 = (bf16[16,32,256]{2,1,0:T(8,128)(2,1)S(1)}, bf16[16,32,256]{2,1,0:T(8,128)(2,1)}, u32[]{:S(2)}) copy-start(bf16[16,32,256]{2,1,0:T(8,128)(2,1)} %cc.1) | copy-start | bytes 786436
  0.6 5.5 %copy-start = (bf16[16,32,256]{2,1,0:T(8,128)(2,1)S(1)}, bf16[16,32,256]{2,1,0:T(8,128)(2,1)}, u32[]{:S(2)}) copy-start(bf16[16,32,256]{2,1,0:T(8,128)(2,1)} %fc.1) | copy-start | bytes 786436
  1.7 10.7 %copy-start.10 = (bf16[2,2,2,64,32]{3,4,2,1,0:T(8,128)(2,1)S(1)}, bf16[2,2,2,64,32]{3,4,2,1,0:T(8,128)(2,1)}, u32[]{:S(2)}) copy-start(bf16[2,2,2,64,32]{3,4,2,1,0:T(8,128)(2,1)} %param.11) | copy-start | bytes 98308
  2.7 9.8 %collective-permute-start = (bf16[12,32,256]{2,1,0:T(8,128)(2,1)S(1)}, bf16[12,32,256]{2,1,0:T(8,128)(2,1)S(1)}, u32[]{:S(2)}, u32[]{:S(2)}) collective-permute-start(bf16[12,32,256]{2,1,0:T(8,128)(2,1)S(1)} %pad_maximum_fusion), channel_id=1, source_target_pairs={{0,16},{16,32},{32,48},{48,64},{64,80},{80,96},{96,112},{112,128},... | collective-permute-start | bytes 589832 | tf_op jit(solution)/shard_map/ppermute | solution.py:492
  5.5 12.2 %copy-start.2 = (bf16[3,3,3,64,64]{4,3,2,1,0:T(8,128)(2,1)S(1)}, bf16[3,3,3,64,64]{4,3,2,1,0:T(8,128)(2,1)}, u32[]{:S(2)}) copy-start(bf16[3,3,3,64,64]{4,3,2,1,0:T(8,128)(2,1)} %param.10) | copy-start | bytes 663556
  5.5 12.2 %copy-start.3 = (bf16[3,3,3,32,32]{4,3,2,1,0:T(8,128)(2,1)S(1)}, bf16[3,3,3,32,32]{4,3,2,1,0:T(8,128)(2,1)}, u32[]{:S(2)}) copy-start(bf16[3,3,3,32,32]{4,3,2,1,0:T(8,128)(2,1)} %param.8) | copy-start | bytes 165892
  5.5 12.2 %copy-start.4 = (bf16[3,3,3,32,32]{4,3,2,1,0:T(8,128)(2,1)S(1)}, bf16[3,3,3,32,32]{4,3,2,1,0:T(8,128)(2,1)}, u32[]{:S(2)}) copy-start(bf16[3,3,3,32,32]{4,3,2,1,0:T(8,128)(2,1)} %param.12) | copy-start | bytes 165892
  5.5 12.2 %copy-start.5 = (bf16[2,2,2,32,64]{4,3,2,1,0:T(8,128)(2,1)S(1)}, bf16[2,2,2,32,64]{4,3,2,1,0:T(8,128)(2,1)}, u32[]{:S(2)}) copy-start(bf16[2,2,2,32,64]{4,3,2,1,0:T(8,128)(2,1)} %param.9) | copy-start | bytes 98308
  5.5 7.0 %collective-permute-start.1 = (bf16[12,32,256]{2,1,0:T(8,128)(2,1)S(1)}, bf16[12,32,256]{2,1,0:T(8,128)(2,1)S(1)}, u32[]{:S(2)}, u32[]{:S(2)}) collective-permute-start(bf16[12,32,256]{2,1,0:T(8,128)(2,1)S(1)} %pad_maximum_fusion.1), channel_id=1, source_target_pairs={{0,240},{16,0},{32,16},{48,32},{64,48},{80,64},{96,80},{112,96},{1... | collective-permute-start | bytes 589832 | tf_op jit(solution)/shard_map/ppermute | solution.py:493
  6.2 17.7 %collective-permute-start.2 = (bf16[32,8,256]{2,1,0:T(8,128)(2,1)S(1)}, bf16[32,8,256]{2,1,0:T(8,128)(2,1)S(1)}, u32[]{:S(2)}, u32[]{:S(2)}) collective-permute-start(bf16[32,8,256]{2,1,0:T(8,128)(2,1)S(1)} %pad_maximum_fusion.2), channel_id=1, source_target_pairs={{0,1},{1,2},{2,3},{3,4},{4,5},{5,6},{6,7},{7,8},{8,9},{9,10},{10,1... | collective-permute-start | bytes 393224 | tf_op jit(solution)/shard_map/ppermute | solution.py:494
  7.0 17.0 %collective-permute-start.3 = (bf16[32,8,256]{2,1,0:T(8,128)(2,1)S(1)}, bf16[32,8,256]{2,1,0:T(8,128)(2,1)S(1)}, u32[]{:S(2)}, u32[]{:S(2)}) collective-permute-start(bf16[32,8,256]{2,1,0:T(8,128)(2,1)S(1)} %pad_maximum_fusion.3), channel_id=1, source_target_pairs={{0,15},{1,0},{2,1},{3,2},{4,3},{5,4},{6,5},{7,6},{8,7},{9,8},{10,9... | collective-permute-start | bytes 393224 | tf_op jit(solution)/shard_map/ppermute | solution.py:495
  12.6 11.4 %collective-permute-start.4 = (bf16[24,8,256]{2,1,0:T(8,128)(2,1)S(1)}, bf16[24,8,256]{2,1,0:T(8,128)(2,1)S(1)}, u32[]{:S(2)}, u32[]{:S(2)}) collective-permute-start(bf16[24,8,256]{2,1,0:T(8,128)(2,1)S(1)} %pad_maximum_fusion.4), channel_id=1, source_target_pairs={{0,1},{1,2},{2,3},{3,4},{4,5},{5,6},{6,7},{7,8},{8,9},{9,10},{10,1... | collective-permute-start | bytes 294920 | tf_op jit(solution)/shard_map/ppermute | solution.py:496
  12.7 11.3 %collective-permute-start.5 = (bf16[24,8,256]{2,1,0:T(8,128)(2,1)S(1)}, bf16[24,8,256]{2,1,0:T(8,128)(2,1)S(1)}, u32[]{:S(2)}, u32[]{:S(2)}) collective-permute-start(bf16[24,8,256]{2,1,0:T(8,128)(2,1)S(1)} %pad_maximum_fusion.5), channel_id=1, source_target_pairs={{0,15},{1,0},{2,1},{3,2},{4,3},{5,4},{6,5},{7,6},{8,7},{9,8},{10,9... | collective-permute-start | bytes 294920 | tf_op jit(solution)/shard_map/ppermute | solution.py:497
  20.1 1.1 copy-start.6
  21.1 1.0 copy-start.7
  22.1 1.0 copy-start.8
  23.2 0.8 copy-start.9

commit v2 on v1

--- a/solution.py
+++ b/solution.py
@@ -12,6 +12,7 @@
 F32 = jnp.float32
 NN = (((1,), (0,)), ((), ()))
 NT = (((1,), (1,)), ((), ()))
+TN = (((0,), (0,)), ((), ()))
 
 HF = 7
 HC = 5
@@ -74,7 +75,7 @@
     high = repeat_matrix(32, W, 64, 32)
     for q in range(4):
         pool = dot(wp[q], same)
-        unpool = dot(wu[2 * q], low) + dot(wu[2 * q + 1], high)
+        unpool = dot(wu[2 * q], low, TN) + dot(wu[2 * q + 1], high, TN)
         for y in range(4):
             rows = slice(q * W + y * 64, q * W + y * 64 + 64)
             pm[rows, :] = jnp.where(group == y, pool, 0.0).astype(BF)
@@ -95,7 +96,7 @@
         w_down.reshape(27 * 32, 32),
         w_pool.reshape(4, 64, 64),
         w_mid.reshape(27 * 64, 64),
-        w_unpool.reshape(8, 64, 32),
+        w_unpool.transpose(0, 1, 2, 4, 3).reshape(8, 32, 64),
         w_up.reshape(27 * 32, 32),
     )
 
@@ -192,9 +193,9 @@
 
 def main_kernel(
     fc, cc, xlo, xhi, ylo, yhi, clo, chi, bd, pm, bm, um, bu,
-    out, gf, terms,
+    terms, v3s, v3d,
     fe, ce, hid, ds_down, skp, ds_up, dup, ddn,
-    v3f, v3c, v3fl, v3s, v3d,
+    v3f, v3c, v3fl,
     parts, co, mid, ds_pool, ds_mid, dmid, v3m, v3dm, v3ml, local,
     hi, lo, him, lom, dsc,
 ):
@@ -226,13 +227,13 @@
     put_rows(hid, slice(30, 32), zero)
 
     def down(i):
-        pre = conv_rows(v3f, 4 * i, 4, bd)
+        pre = conv_rows(v3f, 14 * i, 14, bd)
         sig = jax.nn.sigmoid(pre)
-        at = pl.ds(2 + 4 * i, 4)
-        put_rows(hid, at, rounded(pre * sig).reshape(4, EY, W))
-        put_rows(ds_down, at, (sig * (1.0 + pre * (1.0 - sig))).reshape(4, EY, W))
-
-    loop(7, down)
+        at = pl.ds(2 + 14 * i, 14)
+        put_rows(hid, at, rounded(pre * sig).reshape(14, EY, W))
+        put_rows(ds_down, at, (sig * (1.0 + pre * (1.0 - sig))).reshape(14, EY, W))
+
+    loop(2, down)
 
     pad = jnp.zeros((CY - EY // 2, W), F32)
 
@@ -247,58 +248,49 @@
     def pool(i):
         pre = None
         for q in range(4):
-            piece = parts[q, pl.ds(4 * i, 4)].reshape(4 * CY, W)
+            piece = parts[q, pl.ds(8 * i, 8)].reshape(8 * CY, W)
             part = dot(piece, pm[q * W : (q + 1) * W, :])
             pre = part if pre is None else pre + part
         sig = jax.nn.sigmoid(pre)
-        co[pl.ds(4 * i, 4)] = rounded(pre * sig).reshape(4, CY, W)
-        ds_pool[pl.ds(4 * i, 4)] = (sig * (1.0 + pre * (1.0 - sig))).reshape(4, CY, W)
-
-    loop(4, pool)
+        co[pl.ds(8 * i, 8)] = rounded(pre * sig).reshape(8, CY, W)
+        ds_pool[pl.ds(8 * i, 8)] = (sig * (1.0 + pre * (1.0 - sig))).reshape(8, CY, W)
+
+    loop(2, pool)
 
     loop(14, lambda i: taps_to_lanes(co, 1 + i, v3m, i, 0, CY))
 
-    def middle(i):
-        pre = conv_rows(v3m, 4 * i, 4, bm)
-        sig = jax.nn.sigmoid(pre)
-        own = co[pl.ds(2 + 4 * i, 4)].reshape(4 * CY, W)
-        mid[pl.ds(2 + 4 * i, 4)] = (own + pre * sig).astype(BF).reshape(4, CY, W)
-        ds_mid[pl.ds(2 + 4 * i, 4)] = (sig * (1.0 + pre * (1.0 - sig))).reshape(4, CY, W)
-
-    loop(3, middle)
+    pre_mid = conv_rows(v3m, 0, 12, bm)
+    sig_mid = jax.nn.sigmoid(pre_mid)
+    own_mid = co[2:14].reshape(12 * CY, W)
+    mid[2:14] = (own_mid + pre_mid * sig_mid).astype(BF).reshape(12, CY, W)
+    ds_mid[2:14] = (sig_mid * (1.0 + pre_mid * (1.0 - sig_mid))).reshape(12, CY, W)
 
     def up(x):
-        m = mid[pl.ds(2 + 2 * x, 2)].reshape(2 * CY, W)
+        m = mid[pl.ds(2 + 6 * x, 6)].reshape(6 * CY, W)
         for i in range(2):
             for j in range(2):
                 q = 2 * i + j
                 lifted = dot(m, um[q * W : (q + 1) * W, :])
-                for r in range(2):
-                    row = 2 * (2 + 2 * x + r) + i
+                for r in range(6):
+                    row = 2 * (2 + 6 * x + r) + i
                     own = get_every_second(hid, row, j, EY // 2)
                     pre = own + lifted[r * CY : r * CY + EY // 2]
                     sig = jax.nn.sigmoid(pre)
                     put_every_second(skp, row, j, rounded(pre * sig))
                     put_every_second(ds_up, row, j, sig * (1.0 + pre * (1.0 - sig)))
 
-    loop(6, up)
+    loop(2, up)
 
     loop(18, lambda i: taps_to_lanes(skp, 7 + i, v3s, i, 8, BY))
 
-    def output(i):
-        total = conv_rows(v3s, 4 * i, 4, bu).reshape(4, BY, W)
-        out[pl.ds(4 * i, 4)] = (fc[pl.ds(4 * i, 4)].astype(F32) + total).astype(BF)
-
-    loop(4, output)
-
     loop(26, lambda i: taps_to_lanes(ce, 3 + i, v3c, i, 0, EY))
 
     def d_up(i):
-        total = conv_t_rows(v3c, 4 * i, 4, bu)
-        at = pl.ds(4 + 4 * i, 4)
-        put_rows(dup, at, rounded(total.reshape(4, EY, W) * get_rows(ds_up, at)))
-
-    loop(6, d_up)
+        total = conv_t_rows(v3c, 12 * i, 12, bu)
+        at = pl.ds(4 + 12 * i, 12)
+        put_rows(dup, at, rounded(total.reshape(12, EY, W) * get_rows(ds_up, at)))
+
+    loop(2, d_up)
 
     cot_t = cc[...].reshape(BX * BY, W).astype(F32).T.astype(BF)
     fold = repeat_matrix(32, W, 32, 0)
@@ -308,9 +300,8 @@
         total = dot(matrix, hi[...], NT) + dot(matrix, lo[...], NT)
         for t in range(count):
             rows = matrix.shape[0]
-            terms[(tile * 32 + t * rows) : (tile * 32 + (t + 1) * rows), :] = total[
-                :, t * 128 : (t + 1) * 128
-            ]
+            part = total[:, t * 128 : (t + 1) * 128]
+            terms[(tile * 32 + t * rows) : (tile * 32 + (t + 1) * rows), :] = part.astype(BF)
 
     conv_weight_terms(cot_t, v3s, BX, 32, hi, lo, dsc)
     fold_to(fold, hi, lo, 7, 7)
@@ -323,6 +314,12 @@
 
     loop(8, lambda x: own_parts(dup, x))
     mid_t = mid[4:12].astype(F32)[:, 0:24][:, 4:20].reshape(128, W).T.astype(BF)
+
+    def fold_four(tile):
+        total = dot(fold_mid, him[0:256, :], NT) + dot(fold_mid, lom[0:256, :], NT)
+        for t in range(2):
+            rows = slice(tile * 32 + t * 64, tile * 32 + (t + 1) * 64)
+            terms[rows, :] = total[:, t * 128 : (t + 1) * 128].astype(BF)
 
     def plain_terms(left, q, row):
         d = dot(left, local[q].reshape(128, W))
@@ -334,26 +331,16 @@
 
     for q in range(4):
         plain_terms(mid_t, q, 64 * q)
-    fold_cols = (him[0:256, :], lom[0:256, :])
-    unpool = dot(fold_cols[0], fold_mid, NT) + dot(fold_cols[1], fold_mid, NT)
+    fold_four(46)
+
+    loop(12, lambda x: to_parts(dup, 2 + x))
+
+    d_middle = None
     for q in range(4):
-        half = (q % 2) * 64
-        rows = slice(46 * 32 + (q // 2) * 64, 46 * 32 + (q // 2 + 1) * 64)
-        terms[rows, half : half + 64] = unpool[q * 64 : (q + 1) * 64, :]
-
-    loop(12, lambda x: to_parts(dup, 2 + x))
-
-    def d_middle(i):
-        total = None
-        at = pl.ds(2 + 4 * i, 4)
-        for q in range(4):
-            piece = parts[q, at].reshape(4 * CY, W)
-            part = dot(piece, um[q * W : (q + 1) * W, :], NT)
-            total = part if total is None else total + part
-        dmid[at] = rounded(total * ds_mid[at].reshape(4 * CY, W)).reshape(4, CY, W)
-        ds_mid[at] = total.reshape(4, CY, W)
-
-    loop(3, d_middle)
+        part = dot(parts[q, 2:14].reshape(12 * CY, W), um[q * W : (q + 1) * W, :], NT)
+        d_middle = part if d_middle is None else d_middle + part
+    dmid[2:14] = rounded(d_middle * ds_mid[2:14].reshape(12 * CY, W)).reshape(12, CY, W)
+    ds_mid[2:14] = d_middle.reshape(12, CY, W)
 
     loop(12, lambda i: taps_to_lanes(dmid, 2 + i, v3dm, i, 0, CY))
 
@@ -367,27 +354,20 @@
     conv_weight_terms(dmid_t, v3ml, 8, 64, him, lom, dsc)
     fold_to(fold_mid, him, lom, 14, 14)
 
-    def d_pool(i):
-        at = pl.ds(3 + 2 * i, 2)
-        total = conv_t_rows(v3dm, 2 * i, 2, bm).reshape(2, CY, W)
-        ds_pool[at] = rounded((ds_mid[at] + total) * ds_pool[at])
-
-    loop(5, d_pool)
-
-    def d_down(i):
-        dp = ds_pool[pl.ds(3 + 2 * i, 2)].reshape(2 * CY, W).astype(BF)
-        for a in range(2):
-            for j in range(2):
-                q = 2 * a + j
-                back = dot(dp, pm[q * W : (q + 1) * W, :], NT)
-                for r in range(2):
-                    row = 2 * (3 + 2 * i + r) + a
-                    own = get_every_second(dup, row, j, EY // 2)
-                    d_hidden = own + back[r * CY : r * CY + EY // 2]
-                    slope = get_every_second(ds_down, row, j, EY // 2)
-                    put_every_second(ddn, row, j, rounded(d_hidden * slope))
-
-    loop(5, d_down)
+    d_coarse = ds_mid[3:13] + conv_t_rows(v3dm, 0, 10, bm).reshape(10, CY, W)
+    ds_pool[3:13] = rounded(d_coarse * ds_pool[3:13])
+
+    dp = ds_pool[3:13].reshape(10 * CY, W).astype(BF)
+    for i in range(2):
+        for j in range(2):
+            q = 2 * i + j
+            back = dot(dp, pm[q * W : (q + 1) * W, :], NT)
+            for r in range(10):
+                row = 2 * (3 + r) + i
+                own = get_every_second(dup, row, j, EY // 2)
+                d_hidden = own + back[r * CY : r * CY + EY // 2]
+                slope = get_every_second(ds_down, row, j, EY // 2)
+                put_every_second(ddn, row, j, rounded(d_hidden * slope))
 
     loop(18, lambda i: taps_to_lanes(ddn, 7 + i, v3d, i, 8, BY))
 
@@ -399,35 +379,43 @@
     pool_t = ds_pool[4:12][:, 4:20].reshape(128, W).T.astype(BF)
     for q in range(4):
         plain_terms(pool_t, q, 64 * q)
-    pooled = dot(fold_mid, him[0:256, :], NT) + dot(fold_mid, lom[0:256, :], NT)
-    for t in range(2):
-        terms[42 * 32 + t * 64 : 42 * 32 + (t + 1) * 64, :] = pooled[:, t * 128 : (t + 1) * 128]
+    fold_four(42)
     rest = terms.shape[0] - TILES * 32
     if rest > 0:
-        terms[TILES * 32 :, :] = jnp.zeros((rest, 128), F32)
-
-    def grad_fields(i):
-        total = conv_t_rows(v3d, 4 * i, 4, bd).reshape(4, BY, W)
-        gf[pl.ds(4 * i, 4)] = (cc[pl.ds(4 * i, 4)].astype(F32) + total).astype(BF)
-
-    loop(4, grad_fields)
+        terms[TILES * 32 :, :] = jnp.zeros((rest, 128), BF)
+
+
+def finish_kernel(fc, cc, v3s, v3d, bd, bu, out, gf):
+    total = conv_rows(v3s, 0, BX, bu).reshape(BX, BY, W)
+    out[...] = (fc[...].astype(F32) + total).astype(BF)
+    total = conv_t_rows(v3d, 0, BX, bd).reshape(BX, BY, W)
+    gf[...] = (cc[...].astype(F32) + total).astype(BF)
+
+
+def finish_call(fields, cot, v3s, v3d, bands):
+    block = jax.ShapeDtypeStruct((BX, BY, W), BF)
+    return pl.pallas_call(
+        finish_kernel,
+        out_shape=(block, block),
+        compiler_params=pltpu.CompilerParams(vmem_limit_bytes=20 * 1024 * 1024),
+        cost_estimate=pl.CostEstimate(flops=3 * 10**9, bytes_accessed=10**7, transcendentals=0),
+        name="finish",
+    )(fields, cot, v3s, v3d, bands[0], bands[4])
 
 
 def main_call(fields, cot, halos, bands, term_rows):
-    block = jax.ShapeDtypeStruct((BX, BY, W), BF)
+    taps = jax.ShapeDtypeStruct((18, BY, 3 * W), BF)
     fine = pltpu.VMEM((EX, EY, W), F32)
     split = pltpu.VMEM((2, EX, EY, 128), F32)
     coarse = pltpu.VMEM((CX, CY, W), F32)
     return pl.pallas_call(
         main_kernel,
-        out_shape=(block, block, jax.ShapeDtypeStruct((term_rows, 128), F32)),
+        out_shape=(jax.ShapeDtypeStruct((term_rows, 128), BF), taps, taps),
         scratch_shapes=[fine] * 2
         + [split] * 6
         + [
             pltpu.VMEM((30, EY, 3 * W), BF),
             pltpu.VMEM((26, EY, 3 * W), BF),
-            pltpu.VMEM((18, BY, 3 * W), BF),
-            pltpu.VMEM((18, BY, 3 * W), BF),
             pltpu.VMEM((18, BY, 3 * W), BF),
             pltpu.VMEM((4, CX, CY, W), BF),
             coarse,
@@ -445,7 +433,7 @@
             pltpu.VMEM((28 * 64, W), BF),
             pltpu.VMEM((W, 3 * W), F32),
         ],
-        compiler_params=pltpu.CompilerParams(vmem_limit_bytes=52 * 1024 * 1024),
+        compiler_params=pltpu.CompilerParams(vmem_limit_bytes=36 * 1024 * 1024),
         cost_estimate=pl.CostEstimate(flops=10**10, bytes_accessed=10**7, transcendentals=10**6),
         name="network",
     )(fields, cot, *halos, *bands)
@@ -454,16 +442,14 @@
 def unpack_kernel(terms, down, pool, mid, unpool, up):
     for u in range(27):
         row, lane = (u // 4) * 32, (u % 4) * 32
-        down[u] = terms[row : row + 32, lane : lane + 32]
-        up[u] = terms[224 + row : 224 + row + 32, lane : lane + 32]
+        down[u] = terms[row : row + 32, lane : lane + 32].astype(F32)
+        up[u] = terms[224 + row : 224 + row + 32, lane : lane + 32].astype(F32)
         row, lane = 14 * 32 + (u // 2) * 64, (u % 2) * 64
-        mid[u] = terms[row : row + 64, lane : lane + 64]
+        mid[u] = terms[row : row + 64, lane : lane + 64].astype(F32)
     for q in range(4):
         row, lane = 42 * 32 + (q // 2) * 64, (q % 2) * 64
-        pool[q] = terms[row : row + 64, lane : lane + 64]
-        for l in range(2):
-            row, lane = 46 * 32 + (q // 2) * 64, (q % 2) * 64 + l * 32
-            unpool[2 * q + l] = terms[row : row + 64, lane : lane + 32]
+        pool[q] = terms[row : row + 64, lane : lane + 64].astype(F32)
+        unpool[q] = terms[128 + row : 128 + row + 64, lane : lane + 64].astype(F32)
 
 
 def unpack(terms):
@@ -471,7 +457,7 @@
     return pl.pallas_call(
         unpack_kernel,
         out_shape=(
-            shape(27, 32, 32), shape(4, 64, 64), shape(27, 64, 64), shape(8, 64, 32),
+            shape(27, 32, 32), shape(4, 64, 64), shape(27, 64, 64), shape(4, 64, 64),
             shape(27, 32, 32),
         ),
         name="unpack",
@@ -512,14 +498,16 @@
     rows = -(-TILES * 32 // (8 * n1)) * 8
     bands = build_bands(w_down, w_pool, w_mid, w_unpool, w_up)
     halos = exchange(fields, cotangent)
-    output, grad_fields, terms = main_call(fields, cotangent, halos, bands, n1 * rows)
+    terms, v3s, v3d = main_call(fields, cotangent, halos, bands, n1 * rows)
     swap = functools.partial(
         lax.all_to_all, axis_name=("gx", "gy"), split_axis=0, concat_axis=0, tiled=True
     )
-    part = jnp.sum(swap(terms.reshape(n1, rows, 128), axis_index_groups=near), axis=0)
+    part = swap(terms.reshape(n1, rows, 128), axis_index_groups=near)
+    output, grad_fields = finish_call(fields, cotangent, v3s, v3d, bands)
+    part = jnp.sum(part.astype(F32), axis=0)
     part = swap(jnp.broadcast_to(part, (n2, rows, 128)), axis_index_groups=far)
     cells = fields.shape[0] * fields.shape[1] * 8 * nx * ny
-    part = jnp.sum(part, axis=0) * (1.0 / math.sqrt(cells))
+    part = (jnp.sum(part, axis=0) * (1.0 / math.sqrt(cells))).astype(BF)
     whole = swap(jnp.broadcast_to(part, (n1, rows, 128)), axis_index_groups=near)
     down, pool, mid, unpool, up = unpack(whole.reshape(n1 * rows, 128))
     return (
@@ -528,7 +516,7 @@
         down.reshape(w_down.shape),
         pool.reshape(w_pool.shape),
         mid.reshape(w_mid.shape),
-        unpool.reshape(w_unpool.shape),
+        unpool.reshape(2, 2, 2, 32, 64).transpose(0, 1, 2, 4, 3),
         up.reshape(w_up.shape),
     )
 

time: 119 us -> 93.3 us (0.78)
  blocking collectives: 60.5 us -> 34.6 us
  Pallas kernels: 34.5 us -> 22.4 us
  starting transfers between devices: 14.6 us -> 22.1 us
  waiting for transfers between devices: 0.02 us -> 5.76 us
    all_to_all x2 -> x1, blocking collectives: 49.1 us -> 22.4 us  [per_device(): part = swap(terms.reshape(n1, rows, 128), axis_index_groups=near)]
    pallas_call x1 -> x2, Pallas kernels: 29.3 us -> 17.5 us  [the longest x1 15.3 us: main_call(): pl.pallas_call(main_kernel, out_shape=(jax.ShapeDtypeStruct((term_rows, 1...]
    all_to_all x0 -> x1, starting transfers between devices: none -> 7.17 us  [per_device(): swap(jnp.broadcast_to(part, (n1, rows, 128)), axis_index_groups=near)]
    all_to_all x0 -> x1, waiting for transfers between devices: none -> 5.75 us  [per_device(): swap(jnp.broadcast_to(part, (n1, rows, 128)), axis_index_groups=near)]
    unnamed x24, local copies, waits for them, and re-layouts: 5.76 us -> 4.06 us
  transfers between devices with their start and end apart: 6 -> 7, of which waited for: 0 -> 1; matrix products, arithmetic and copies ran while one was open for 0% -> 0% of each run, Pallas kernels for 2% -> 5%
where the time goes in v2:
time: 93.3 us; the launch traced here: 92.8 us
  blocking collectives  34.6 us (37%)
  Pallas kernels  22.4 us (24%)
  starting transfers between devices  22.1 us (24%)
  local copies, waits for them, and re-layouts  6.93 us (7%)
  waiting for transfers between devices  5.76 us (6%)
    all_to_all x1, blocking collectives, per_device(): part = swap(terms.reshape(n1, rows, 128), axis_index_groups=near)  22.4 us
    pallas_call x1, Pallas kernels, main_call(): pl.pallas_call(main_kernel, out_shape=(jax.ShapeDtypeStruct((term_rows, 1...  15.3 us
    all_to_all x1, blocking collectives, per_device(): part = swap(jnp.broadcast_to(part, (n2, rows, 128)), axis_index_groups=far)  12.2 us
    all_to_all x1, starting transfers between devices, per_device(): swap(jnp.broadcast_to(part, (n1, rows, 128)), axis_index_groups=near)  7.17 us
    all_to_all x1, waiting for transfers between devices, per_device(): swap(jnp.broadcast_to(part, (n1, rows, 128)), axis_index_groups=near)  5.75 us
    ppermute x1, starting transfers between devices, exchange(): yhi = lax.ppermute(columns(fields, cot, 0), 'gy', ring('gy', -1))  5.39 us
    ppermute x1, starting transfers between devices, exchange(): chi = lax.ppermute(columns(xlo, xhi, 0), 'gy', ring('gy', -1))  5.34 us
    unnamed x24, local copies, waits for them, and re-layouts  4.06 us
  transfers between devices with their start and end apart: 7, of which 1 were waited for; matrix products, arithmetic and copies ran while one was open for 0% of the time, Pallas kernels for 5%

profile of v2, /device:TPU:1, one launch (start us, length us, event | category | flops | bytes accessed | tf_op | source)
XLA Modules:
  0.0 92.8 jit_solution(14852758453106230695)
XLA Ops:
  0.6 0.0 copy-start
  0.7 1.0 %fusion.3 = (bf16[5,32,256]{2,1,0:T(8,128)(2,1)S(1)}, bf16[5,32,256]{2,1,0:T(8,128)(2,1)S(1)}) fusion(bf16[16,32,256]{2,1,0:T(8,128)(2,1)} %cc.3), kind=kLoop, calls=%fused_computation.11 | loop fusion | bytes 327680 | tf_op jit(solution)/shard_map/slice | solution.py:477
  1.7 1.0 %fusion.2 = (bf16[7,32,256]{2,1,0:T(8,128)(2,1)S(1)}, bf16[7,32,256]{2,1,0:T(8,128)(2,1)S(1)}) fusion(bf16[16,32,256]{2,1,0:T(8,128)(2,1)} %fc.3), kind=kLoop, calls=%fused_computation.10 | loop fusion | bytes 458752 | tf_op jit(solution)/shard_map/slice | solution.py:477
  2.7 0.0 copy-start.2
  2.7 0.0 copy-start.3
  2.7 0.0 copy-start.4
  2.7 0.0 copy-start.5
  2.7 0.0 copy-start.6
  2.7 2.8 %collective-permute-start = (bf16[12,32,256]{2,1,0:T(8,128)(2,1)S(1)}, bf16[12,32,256]{2,1,0:T(8,128)(2,1)S(1)}, u32[]{:S(2)}, u32[]{:S(2)}) collective-permute-start(bf16[12,32,256]{2,1,0:T(8,128)(2,1)S(1)} %pad_maximum_fusion), channel_id=1, source_target_pairs={{0,16},{16,32},{32,48},{48,64},{64,80},{80,96},{96,112},{112,128},... | collective-permute-start | bytes 589832 | tf_op jit(solution)/shard_map/ppermute | solution.py:478
  5.5 0.7 collective-permute-start.1
  6.2 0.7 collective-permute-start.2
  7.0 5.4 %collective-permute-start.3 = (bf16[32,8,256]{2,1,0:T(8,128)(2,1)S(1)}, bf16[32,8,256]{2,1,0:T(8,128)(2,1)S(1)}, u32[]{:S(2)}, u32[]{:S(2)}) collective-permute-start(bf16[32,8,256]{2,1,0:T(8,128)(2,1)S(1)} %pad_maximum_fusion.3), channel_id=1, source_target_pairs={{0,15},{1,0},{2,1},{3,2},{4,3},{5,4},{6,5},{7,6},{8,7},{9,8},{10,9... | collective-permute-start | bytes 393224 | tf_op jit(solution)/shard_map/ppermute | solution.py:481
  12.4 0.0 collective-permute-done.1.xhi
  12.4 0.1 collective-permute-start.4
  12.5 5.3 %collective-permute-start.5 = (bf16[24,8,256]{2,1,0:T(8,128)(2,1)S(1)}, bf16[24,8,256]{2,1,0:T(8,128)(2,1)S(1)}, u32[]{:S(2)}, u32[]{:S(2)}) collective-permute-start(bf16[24,8,256]{2,1,0:T(8,128)(2,1)S(1)} %pad_maximum_fusion.5), channel_id=1, source_target_pairs={{0,15},{1,0},{2,1},{3,2},{4,3},{5,4},{6,5},{7,6},{8,7},{9,8},{10,9... | collective-permute-start | bytes 294920 | tf_op jit(solution)/shard_map/ppermute | solution.py:483
  17.9 2.4 %bands.1 = (bf16[2304,256]{1,0:T(8,128)(2,1)S(1)}, bf16[1024,256]{1,0:T(8,128)(2,1)S(1)}, bf16[2304,256]{1,0:T(8,128)(2,1)S(1)}, bf16[1024,256]{1,0:T(8,128)(2,1)S(1)}, bf16[2304,256]{1,0:T(8,128)(2,1)S(1)}) custom-call(bf16[864,32]{1,0:T(8,128)(2,1)S(1)} %bitcast.18, bf16[4,64,64]{2,1,0:T(8,128)(2,1)S(1)} %bitcast.20, bf16[1728,64]{1,0:T(8,128)(2,1)S(1)} %bitcast.17, ...), custom_call_target="tpu_custom_call" | custom-call | flops 2000000000 | bytes 8000000 | tf_op jit(solution)/shard_map/bands/pallas_call | solution.py:88
  20.3 0.0 collective-permute-done.2.ylo
  20.3 0.0 collective-permute-done.3.yhi
  20.3 15.3 %network.1 = (bf16[1792,128]{1,0:T(8,128)(2,1)S(1)}, bf16[18,32,768]{2,1,0:T(8,128)(2,1)S(1)}, bf16[18,32,768]{2,1,0:T(8,128)(2,1)S(1)}) custom-call(bf16[16,32,256]{2,1,0:T(8,128)(2,1)S(1)} %copy-done, bf16[16,32,256]{2,1,0:T(8,128)(2,1)S(1)} %copy-done.1, bf16[12,32,256]{2,1,0:T(8,128)(2,1)S(1)} %collective-permute-done.xlo, ...), custom_call_target="tpu_custom_call" | custom-call | flops 10000000000 | bytes 10000000 | tf_op jit(solution)/shard_map/network/pallas_call | solution.py:411
  35.6 0.9 copy-done.9
  36.6 22.4 %all_to_all.15 = bf16[32,56,128]{2,1,0:T(8,128)(2,1)S(1)} all-to-all(bf16[32,56,128]{2,1,0:T(8,128)(2,1)S(1)} %bitcast.16), channel_id=1, replica_groups={{0,1,16,17,32,33,48,49,64,65,80,81,96,97,112,113,128,129,144,145,160,16..., dimensions={0} | all-to-all | bytes 917504 | tf_op jit(solution)/shard_map/all_to_all | solution.py:505
  59.0 0.1 convert_reduce_fusion
  59.1 12.2 %all_to_all.16 = f32[8,56,128]{2,1,0:T(8,128)S(1)} all-to-all(f32[8,56,128]{2,1,0:T(8,128)S(1)} %broadcast_in_dim.6), channel_id=1, replica_groups={{0,2,4,6,8,10,12,14},{1,3,5,7,9,11,13,15},{16,18,20,22,24,26,28,30},{17..., dimensions={0} | all-to-all | bytes 458752 | tf_op jit(solution)/shard_map/all_to_all | solution.py:508
  71.3 0.9 broadcast_in_dim.7
  72.1 7.2 %all-to-all-start.2 = ((bf16[32,56,128]{2,1,0:T(8,128)(2,1)}), bf16[32,56,128]{2,1,0:T(8,128)(2,1)S(1)}, u32[]{:S(2)}, u32[]{:S(2)}) async-start(bf16[32,56,128]{2,1,0:T(8,128)(2,1)} %broadcast_in_dim.7), calls=%async_computation.2 | async-start | bytes 917504 | tf_op jit(solution)/shard_map/all_to_all | solution.py:511
  79.3 0.0 copy-start.8
  79.3 1.2 %copy-done.8 = bf16[18,32,768]{2,1,0:T(8,128)(2,1)S(1)} copy-done((bf16[18,32,768]{2,1,0:T(8,128)(2,1)S(1)}, bf16[18,32,768]{2,1,0:T(8,128)(2,1)}, u32[]{:S(2)}) %copy-start.8) | copy-done | bytes 884760
  80.5 1.2 %copy-done.10 = bf16[18,32,768]{2,1,0:T(8,128)(2,1)S(1)} copy-done((bf16[18,32,768]{2,1,0:T(8,128)(2,1)S(1)}, bf16[18,32,768]{2,1,0:T(8,128)(2,1)}, u32[]{:S(2)}) %copy-start.10) | copy-done | bytes 884760
  81.6 2.2 %finish.1 = (bf16[16,32,256]{2,1,0:T(8,128)(2,1)}, bf16[16,32,256]{2,1,0:T(8,128)(2,1)}) custom-call(bf16[16,32,256]{2,1,0:T(8,128)(2,1)S(1)} %copy-done, bf16[16,32,256]{2,1,0:T(8,128)(2,1)S(1)} %copy-done.1, bf16[18,32,768]{2,1,0:T(8,128)(2,1)S(1)} %copy-done.8, bf16[18,32,768]{2,1,0:T(8,128)(2,1)S(1)} %copy-done.10, ...), custom_call_target="tpu_custom_call" | custom-call | flops 3000000000 | bytes 10000000 | tf_op jit(solution)/shard_map/finish/pallas_call | solution.py:397
  83.8 5.7 %all-to-all-done.2 = bf16[32,56,128]{2,1,0:T(8,128)(2,1)S(1)} async-done(((bf16[32,56,128]{2,1,0:T(8,128)(2,1)}), bf16[32,56,128]{2,1,0:T(8,128)(2,1)S(1)}, u32[]{:S(2)}, u32[]{:S(2)}) %all-to-all-start.2) | async-done | bytes 458784 | tf_op jit(solution)/shard_map/all_to_all | solution.py:511
  89.5 0.8 copy-done.11
  90.3 2.5 %unpack.1 = (f32[27,32,32]{2,1,0:T(8,128)}, f32[4,64,64]{2,1,0:T(8,128)}, f32[27,64,64]{2,1,0:T(8,128)}, f32[4,64,64]{2,1,0:T(8,128)}, f32[27,32,32]{2,1,0:T(8,128)}) custom-call(bf16[1792,128]{1,0:T(8,128)(2,1)} %bitcast.22), custom_call_target="tpu_custom_call" | custom-call | tf_op jit(solution)/shard_map/unpack/pallas_call | solution.py:457
  (28 shorter events, 0.2 us)
Async XLA Ops:
  0.6 5.5 %copy-start.1 = (bf16[16,32,256]{2,1,0:T(8,128)(2,1)S(1)}, bf16[16,32,256]{2,1,0:T(8,128)(2,1)}, u32[]{:S(2)}) copy-start(bf16[16,32,256]{2,1,0:T(8,128)(2,1)} %cc.3) | copy-start | bytes 786436
  0.6 5.5 %copy-start = (bf16[16,32,256]{2,1,0:T(8,128)(2,1)S(1)}, bf16[16,32,256]{2,1,0:T(8,128)(2,1)}, u32[]{:S(2)}) copy-start(bf16[16,32,256]{2,1,0:T(8,128)(2,1)} %fc.3) | copy-start | bytes 786436
  2.7 15.2 %copy-start.2 = (bf16[3,3,3,64,64]{4,3,2,1,0:T(8,128)(2,1)S(1)}, bf16[3,3,3,64,64]{4,3,2,1,0:T(8,128)(2,1)}, u32[]{:S(2)}) copy-start(bf16[3,3,3,64,64]{4,3,2,1,0:T(8,128)(2,1)} %param.10) | copy-start | bytes 663556
  2.7 15.2 %copy-start.3 = (bf16[3,3,3,32,32]{4,3,2,1,0:T(8,128)(2,1)S(1)}, bf16[3,3,3,32,32]{4,3,2,1,0:T(8,128)(2,1)}, u32[]{:S(2)}) copy-start(bf16[3,3,3,32,32]{4,3,2,1,0:T(8,128)(2,1)} %param.8) | copy-start | bytes 165892
  2.7 15.2 %copy-start.4 = (bf16[3,3,3,32,32]{4,3,2,1,0:T(8,128)(2,1)S(1)}, bf16[3,3,3,32,32]{4,3,2,1,0:T(8,128)(2,1)}, u32[]{:S(2)}) copy-start(bf16[3,3,3,32,32]{4,3,2,1,0:T(8,128)(2,1)} %param.12) | copy-start | bytes 165892
  2.7 15.2 %copy-start.5 = (bf16[2,2,2,32,64]{4,3,2,1,0:T(8,128)(2,1)S(1)}, bf16[2,2,2,32,64]{4,3,2,1,0:T(8,128)(2,1)}, u32[]{:S(2)}) copy-start(bf16[2,2,2,32,64]{4,3,2,1,0:T(8,128)(2,1)} %param.9) | copy-start | bytes 98308
  2.7 15.2 %copy-start.6 = (bf16[2,2,2,64,32]{3,4,2,1,0:T(8,128)(2,1)S(1)}, bf16[2,2,2,64,32]{3,4,2,1,0:T(8,128)(2,1)}, u32[]{:S(2)}) copy-start(bf16[2,2,2,64,32]{3,4,2,1,0:T(8,128)(2,1)} %param.11) | copy-start | bytes 98308
  2.7 9.6 %collective-permute-start = (bf16[12,32,256]{2,1,0:T(8,128)(2,1)S(1)}, bf16[12,32,256]{2,1,0:T(8,128)(2,1)S(1)}, u32[]{:S(2)}, u32[]{:S(2)}) collective-permute-start(bf16[12,32,256]{2,1,0:T(8,128)(2,1)S(1)} %pad_maximum_fusion), channel_id=1, source_target_pairs={{0,16},{16,32},{32,48},{48,64},{64,80},{80,96},{96,112},{112,128},... | collective-permute-start | bytes 589832 | tf_op jit(solution)/shard_map/ppermute | solution.py:478
  5.5 6.9 %collective-permute-start.1 = (bf16[12,32,256]{2,1,0:T(8,128)(2,1)S(1)}, bf16[12,32,256]{2,1,0:T(8,128)(2,1)S(1)}, u32[]{:S(2)}, u32[]{:S(2)}) collective-permute-start(bf16[12,32,256]{2,1,0:T(8,128)(2,1)S(1)} %pad_maximum_fusion.1), channel_id=1, source_target_pairs={{0,240},{16,0},{32,16},{48,32},{64,48},{80,64},{96,80},{112,96},{1... | collective-permute-start | bytes 589832 | tf_op jit(solution)/shard_map/ppermute | solution.py:479
  6.2 14.1 %collective-permute-start.2 = (bf16[32,8,256]{2,1,0:T(8,128)(2,1)S(1)}, bf16[32,8,256]{2,1,0:T(8,128)(2,1)S(1)}, u32[]{:S(2)}, u32[]{:S(2)}) collective-permute-start(bf16[32,8,256]{2,1,0:T(8,128)(2,1)S(1)} %pad_maximum_fusion.2), channel_id=1, source_target_pairs={{0,1},{1,2},{2,3},{3,4},{4,5},{5,6},{6,7},{7,8},{8,9},{9,10},{10,1... | collective-permute-start | bytes 393224 | tf_op jit(solution)/shard_map/ppermute | solution.py:480
  7.0 13.3 %collective-permute-start.3 = (bf16[32,8,256]{2,1,0:T(8,128)(2,1)S(1)}, bf16[32,8,256]{2,1,0:T(8,128)(2,1)S(1)}, u32[]{:S(2)}, u32[]{:S(2)}) collective-permute-start(bf16[32,8,256]{2,1,0:T(8,128)(2,1)S(1)} %pad_maximum_fusion.3), channel_id=1, source_target_pairs={{0,15},{1,0},{2,1},{3,2},{4,3},{5,4},{6,5},{7,6},{8,7},{9,8},{10,9... | collective-permute-start | bytes 393224 | tf_op jit(solution)/shard_map/ppermute | solution.py:481
  12.4 7.9 %collective-permute-start.4 = (bf16[24,8,256]{2,1,0:T(8,128)(2,1)S(1)}, bf16[24,8,256]{2,1,0:T(8,128)(2,1)S(1)}, u32[]{:S(2)}, u32[]{:S(2)}) collective-permute-start(bf16[24,8,256]{2,1,0:T(8,128)(2,1)S(1)} %pad_maximum_fusion.4), channel_id=1, source_target_pairs={{0,1},{1,2},{2,3},{3,4},{4,5},{5,6},{6,7},{7,8},{8,9},{9,10},{10,1... | collective-permute-start | bytes 294920 | tf_op jit(solution)/shard_map/ppermute | solution.py:482
  12.5 7.8 %collective-permute-start.5 = (bf16[24,8,256]{2,1,0:T(8,128)(2,1)S(1)}, bf16[24,8,256]{2,1,0:T(8,128)(2,1)S(1)}, u32[]{:S(2)}, u32[]{:S(2)}) collective-permute-start(bf16[24,8,256]{2,1,0:T(8,128)(2,1)S(1)} %pad_maximum_fusion.5), channel_id=1, source_target_pairs={{0,15},{1,0},{2,1},{3,2},{4,3},{5,4},{6,5},{7,6},{8,7},{9,8},{10,9... | collective-permute-start | bytes 294920 | tf_op jit(solution)/shard_map/ppermute | solution.py:483
  35.6 0.9 copy-start.9
  36.6 22.4 %copy-start.7 = (bf16[18,32,768]{2,1,0:T(8,128)(2,1)}, bf16[18,32,768]{2,1,0:T(8,128)(2,1)S(1)}, u32[]{:S(2)}) copy-start(bf16[18,32,768]{2,1,0:T(8,128)(2,1)S(1)} %get-tuple-element.27.v3s) | copy-start | bytes 2654212
  72.1 17.4 %all-to-all-start.2 = ((bf16[32,56,128]{2,1,0:T(8,128)(2,1)}), bf16[32,56,128]{2,1,0:T(8,128)(2,1)S(1)}, u32[]{:S(2)}, u32[]{:S(2)}) async-start(bf16[32,56,128]{2,1,0:T(8,128)(2,1)} %broadcast_in_dim.7), calls=%async_computation.2 | async-start | bytes 917504 | tf_op jit(solution)/shard_map/all_to_all | solution.py:511
  79.3 1.2 %copy-start.8 = (bf16[18,32,768]{2,1,0:T(8,128)(2,1)S(1)}, bf16[18,32,768]{2,1,0:T(8,128)(2,1)}, u32[]{:S(2)}) copy-start(bf16[18,32,768]{2,1,0:T(8,128)(2,1)} %copy-done.7) | copy-start | bytes 2654212
  80.5 1.2 %copy-start.10 = (bf16[18,32,768]{2,1,0:T(8,128)(2,1)S(1)}, bf16[18,32,768]{2,1,0:T(8,128)(2,1)}, u32[]{:S(2)}) copy-start(bf16[18,32,768]{2,1,0:T(8,128)(2,1)} %copy-done.9) | copy-start | bytes 2654212
  89.5 0.8 copy-start.11

commit v3 on v2

--- a/solution.py
+++ b/solution.py
@@ -102,13 +102,25 @@
 
 
 def get_row(src, row):
+    if len(src.shape) == 3 and src.shape[2] == 128:
+        at = pl.ds(pl.multiple_of(row * EY, 8), EY)
+        return jnp.concatenate([src[0, at, :], src[1, at, :]], axis=1)
     if len(src.shape) == 3:
         return src[row]
     return jnp.concatenate([src[0, row], src[1, row]], axis=1)
 
 
+def clear_ends(src, half, row):
+    for at in (0, 40):
+        src[half, pl.ds(pl.multiple_of(row * EY + at, 8), 8), :] = jnp.zeros((8, 128), F32)
+
+
 def get_rows(src, rows):
     return jnp.concatenate([src[0, rows], src[1, rows]], axis=2)
+
+
+def put_row(dst, row, value):
+    dst[row] = value.astype(BF)
 
 
 def put_rows(dst, rows, value):
@@ -128,7 +140,7 @@
 
 
 def taps_to_lanes(src, row, out, at, lo, size):
-    v = get_row(src, row)
+    v = get_row(src, row).astype(F32)
     n = v.shape[0]
     out[at, :, 0:W] = pltpu.roll(v, 1, 0)[lo : lo + size].astype(BF)
     out[at, :, W : 2 * W] = v[lo : lo + size].astype(BF)
@@ -193,32 +205,43 @@
 
 def main_kernel(
     fc, cc, xlo, xhi, ylo, yhi, clo, chi, bd, pm, bm, um, bu,
-    terms, v3s, v3d,
+    terms, skip_rows, down_rows,
     fe, ce, hid, ds_down, skp, ds_up, dup, ddn,
-    v3f, v3c, v3fl,
+    v3f, v3c, v3fl, v3s,
     parts, co, mid, ds_pool, ds_mid, dmid, v3m, v3dm, v3ml, local,
     hi, lo, him, lom, dsc,
 ):
-    def gather(dst, count, center, off_x, off_y):
-        def own(i):
-            dst[8 + i, 0:8] = ylo[off_y + i].astype(F32)
-            dst[8 + i, 8:40] = center[i].astype(F32)
-            dst[8 + i, 40:48] = yhi[off_y + i].astype(F32)
-
-        loop(BX, own)
+    def gather(dst, count, center, off):
+        def put(row, value):
+            at = pl.ds(pl.multiple_of(row * EY + 8, 8), BY)
+            dst[0, at, :] = value[:, 0:128]
+            dst[1, at, :] = value[:, 128:256]
+
+        loop(BX, lambda i: put(8 + i, center[i].astype(F32)))
 
         def edge(i):
-            dst[8 - count + i, 0:8] = clo[off_x + i].astype(F32)
-            dst[8 - count + i, 8:40] = xlo[off_x + i].astype(F32)
-            dst[8 - count + i, 40:48] = chi[off_x + i].astype(F32)
-            dst[24 + i, 0:8] = clo[HF + HC + off_x + i].astype(F32)
-            dst[24 + i, 8:40] = xhi[off_x + i].astype(F32)
-            dst[24 + i, 40:48] = chi[HF + HC + off_x + i].astype(F32)
+            put(8 - count + i, xlo[off + i].astype(F32))
+            put(24 + i, xhi[off + i].astype(F32))
 
         loop(count, edge)
-
-    gather(fe, HF, fc, 0, 0)
-    gather(ce, HC, cc, HF, BX)
+        for c in range(count):
+            for side, y, other in ((ylo, 8 - count + c, 0), (yhi, 40 + c, HF + HC)):
+                column = jnp.concatenate(
+                    [
+                        clo[other + off + c].astype(F32),
+                        side[off + c].astype(F32),
+                        chi[other + off + c].astype(F32),
+                    ],
+                    axis=0,
+                )
+                for h in range(2):
+                    dst[h, pl.ds(y, EX, stride=EY), :] = column[:, h * 128 : h * 128 + 128]
+
+    for ext in (fe, ce):
+        for h in range(2):
+            loop(EX, lambda x: clear_ends(ext, h, x))
+    gather(fe, HF, fc, 0)
+    gather(ce, HC, cc, HF)
 
     loop(30, lambda i: taps_to_lanes(fe, 1 + i, v3f, i, 0, EY))
     loop(18, lambda i: taps_to_lanes(fe, 7 + i, v3fl, i, 8, BY))
@@ -282,6 +305,7 @@
     loop(2, up)
 
     loop(18, lambda i: taps_to_lanes(skp, 7 + i, v3s, i, 8, BY))
+    loop(18, lambda i: put_row(skip_rows, i, get_row(skp, 7 + i)))
 
     loop(26, lambda i: taps_to_lanes(ce, 3 + i, v3c, i, 0, EY))
 
@@ -369,7 +393,7 @@
                 slope = get_every_second(ds_down, row, j, EY // 2)
                 put_every_second(ddn, row, j, rounded(d_hidden * slope))
 
-    loop(18, lambda i: taps_to_lanes(ddn, 7 + i, v3d, i, 8, BY))
+    loop(18, lambda i: put_row(down_rows, i, get_row(ddn, 7 + i)))
 
     down_t = get_rows(ddn, slice(8, 24))[:, 8:40].reshape(BX * BY, W).T.astype(BF)
     conv_weight_terms(down_t, v3fl, BX, 32, hi, lo, dsc)
@@ -385,37 +409,41 @@
         terms[TILES * 32 :, :] = jnp.zeros((rest, 128), BF)
 
 
-def finish_kernel(fc, cc, v3s, v3d, bd, bu, out, gf):
-    total = conv_rows(v3s, 0, BX, bu).reshape(BX, BY, W)
+def finish_kernel(fc, cc, skip_rows, down_rows, bd, bu, out, gf, v3):
+    loop(18, lambda i: taps_to_lanes(skip_rows, i, v3, i, 8, BY))
+    total = conv_rows(v3, 0, BX, bu).reshape(BX, BY, W)
     out[...] = (fc[...].astype(F32) + total).astype(BF)
-    total = conv_t_rows(v3d, 0, BX, bd).reshape(BX, BY, W)
+    loop(18, lambda i: taps_to_lanes(down_rows, i, v3, i, 8, BY))
+    total = conv_t_rows(v3, 0, BX, bd).reshape(BX, BY, W)
     gf[...] = (cc[...].astype(F32) + total).astype(BF)
 
 
-def finish_call(fields, cot, v3s, v3d, bands):
+def finish_call(fields, cot, skip_rows, down_rows, bands):
     block = jax.ShapeDtypeStruct((BX, BY, W), BF)
     return pl.pallas_call(
         finish_kernel,
         out_shape=(block, block),
-        compiler_params=pltpu.CompilerParams(vmem_limit_bytes=20 * 1024 * 1024),
+        scratch_shapes=[pltpu.VMEM((18, BY, 3 * W), BF)],
+        compiler_params=pltpu.CompilerParams(vmem_limit_bytes=16 * 1024 * 1024),
         cost_estimate=pl.CostEstimate(flops=3 * 10**9, bytes_accessed=10**7, transcendentals=0),
         name="finish",
-    )(fields, cot, v3s, v3d, bands[0], bands[4])
+    )(fields, cot, skip_rows, down_rows, bands[0], bands[4])
 
 
 def main_call(fields, cot, halos, bands, term_rows):
-    taps = jax.ShapeDtypeStruct((18, BY, 3 * W), BF)
-    fine = pltpu.VMEM((EX, EY, W), F32)
+    some = jax.ShapeDtypeStruct((18, EY, W), BF)
+    flat = pltpu.VMEM((2, EX * EY, 128), F32)
     split = pltpu.VMEM((2, EX, EY, 128), F32)
     coarse = pltpu.VMEM((CX, CY, W), F32)
     return pl.pallas_call(
         main_kernel,
-        out_shape=(jax.ShapeDtypeStruct((term_rows, 128), BF), taps, taps),
-        scratch_shapes=[fine] * 2
+        out_shape=(jax.ShapeDtypeStruct((term_rows, 128), BF), some, some),
+        scratch_shapes=[flat] * 2
         + [split] * 6
         + [
             pltpu.VMEM((30, EY, 3 * W), BF),
             pltpu.VMEM((26, EY, 3 * W), BF),
+            pltpu.VMEM((18, BY, 3 * W), BF),
             pltpu.VMEM((18, BY, 3 * W), BF),
             pltpu.VMEM((4, CX, CY, W), BF),
             coarse,
@@ -439,27 +467,44 @@
     )(fields, cot, *halos, *bands)
 
 
-def unpack_kernel(terms, down, pool, mid, unpool, up):
-    for u in range(27):
-        row, lane = (u // 4) * 32, (u % 4) * 32
-        down[u] = terms[row : row + 32, lane : lane + 32].astype(F32)
-        up[u] = terms[224 + row : 224 + row + 32, lane : lane + 32].astype(F32)
-        row, lane = 14 * 32 + (u // 2) * 64, (u % 2) * 64
-        mid[u] = terms[row : row + 64, lane : lane + 64].astype(F32)
-    for q in range(4):
-        row, lane = 42 * 32 + (q // 2) * 64, (q % 2) * 64
-        pool[q] = terms[row : row + 64, lane : lane + 64].astype(F32)
-        unpool[q] = terms[128 + row : 128 + row + 64, lane : lane + 64].astype(F32)
+def unpack_kernel(
+    terms, down, pool, mid, unpool, up, down_v, pool_v, mid_v, unpool_v, up_v, sems
+):
+    def send(k, src, dst):
+        copy = pltpu.make_async_copy(src, dst, sems.at[k])
+        copy.start()
+        return copy
+
+    copies = []
+    for part in range(3):
+        for u in range(9 * part, 9 * part + 9):
+            row, lane = 14 * 32 + (u // 2) * 64, (u % 2) * 64
+            mid_v[u] = terms[row : row + 64, lane : lane + 64].astype(F32)
+        at = pl.ds(9 * part, 9)
+        copies.append(send(part, mid_v.at[at], mid.at[at]))
+    for first, src, dst in ((0, down_v, down), (224, up_v, up)):
+        for u in range(27):
+            row, lane = first + (u // 4) * 32, (u % 4) * 32
+            src[u] = terms[row : row + 32, lane : lane + 32].astype(F32)
+        copies.append(send(3 if first == 0 else 4, src, dst))
+    for first, src, dst in ((42 * 32, pool_v, pool), (46 * 32, unpool_v, unpool)):
+        for q in range(4):
+            row, lane = first + (q // 2) * 64, (q % 2) * 64
+            src[q] = terms[row : row + 64, lane : lane + 64].astype(F32)
+        copies.append(send(5 if src is pool_v else 6, src, dst))
+    for copy in copies:
+        copy.wait()
 
 
 def unpack(terms):
-    shape = lambda *s: jax.ShapeDtypeStruct(s, F32)
+    shapes = ((27, 32, 32), (4, 64, 64), (27, 64, 64), (4, 64, 64), (27, 32, 32))
     return pl.pallas_call(
         unpack_kernel,
-        out_shape=(
-            shape(27, 32, 32), shape(4, 64, 64), shape(27, 64, 64), shape(4, 64, 64),
-            shape(27, 32, 32),
-        ),
+        out_shape=tuple(jax.ShapeDtypeStruct(s, F32) for s in shapes),
+        in_specs=[pl.BlockSpec(memory_space=pltpu.VMEM)],
+        out_specs=tuple(pl.BlockSpec(memory_space=pl.ANY) for _ in shapes),
+        scratch_shapes=[pltpu.VMEM(s, F32) for s in shapes] + [pltpu.SemaphoreType.DMA((7,))],
+        compiler_params=pltpu.CompilerParams(vmem_limit_bytes=8 * 1024 * 1024),
         name="unpack",
     )(terms)
 
@@ -469,18 +514,46 @@
     return [(i, (i + step) % n) for i in range(n)]
 
 
+def pack_kernel(fc, cc, first_x, last_x, first_y, last_y, wide):
+    first_x[0:HF] = fc[0:HF]
+    first_x[HF : HF + HC] = cc[0:HC]
+    last_x[0:HF] = fc[BX - HF : BX]
+    last_x[HF : HF + HC] = cc[BX - HC : BX]
+    for src, count, at in ((fc, HF, 0), (cc, HC, HF)):
+        for h in range(2):
+            lanes = slice(h * 128, h * 128 + 128)
+            wide[h] = src[:, :, lanes].reshape(BX * BY, 128).astype(F32)
+        for c in range(count):
+            for h in range(2):
+                lanes = slice(h * 128, h * 128 + 128)
+                column = wide[h, pl.ds(c, BX, stride=BY), :]
+                first_y[at + c, :, lanes] = column.astype(BF)
+                column = wide[h, pl.ds(BY - count + c, BX, stride=BY), :]
+                last_y[at + c, :, lanes] = column.astype(BF)
+
+
+def pack(fields, cot):
+    rows = jax.ShapeDtypeStruct((HF + HC, BY, W), BF)
+    columns = jax.ShapeDtypeStruct((HF + HC, BX, W), BF)
+    return pl.pallas_call(
+        pack_kernel,
+        out_shape=(rows, rows, columns, columns),
+        scratch_shapes=[pltpu.VMEM((2, BX * BY, 128), F32)],
+        compiler_params=pltpu.CompilerParams(vmem_limit_bytes=8 * 1024 * 1024),
+        name="pack",
+    )(fields, cot)
+
+
 def exchange(fields, cot):
-    def columns(a, b, lo):
-        return jnp.concatenate([a[:, lo : lo + 8], b[:, lo : lo + 8]], axis=0)
-
-    last = jnp.concatenate([fields[BX - HF :], cot[BX - HC :]], axis=0)
-    first = jnp.concatenate([fields[:HF], cot[:HC]], axis=0)
-    xlo = lax.ppermute(last, "gx", ring("gx", 1))
-    xhi = lax.ppermute(first, "gx", ring("gx", -1))
-    ylo = lax.ppermute(columns(fields, cot, BY - 8), "gy", ring("gy", 1))
-    yhi = lax.ppermute(columns(fields, cot, 0), "gy", ring("gy", -1))
-    clo = lax.ppermute(columns(xlo, xhi, BY - 8), "gy", ring("gy", 1))
-    chi = lax.ppermute(columns(xlo, xhi, 0), "gy", ring("gy", -1))
+    first_x, last_x, first_y, last_y = pack(fields, cot)
+    ylo = lax.ppermute(last_y, "gy", ring("gy", 1))
+    yhi = lax.ppermute(first_y, "gy", ring("gy", -1))
+    xlo = lax.ppermute(last_x, "gx", ring("gx", 1))
+    xhi = lax.ppermute(first_x, "gx", ring("gx", -1))
+    last_c = jnp.concatenate([ylo[:, BX - 8 :], yhi[:, BX - 8 :]], axis=0)
+    first_c = jnp.concatenate([ylo[:, :8], yhi[:, :8]], axis=0)
+    clo = lax.ppermute(last_c, "gx", ring("gx", 1))
+    chi = lax.ppermute(first_c, "gx", ring("gx", -1))
     return (xlo, xhi, ylo, yhi, clo, chi)
 
 
@@ -498,16 +571,17 @@
     rows = -(-TILES * 32 // (8 * n1)) * 8
     bands = build_bands(w_down, w_pool, w_mid, w_unpool, w_up)
     halos = exchange(fields, cotangent)
-    terms, v3s, v3d = main_call(fields, cotangent, halos, bands, n1 * rows)
+    terms, skip_rows, down_rows = main_call(fields, cotangent, halos, bands, n1 * rows)
     swap = functools.partial(
         lax.all_to_all, axis_name=("gx", "gy"), split_axis=0, concat_axis=0, tiled=True
     )
     part = swap(terms.reshape(n1, rows, 128), axis_index_groups=near)
-    output, grad_fields = finish_call(fields, cotangent, v3s, v3d, bands)
-    part = jnp.sum(part.astype(F32), axis=0)
-    part = swap(jnp.broadcast_to(part, (n2, rows, 128)), axis_index_groups=far)
+    output, grad_fields = finish_call(fields, cotangent, skip_rows, down_rows, bands)
     cells = fields.shape[0] * fields.shape[1] * 8 * nx * ny
-    part = (jnp.sum(part, axis=0) * (1.0 / math.sqrt(cells))).astype(BF)
+    root = 1.0 / math.sqrt(math.sqrt(cells))
+    part = (jnp.sum(part.astype(F32), axis=0) * root).astype(BF)
+    part = swap(jnp.broadcast_to(part, (n2, rows, 128)), axis_index_groups=far).astype(F32)
+    part = (jnp.sum(part, axis=0) * root).astype(BF)
     whole = swap(jnp.broadcast_to(part, (n1, rows, 128)), axis_index_groups=near)
     down, pool, mid, unpool, up = unpack(whole.reshape(n1 * rows, 128))
     return (

time: 93.3 us -> 90.7 us (0.972)
  local copies, waits for them, and re-layouts: 6.93 us -> 4.82 us
  Pallas kernels: 22.4 us -> 24.2 us
  starting transfers between devices: 22.1 us -> 20.3 us
    slice x5 -> x2, local copies, waits for them, and re-layouts: 2 us -> 0.02 us  [exchange(): first_c = jnp.concatenate([ylo[:, :8], yhi[:, :8]], axis=0)]
    all_to_all x1, waiting for transfers between devices: 5.75 us -> 4.45 us  [per_device(): swap(jnp.broadcast_to(part, (n1, rows, 128)), axis_index_groups=near)]
    ppermute x6, starting transfers between devices: 15 us -> 13.9 us  [the longest x1 5.38 us: exchange(): yhi = lax.ppermute(first_y, 'gy', ring('gy', -1))]
    pallas_call x1, Pallas kernels: 15.3 us -> 16.3 us  [main_call(): pl.pallas_call(main_kernel, out_shape=(jax.ShapeDtypeStruct((term_rows, 1...]
    pallas_call x2 -> x3, Pallas kernels: 4.68 us -> 5.59 us  [the longest x1 3.87 us: finish_call(): pl.pallas_call(finish_kernel, out_shape=(block, block), scratch_shapes=[p...]
    unnamed x24 -> x26, local copies, waits for them, and re-layouts: 4.06 us -> 3.96 us
  transfers between devices with their start and end apart: 7 -> 7, of which waited for: 1 -> 3; matrix products, arithmetic and copies ran while one was open for 0% -> 0% of each run, Pallas kernels for 5% -> 7%
where the time goes in v3:
time: 90.7 us; the launch traced here: 90.3 us
  blocking collectives  35 us (39%)
  Pallas kernels  24.2 us (27%)
  starting transfers between devices  20.3 us (22%)
  waiting for transfers between devices  4.84 us (5%)
  local copies, waits for them, and re-layouts  4.82 us (5%)
  between operations  0.99 us (1%)
    all_to_all x1, blocking collectives, per_device(): part = swap(terms.reshape(n1, rows, 128), axis_index_groups=near)  21.9 us
    pallas_call x1, Pallas kernels, main_call(): pl.pallas_call(main_kernel, out_shape=(jax.ShapeDtypeStruct((term_rows, 1...  16.3 us
    all_to_all x1, blocking collectives, per_device(): swap(jnp.broadcast_to(part, (n2, rows, 128)), axis_index_groups=far)  13.1 us
    all_to_all x1, starting transfers between devices, per_device(): swap(jnp.broadcast_to(part, (n1, rows, 128)), axis_index_groups=near)  6.4 us
    ppermute x1, starting transfers between devices, exchange(): yhi = lax.ppermute(first_y, 'gy', ring('gy', -1))  5.38 us
    all_to_all x1, waiting for transfers between devices, per_device(): swap(jnp.broadcast_to(part, (n1, rows, 128)), axis_index_groups=near)  4.45 us
    unnamed x26, local copies, waits for them, and re-layouts  3.96 us
    pallas_call x1, Pallas kernels, finish_call(): pl.pallas_call(finish_kernel, out_shape=(block, block), scratch_shapes=[p...  3.87 us
  transfers between devices with their start and end apart: 7, of which 3 were waited for; matrix products, arithmetic and copies ran while one was open for 0% of the time, Pallas kernels for 7%

profile of v3, /device:TPU:1, one launch (start us, length us, event | category | flops | bytes accessed | tf_op | source)
XLA Modules:
  0.0 90.3 jit_solution(7153076890661128159)
XLA Ops:
  0.6 0.0 copy-start
  0.6 0.9 %copy-done = bf16[16,32,256]{2,1,0:T(8,128)(2,1)S(1)} copy-done((bf16[16,32,256]{2,1,0:T(8,128)(2,1)S(1)}, bf16[16,32,256]{2,1,0:T(8,128)(2,1)}, u32[]{:S(2)}) %copy-start) | copy-done | bytes 262168
  1.6 0.9 %copy-done.2 = bf16[16,32,256]{2,1,0:T(8,128)(2,1)S(1)} copy-done((bf16[16,32,256]{2,1,0:T(8,128)(2,1)S(1)}, bf16[16,32,256]{2,1,0:T(8,128)(2,1)}, u32[]{:S(2)}) %copy-start.2) | copy-done | bytes 262168
  2.6 0.3 pack.1
  2.9 2.1 %collective-permute-start.2 = (bf16[12,16,256]{2,1,0:T(8,128)(2,1)S(1)}, bf16[12,16,256]{2,1,0:T(8,128)(2,1)S(1)}, u32[]{:S(2)}, u32[]{:S(2)}) collective-permute-start(bf16[12,16,256]{2,1,0:T(8,128)(2,1)S(1)} %get-tuple-element.28), channel_id=1, source_target_pairs={{0,1},{1,2},{2,3},{3,4},{4,5},{5,6},{6,7},{7,8},{8,9},{9,10},{10,1... | collective-permute-start | bytes 294920 | tf_op jit(solution)/shard_map/ppermute | solution.py:549
  5.0 5.4 %collective-permute-start.3 = (bf16[12,16,256]{2,1,0:T(8,128)(2,1)S(1)}, bf16[12,16,256]{2,1,0:T(8,128)(2,1)S(1)}, u32[]{:S(2)}, u32[]{:S(2)}) collective-permute-start(bf16[12,16,256]{2,1,0:T(8,128)(2,1)S(1)} %get-tuple-element.29), channel_id=1, source_target_pairs={{0,15},{1,0},{2,1},{3,2},{4,3},{5,4},{6,5},{7,6},{8,7},{9,8},{10,9... | collective-permute-start | bytes 294920 | tf_op jit(solution)/shard_map/ppermute | solution.py:550
  10.4 2.1 %collective-permute-start = (bf16[12,32,256]{2,1,0:T(8,128)(2,1)S(1)}, bf16[12,32,256]{2,1,0:T(8,128)(2,1)S(1)}, u32[]{:S(2)}, u32[]{:S(2)}) collective-permute-start(bf16[12,32,256]{2,1,0:T(8,128)(2,1)S(1)} %get-tuple-element.26), channel_id=1, source_target_pairs={{0,16},{16,32},{32,48},{48,64},{64,80},{80,96},{96,112},{112,128},... | collective-permute-start | bytes 589832 | tf_op jit(solution)/shard_map/ppermute | solution.py:551
  12.5 0.0 collective-permute-start.1
  12.5 0.3 collective-permute-done.2.ylo
  12.8 0.0 collective-permute-done.3.yhi
  12.8 2.5 %collective-permute-start.4 = (bf16[24,8,256]{2,1,0:T(8,128)(2,1)S(1)}, bf16[24,8,256]{2,1,0:T(8,128)(2,1)S(1)}, u32[]{:S(2)}, u32[]{:S(2)}) collective-permute-start(bf16[24,8,256]{2,1,0:T(8,128)(2,1)S(1)} %pad_maximum_fusion), channel_id=1, source_target_pairs={{0,16},{16,32},{32,48},{48,64},{64,80},{80,96},{96,112},{112,128},... | collective-permute-start | bytes 294920 | tf_op jit(solution)/shard_map/ppermute | solution.py:555
  15.3 1.8 %collective-permute-start.5 = (bf16[24,8,256]{2,1,0:T(8,128)(2,1)S(1)}, bf16[24,8,256]{2,1,0:T(8,128)(2,1)S(1)}, u32[]{:S(2)}, u32[]{:S(2)}) collective-permute-start(bf16[24,8,256]{2,1,0:T(8,128)(2,1)S(1)} %pad_maximum_fusion.1), channel_id=1, source_target_pairs={{0,240},{16,0},{32,16},{48,32},{64,48},{80,64},{96,80},{112,96},{1... | collective-permute-start | bytes 294920 | tf_op jit(solution)/shard_map/ppermute | solution.py:556
  17.1 0.0 copy-start.1
  17.1 0.0 copy-start.3
  17.1 2.4 %bands.1 = (bf16[2304,256]{1,0:T(8,128)(2,1)S(1)}, bf16[1024,256]{1,0:T(8,128)(2,1)S(1)}, bf16[2304,256]{1,0:T(8,128)(2,1)S(1)}, bf16[1024,256]{1,0:T(8,128)(2,1)S(1)}, bf16[2304,256]{1,0:T(8,128)(2,1)S(1)}) custom-call(bf16[864,32]{1,0:T(8,128)(2,1)S(1)} %bitcast.19, bf16[4,64,64]{2,1,0:T(8,128)(2,1)S(1)} %bitcast.21, bf16[1728,64]{1,0:T(8,128)(2,1)S(1)} %bitcast.18, ...), custom_call_target="tpu_custom_call" | custom-call | flops 2000000000 | bytes 8000000 | tf_op jit(solution)/shard_map/bands/pallas_call | solution.py:88
  19.5 0.0 collective-permute-done.4.clo
  19.6 0.1 collective-permute-done.5.chi
  19.6 0.0 collective-permute-done.xlo
  19.7 16.3 %network.1 = (bf16[1792,128]{1,0:T(8,128)(2,1)S(1)}, bf16[18,48,256]{2,1,0:T(8,128)(2,1)S(1)}, bf16[18,48,256]{2,1,0:T(8,128)(2,1)S(1)}) custom-call(bf16[16,32,256]{2,1,0:T(8,128)(2,1)S(1)} %copy-done.1, bf16[16,32,256]{2,1,0:T(8,128)(2,1)S(1)} %copy-done.3, bf16[12,32,256]{2,1,0:T(8,128)(2,1)S(1)} %collective-permute-done.xlo, ...), custom_call_target="tpu_custom_call" | custom-call | flops 10000000000 | bytes 10000000 | tf_op jit(solution)/shard_map/network/pallas_call | solution.py:438
  35.9 0.0 copy-start.9
  35.9 0.0 copy-start.11
  36.0 21.9 %all_to_all.15 = bf16[32,56,128]{2,1,0:T(8,128)(2,1)S(1)} all-to-all(bf16[32,56,128]{2,1,0:T(8,128)(2,1)S(1)} %bitcast.17), channel_id=1, replica_groups={{0,1,16,17,32,33,48,49,64,65,80,81,96,97,112,113,128,129,144,145,160,16..., dimensions={0} | all-to-all | bytes 917504 | tf_op jit(solution)/shard_map/all_to_all | solution.py:578
  57.9 0.1 convert_reduce_fusion
  58.0 13.1 %all_to_all.16 = bf16[8,56,128]{2,1,0:T(8,128)(2,1)S(1)} all-to-all(bf16[8,56,128]{2,1,0:T(8,128)(2,1)S(1)} %broadcast_in_dim.6), channel_id=1, replica_groups={{0,2,4,6,8,10,12,14},{1,3,5,7,9,11,13,15},{16,18,20,22,24,26,28,30},{17..., dimensions={0} | all-to-all | bytes 229376 | tf_op jit(solution)/shard_map/all_to_all | solution.py:583
  71.1 0.8 broadcast_in_dim.7
  71.9 6.4 %all-to-all-start.2 = ((bf16[32,56,128]{2,1,0:T(8,128)(2,1)}), bf16[32,56,128]{2,1,0:T(8,128)(2,1)S(1)}, u32[]{:S(2)}, u32[]{:S(2)}) async-start(bf16[32,56,128]{2,1,0:T(8,128)(2,1)} %broadcast_in_dim.7), calls=%async_computation.2 | async-start | bytes 917504 | tf_op jit(solution)/shard_map/all_to_all | solution.py:585
  78.4 0.0 copy-start.10
  78.4 1.0 %copy-done.10 = bf16[18,48,256]{2,1,0:T(8,128)(2,1)S(1)} copy-done((bf16[18,48,256]{2,1,0:T(8,128)(2,1)S(1)}, bf16[18,48,256]{2,1,0:T(8,128)(2,1)}, u32[]{:S(2)}) %copy-start.10) | copy-done | bytes 442392
  79.4 1.0 %copy-done.12 = bf16[18,48,256]{2,1,0:T(8,128)(2,1)S(1)} copy-done((bf16[18,48,256]{2,1,0:T(8,128)(2,1)S(1)}, bf16[18,48,256]{2,1,0:T(8,128)(2,1)}, u32[]{:S(2)}) %copy-start.12) | copy-done | bytes 442392
  80.4 3.9 %finish.1 = (bf16[16,32,256]{2,1,0:T(8,128)(2,1)}, bf16[16,32,256]{2,1,0:T(8,128)(2,1)}) custom-call(bf16[16,32,256]{2,1,0:T(8,128)(2,1)S(1)} %copy-done.1, bf16[16,32,256]{2,1,0:T(8,128)(2,1)S(1)} %copy-done.3, bf16[18,48,256]{2,1,0:T(8,128)(2,1)S(1)} %copy-done.10, bf16[18,48,256]{2,1,0:T(8,128)(2,1)S(1)} %copy-done.12, ...), custom_call_target="tpu_custom_call" | custom-call | flops 3000000000 | bytes 10000000 | tf_op jit(solution)/shard_map/finish/pallas_call | solution.py:423
  84.3 4.5 %all-to-all-done.2 = bf16[32,56,128]{2,1,0:T(8,128)(2,1)S(1)} async-done(((bf16[32,56,128]{2,1,0:T(8,128)(2,1)}), bf16[32,56,128]{2,1,0:T(8,128)(2,1)S(1)}, u32[]{:S(2)}, u32[]{:S(2)}) %all-to-all-start.2) | async-done | bytes 458784 | tf_op jit(solution)/shard_map/all_to_all | solution.py:585
  88.7 1.4 %unpack.1 = (f32[27,32,32]{2,1,0:T(8,128)}, f32[4,64,64]{2,1,0:T(8,128)}, f32[27,64,64]{2,1,0:T(8,128)}, f32[4,64,64]{2,1,0:T(8,128)}, f32[27,32,32]{2,1,0:T(8,128)}) custom-call(bf16[1792,128]{1,0:T(8,128)(2,1)S(1)} %bitcast.16), custom_call_target="tpu_custom_call" | custom-call | tf_op jit(solution)/shard_map/unpack/pallas_call | solution.py:501
  (25 shorter events, 0.1 us)
Async XLA Ops:
  0.6 1.0 %copy-start = (bf16[16,32,256]{2,1,0:T(8,128)(2,1)S(1)}, bf16[16,32,256]{2,1,0:T(8,128)(2,1)}, u32[]{:S(2)}) copy-start(bf16[16,32,256]{2,1,0:T(8,128)(2,1)} %fc.5) | copy-start | bytes 786436
  1.6 0.9 %copy-start.2 = (bf16[16,32,256]{2,1,0:T(8,128)(2,1)S(1)}, bf16[16,32,256]{2,1,0:T(8,128)(2,1)}, u32[]{:S(2)}) copy-start(bf16[16,32,256]{2,1,0:T(8,128)(2,1)} %cc.5) | copy-start | bytes 786436
  2.5 14.6 %copy-start.4 = (bf16[3,3,3,64,64]{4,3,2,1,0:T(8,128)(2,1)S(1)}, bf16[3,3,3,64,64]{4,3,2,1,0:T(8,128)(2,1)}, u32[]{:S(2)}) copy-start(bf16[3,3,3,64,64]{4,3,2,1,0:T(8,128)(2,1)} %param.10) | copy-start | bytes 663556
  2.5 14.6 %copy-start.5 = (bf16[3,3,3,32,32]{4,3,2,1,0:T(8,128)(2,1)S(1)}, bf16[3,3,3,32,32]{4,3,2,1,0:T(8,128)(2,1)}, u32[]{:S(2)}) copy-start(bf16[3,3,3,32,32]{4,3,2,1,0:T(8,128)(2,1)} %param.8) | copy-start | bytes 165892
  2.5 14.6 %copy-start.6 = (bf16[3,3,3,32,32]{4,3,2,1,0:T(8,128)(2,1)S(1)}, bf16[3,3,3,32,32]{4,3,2,1,0:T(8,128)(2,1)}, u32[]{:S(2)}) copy-start(bf16[3,3,3,32,32]{4,3,2,1,0:T(8,128)(2,1)} %param.12) | copy-start | bytes 165892
  2.5 14.6 %copy-start.7 = (bf16[2,2,2,32,64]{4,3,2,1,0:T(8,128)(2,1)S(1)}, bf16[2,2,2,32,64]{4,3,2,1,0:T(8,128)(2,1)}, u32[]{:S(2)}) copy-start(bf16[2,2,2,32,64]{4,3,2,1,0:T(8,128)(2,1)} %param.9) | copy-start | bytes 98308
  2.5 14.6 %copy-start.8 = (bf16[2,2,2,64,32]{3,4,2,1,0:T(8,128)(2,1)S(1)}, bf16[2,2,2,64,32]{3,4,2,1,0:T(8,128)(2,1)}, u32[]{:S(2)}) copy-start(bf16[2,2,2,64,32]{3,4,2,1,0:T(8,128)(2,1)} %param.11) | copy-start | bytes 98308
  2.9 9.9 %collective-permute-start.2 = (bf16[12,16,256]{2,1,0:T(8,128)(2,1)S(1)}, bf16[12,16,256]{2,1,0:T(8,128)(2,1)S(1)}, u32[]{:S(2)}, u32[]{:S(2)}) collective-permute-start(bf16[12,16,256]{2,1,0:T(8,128)(2,1)S(1)} %get-tuple-element.28), channel_id=1, source_target_pairs={{0,1},{1,2},{2,3},{3,4},{4,5},{5,6},{6,7},{7,8},{8,9},{9,10},{10,1... | collective-permute-start | bytes 294920 | tf_op jit(solution)/shard_map/ppermute | solution.py:549
  5.0 7.8 %collective-permute-start.3 = (bf16[12,16,256]{2,1,0:T(8,128)(2,1)S(1)}, bf16[12,16,256]{2,1,0:T(8,128)(2,1)S(1)}, u32[]{:S(2)}, u32[]{:S(2)}) collective-permute-start(bf16[12,16,256]{2,1,0:T(8,128)(2,1)S(1)} %get-tuple-element.29), channel_id=1, source_target_pairs={{0,15},{1,0},{2,1},{3,2},{4,3},{5,4},{6,5},{7,6},{8,7},{9,8},{10,9... | collective-permute-start | bytes 294920 | tf_op jit(solution)/shard_map/ppermute | solution.py:550
  10.4 9.3 %collective-permute-start = (bf16[12,32,256]{2,1,0:T(8,128)(2,1)S(1)}, bf16[12,32,256]{2,1,0:T(8,128)(2,1)S(1)}, u32[]{:S(2)}, u32[]{:S(2)}) collective-permute-start(bf16[12,32,256]{2,1,0:T(8,128)(2,1)S(1)} %get-tuple-element.26), channel_id=1, source_target_pairs={{0,16},{16,32},{32,48},{48,64},{64,80},{80,96},{96,112},{112,128},... | collective-permute-start | bytes 589832 | tf_op jit(solution)/shard_map/ppermute | solution.py:551
  12.5 7.2 %collective-permute-start.1 = (bf16[12,32,256]{2,1,0:T(8,128)(2,1)S(1)}, bf16[12,32,256]{2,1,0:T(8,128)(2,1)S(1)}, u32[]{:S(2)}, u32[]{:S(2)}) collective-permute-start(bf16[12,32,256]{2,1,0:T(8,128)(2,1)S(1)} %get-tuple-element.27), channel_id=1, source_target_pairs={{0,240},{16,0},{32,16},{48,32},{64,48},{80,64},{96,80},{112,96},{1... | collective-permute-start | bytes 589832 | tf_op jit(solution)/shard_map/ppermute | solution.py:552
  12.8 6.7 %collective-permute-start.4 = (bf16[24,8,256]{2,1,0:T(8,128)(2,1)S(1)}, bf16[24,8,256]{2,1,0:T(8,128)(2,1)S(1)}, u32[]{:S(2)}, u32[]{:S(2)}) collective-permute-start(bf16[24,8,256]{2,1,0:T(8,128)(2,1)S(1)} %pad_maximum_fusion), channel_id=1, source_target_pairs={{0,16},{16,32},{32,48},{48,64},{64,80},{80,96},{96,112},{112,128},... | collective-permute-start | bytes 294920 | tf_op jit(solution)/shard_map/ppermute | solution.py:555
  15.3 4.3 %collective-permute-start.5 = (bf16[24,8,256]{2,1,0:T(8,128)(2,1)S(1)}, bf16[24,8,256]{2,1,0:T(8,128)(2,1)S(1)}, u32[]{:S(2)}, u32[]{:S(2)}) collective-permute-start(bf16[24,8,256]{2,1,0:T(8,128)(2,1)S(1)} %pad_maximum_fusion.1), channel_id=1, source_target_pairs={{0,240},{16,0},{32,16},{48,32},{64,48},{80,64},{96,80},{112,96},{1... | collective-permute-start | bytes 294920 | tf_op jit(solution)/shard_map/ppermute | solution.py:556
  17.1 2.5 %copy-start.1 = (bf16[16,32,256]{2,1,0:T(8,128)(2,1)S(1)}, bf16[16,32,256]{2,1,0:T(8,128)(2,1)}, u32[]{:S(2)}) copy-start(bf16[16,32,256]{2,1,0:T(8,128)(2,1)} %fc.5) | copy-start | bytes 786436
  17.1 2.5 %copy-start.3 = (bf16[16,32,256]{2,1,0:T(8,128)(2,1)S(1)}, bf16[16,32,256]{2,1,0:T(8,128)(2,1)}, u32[]{:S(2)}) copy-start(bf16[16,32,256]{2,1,0:T(8,128)(2,1)} %cc.5) | copy-start | bytes 786436
  35.9 22.0 %copy-start.9 = (bf16[18,48,256]{2,1,0:T(8,128)(2,1)}, bf16[18,48,256]{2,1,0:T(8,128)(2,1)S(1)}, u32[]{:S(2)}) copy-start(bf16[18,48,256]{2,1,0:T(8,128)(2,1)S(1)} %get-tuple-element.35.skip_rows) | copy-start | bytes 1327108
  35.9 22.0 %copy-start.11 = (bf16[18,48,256]{2,1,0:T(8,128)(2,1)}, bf16[18,48,256]{2,1,0:T(8,128)(2,1)S(1)}, u32[]{:S(2)}) copy-start(bf16[18,48,256]{2,1,0:T(8,128)(2,1)S(1)} %get-tuple-element.36.down_rows) | copy-start | bytes 1327108
  71.9 16.8 %all-to-all-start.2 = ((bf16[32,56,128]{2,1,0:T(8,128)(2,1)}), bf16[32,56,128]{2,1,0:T(8,128)(2,1)S(1)}, u32[]{:S(2)}, u32[]{:S(2)}) async-start(bf16[32,56,128]{2,1,0:T(8,128)(2,1)} %broadcast_in_dim.7), calls=%async_computation.2 | async-start | bytes 917504 | tf_op jit(solution)/shard_map/all_to_all | solution.py:585
  78.4 1.0 %copy-start.10 = (bf16[18,48,256]{2,1,0:T(8,128)(2,1)S(1)}, bf16[18,48,256]{2,1,0:T(8,128)(2,1)}, u32[]{:S(2)}) copy-start(bf16[18,48,256]{2,1,0:T(8,128)(2,1)} %copy-done.9) | copy-start | bytes 1327108
  79.4 1.0 %copy-start.12 = (bf16[18,48,256]{2,1,0:T(8,128)(2,1)S(1)}, bf16[18,48,256]{2,1,0:T(8,128)(2,1)}, u32[]{:S(2)}) copy-start(bf16[18,48,256]{2,1,0:T(8,128)(2,1)} %copy-done.11) | copy-start | bytes 1327108

commit v4 on v3

--- a/solution.py
+++ b/solution.py
@@ -31,12 +31,25 @@
     return v.astype(BF).astype(F32)
 
 
-def loop(n, body):
+MOST = 6
+
+
+def loop(n, body, most=None):
+    together = max(k for k in range(1, (most or MOST) + 1) if n % k == 0)
+
     def step(i, carry):
-        body(i)
+        for k in range(together):
+            body(i * together + k)
         return carry
 
-    lax.fori_loop(0, n, step, 0)
+    if together == n:
+        step(0, 0)
+    else:
+        lax.fori_loop(0, n // together, step, 0)
+
+
+def aligned(at):
+    return at if isinstance(at, int) else pl.multiple_of(at, 8)
 
 
 def repeat_matrix(rows, cols, period, first):
@@ -52,7 +65,7 @@
         group = lax.broadcasted_iota(jnp.int32, (ch, W), 1) // ch
 
         def tap(t):
-            base = pl.multiple_of(t * 3 * ch, ch)
+            base = t * 3 * ch if isinstance(t, int) else pl.multiple_of(t * 3 * ch, ch)
             t0 = wide[pl.ds(base, ch), :]
             t1 = wide[pl.ds(base + ch, ch), :]
             t2 = wide[pl.ds(base + 2 * ch, ch), :]
@@ -64,7 +77,7 @@
                     rows = jnp.where(group == p - 1, t2, rows)
                 out[pl.ds(pl.multiple_of(t * W + p * ch, ch), ch), :] = rows.astype(BF)
 
-        loop(9, tap)
+        loop(9, tap, 3)
 
     band(wd, bd, wide, 32)
     band(wup, bu, wide, 32)
@@ -103,16 +116,11 @@
 
 def get_row(src, row):
     if len(src.shape) == 3 and src.shape[2] == 128:
-        at = pl.ds(pl.multiple_of(row * EY, 8), EY)
+        at = pl.ds(aligned(row * EY), EY)
         return jnp.concatenate([src[0, at, :], src[1, at, :]], axis=1)
     if len(src.shape) == 3:
         return src[row]
     return jnp.concatenate([src[0, row], src[1, row]], axis=1)
-
-
-def clear_ends(src, half, row):
-    for at in (0, 40):
-        src[half, pl.ds(pl.multiple_of(row * EY + at, 8), 8), :] = jnp.zeros((8, 128), F32)
 
 
 def get_rows(src, rows):
@@ -213,7 +221,7 @@
 ):
     def gather(dst, count, center, off):
         def put(row, value):
-            at = pl.ds(pl.multiple_of(row * EY + 8, 8), BY)
+            at = pl.ds(aligned(row * EY + 8), BY)
             dst[0, at, :] = value[:, 0:128]
             dst[1, at, :] = value[:, 128:256]
 
@@ -237,9 +245,6 @@
                 for h in range(2):
                     dst[h, pl.ds(y, EX, stride=EY), :] = column[:, h * 128 : h * 128 + 128]
 
-    for ext in (fe, ce):
-        for h in range(2):
-            loop(EX, lambda x: clear_ends(ext, h, x))
     gather(fe, HF, fc, 0)
     gather(ce, HC, cc, HF)
 
@@ -256,7 +261,7 @@
         put_rows(hid, at, rounded(pre * sig).reshape(14, EY, W))
         put_rows(ds_down, at, (sig * (1.0 + pre * (1.0 - sig))).reshape(14, EY, W))
 
-    loop(2, down)
+    loop(2, down, 1)
 
     pad = jnp.zeros((CY - EY // 2, W), F32)
 
@@ -278,7 +283,7 @@
         co[pl.ds(8 * i, 8)] = rounded(pre * sig).reshape(8, CY, W)
         ds_pool[pl.ds(8 * i, 8)] = (sig * (1.0 + pre * (1.0 - sig))).reshape(8, CY, W)
 
-    loop(2, pool)
+    loop(2, pool, 1)
 
     loop(14, lambda i: taps_to_lanes(co, 1 + i, v3m, i, 0, CY))
 
@@ -302,7 +307,7 @@
                     put_every_second(skp, row, j, rounded(pre * sig))
                     put_every_second(ds_up, row, j, sig * (1.0 + pre * (1.0 - sig)))
 
-    loop(2, up)
+    loop(2, up, 1)
 
     loop(18, lambda i: taps_to_lanes(skp, 7 + i, v3s, i, 8, BY))
     loop(18, lambda i: put_row(skip_rows, i, get_row(skp, 7 + i)))
@@ -314,7 +319,7 @@
         at = pl.ds(4 + 12 * i, 12)
         put_rows(dup, at, rounded(total.reshape(12, EY, W) * get_rows(ds_up, at)))
 
-    loop(2, d_up)
+    loop(2, d_up, 1)
 
     cot_t = cc[...].reshape(BX * BY, W).astype(F32).T.astype(BF)
     fold = repeat_matrix(32, W, 32, 0)
@@ -514,22 +519,34 @@
     return [(i, (i + step) % n) for i in range(n)]
 
 
-def pack_kernel(fc, cc, first_x, last_x, first_y, last_y, wide):
-    first_x[0:HF] = fc[0:HF]
-    first_x[HF : HF + HC] = cc[0:HC]
-    last_x[0:HF] = fc[BX - HF : BX]
-    last_x[HF : HF + HC] = cc[BX - HC : BX]
+def pack_kernel(fc, cc, first_x, last_x, first_y, last_y, side, wide, sems):
+    copies = []
+
+    def fetch(src, dst):
+        copy = pltpu.make_async_copy(src, dst, sems.at[len(copies)])
+        copy.start()
+        copies.append(copy)
+
+    for k, src in enumerate((fc, cc)):
+        fetch(src.at[:, 0:16], side.at[2 * k])
+        fetch(src.at[:, BY - 16 : BY], side.at[2 * k + 1])
     for src, count, at in ((fc, HF, 0), (cc, HC, HF)):
-        for h in range(2):
-            lanes = slice(h * 128, h * 128 + 128)
-            wide[h] = src[:, :, lanes].reshape(BX * BY, 128).astype(F32)
-        for c in range(count):
+        fetch(src.at[0:count], first_x.at[at : at + count])
+        fetch(src.at[BX - count : BX], last_x.at[at : at + count])
+    for copy in copies[:4]:
+        copy.wait()
+    for k, (count, at) in enumerate(((HF, 0), (HC, HF))):
+        for e, (out, first) in enumerate(((first_y, 0), (last_y, 16 - count))):
             for h in range(2):
                 lanes = slice(h * 128, h * 128 + 128)
-                column = wide[h, pl.ds(c, BX, stride=BY), :]
-                first_y[at + c, :, lanes] = column.astype(BF)
-                column = wide[h, pl.ds(BY - count + c, BX, stride=BY), :]
-                last_y[at + c, :, lanes] = column.astype(BF)
+                wide[h] = side[2 * k + e, :, :, lanes].reshape(BX * 16, 128).astype(F32)
+            for c in range(count):
+                for h in range(2):
+                    lanes = slice(h * 128, h * 128 + 128)
+                    column = wide[h, pl.ds(first + c, BX, stride=16), :]
+                    out[at + c, :, lanes] = column.astype(BF)
+    for copy in copies[4:]:
+        copy.wait()
 
 
 def pack(fields, cot):
@@ -538,8 +555,13 @@
     return pl.pallas_call(
         pack_kernel,
         out_shape=(rows, rows, columns, columns),
-        scratch_shapes=[pltpu.VMEM((2, BX * BY, 128), F32)],
-        compiler_params=pltpu.CompilerParams(vmem_limit_bytes=8 * 1024 * 1024),
+        in_specs=[pl.BlockSpec(memory_space=pl.ANY)] * 2,
+        scratch_shapes=[
+            pltpu.VMEM((4, BX, 16, W), BF),
+            pltpu.VMEM((2, BX * 16, 128), F32),
+            pltpu.SemaphoreType.DMA((8,)),
+        ],
+        compiler_params=pltpu.CompilerParams(vmem_limit_bytes=56 * 1024 * 1024),
         name="pack",
     )(fields, cot)
 

time: 90.7 us -> 89.2 us (0.983)
  local copies, waits for them, and re-layouts: 4.82 us -> 2.93 us
    pallas_call x1, Pallas kernels: 0.29 us -> 2.22 us  [pack(): pl.pallas_call(pack_kernel, out_shape=(rows, rows, columns, columns), in_...]
    unnamed x26 -> x22, local copies, waits for them, and re-layouts: 3.96 us -> 2.07 us
    pallas_call x1, Pallas kernels: 16.3 us -> 14.8 us  [main_call(): pl.pallas_call(main_kernel, out_shape=(jax.ShapeDtypeStruct((term_rows, 1...]
where the time goes in v4:
time: 89.2 us; the launch traced here: 88.9 us
  blocking collectives  34.8 us (39%)
  Pallas kernels  24.4 us (27%)
  starting transfers between devices  20.1 us (23%)
  waiting for transfers between devices  5.49 us (6%)
  local copies, waits for them, and re-layouts  2.93 us (3%)
  between operations  1.01 us (1%)
    all_to_all x1, blocking collectives, per_device(): part = swap(terms.reshape(n1, rows, 128), axis_index_groups=near)  21.7 us
    pallas_call x1, Pallas kernels, main_call(): pl.pallas_call(main_kernel, out_shape=(jax.ShapeDtypeStruct((term_rows, 1...  14.8 us
    all_to_all x1, blocking collectives, per_device(): swap(jnp.broadcast_to(part, (n2, rows, 128)), axis_index_groups=far)  13.1 us
    all_to_all x1, starting transfers between devices, per_device(): swap(jnp.broadcast_to(part, (n1, rows, 128)), axis_index_groups=near)  6.4 us
    ppermute x1, starting transfers between devices, exchange(): yhi = lax.ppermute(first_y, 'gy', ring('gy', -1))  5.38 us
    all_to_all x1, waiting for transfers between devices, per_device(): swap(jnp.broadcast_to(part, (n1, rows, 128)), axis_index_groups=near)  4.6 us
    pallas_call x1, Pallas kernels, finish_call(): pl.pallas_call(finish_kernel, out_shape=(block, block), scratch_shapes=[p...  3.72 us
    ppermute x1, starting transfers between devices, exchange(): clo = lax.ppermute(last_c, 'gx', ring('gx', 1))  2.49 us
  transfers between devices with their start and end apart: 7, of which 3 were waited for; matrix products, arithmetic and copies ran while one was open for 0% of the time, Pallas kernels for 7%

profile of v4, /device:TPU:1, one launch (start us, length us, event | category | flops | bytes accessed | tf_op | source)
XLA Modules:
  0.0 88.9 jit_solution(12704837559300427163)
XLA Ops:
  0.7 2.2 %pack.1 = (bf16[12,32,256]{2,1,0:T(8,128)(2,1)}, bf16[12,32,256]{2,1,0:T(8,128)(2,1)}, bf16[12,16,256]{2,1,0:T(8,128)(2,1)}, bf16[12,16,256]{2,1,0:T(8,128)(2,1)}) custom-call(bf16[16,32,256]{2,1,0:T(8,128)(2,1)} %fc.5, bf16[16,32,256]{2,1,0:T(8,128)(2,1)} %cc.5), custom_call_target="tpu_custom_call" | custom-call | tf_op jit(solution)/shard_map/pack/pallas_call | solution.py:555
  2.9 2.1 %collective-permute-start.2 = (bf16[12,16,256]{2,1,0:T(8,128)(2,1)}, bf16[12,16,256]{2,1,0:T(8,128)(2,1)S(1)}, u32[]{:S(2)}, u32[]{:S(2)}) collective-permute-start(bf16[12,16,256]{2,1,0:T(8,128)(2,1)} %get-tuple-element.28), channel_id=1, source_target_pairs={{0,1},{1,2},{2,3},{3,4},{4,5},{5,6},{6,7},{7,8},{8,9},{9,10},{10,1... | collective-permute-start | bytes 294920 | tf_op jit(solution)/shard_map/ppermute | solution.py:571
  5.0 5.4 %collective-permute-start.3 = (bf16[12,16,256]{2,1,0:T(8,128)(2,1)}, bf16[12,16,256]{2,1,0:T(8,128)(2,1)S(1)}, u32[]{:S(2)}, u32[]{:S(2)}) collective-permute-start(bf16[12,16,256]{2,1,0:T(8,128)(2,1)} %get-tuple-element.29), channel_id=1, source_target_pairs={{0,15},{1,0},{2,1},{3,2},{4,3},{5,4},{6,5},{7,6},{8,7},{9,8},{10,9... | collective-permute-start | bytes 294920 | tf_op jit(solution)/shard_map/ppermute | solution.py:572
  10.4 2.1 %collective-permute-start = (bf16[12,32,256]{2,1,0:T(8,128)(2,1)}, bf16[12,32,256]{2,1,0:T(8,128)(2,1)S(1)}, u32[]{:S(2)}, u32[]{:S(2)}) collective-permute-start(bf16[12,32,256]{2,1,0:T(8,128)(2,1)} %get-tuple-element.26), channel_id=1, source_target_pairs={{0,16},{16,32},{32,48},{48,64},{64,80},{80,96},{96,112},{112,128},... | collective-permute-start | bytes 589832 | tf_op jit(solution)/shard_map/ppermute | solution.py:573
  12.5 0.0 collective-permute-start.1
  12.5 0.5 collective-permute-done.2.ylo
  13.1 0.0 collective-permute-done.3.yhi
  13.1 2.5 %collective-permute-start.4 = (bf16[24,8,256]{2,1,0:T(8,128)(2,1)S(1)}, bf16[24,8,256]{2,1,0:T(8,128)(2,1)S(1)}, u32[]{:S(2)}, u32[]{:S(2)}) collective-permute-start(bf16[24,8,256]{2,1,0:T(8,128)(2,1)S(1)} %pad_maximum_fusion), channel_id=1, source_target_pairs={{0,16},{16,32},{32,48},{48,64},{64,80},{80,96},{96,112},{112,128},... | collective-permute-start | bytes 294920 | tf_op jit(solution)/shard_map/ppermute | solution.py:577
  15.6 1.5 %collective-permute-start.5 = (bf16[24,8,256]{2,1,0:T(8,128)(2,1)S(1)}, bf16[24,8,256]{2,1,0:T(8,128)(2,1)S(1)}, u32[]{:S(2)}, u32[]{:S(2)}) collective-permute-start(bf16[24,8,256]{2,1,0:T(8,128)(2,1)S(1)} %pad_maximum_fusion.1), channel_id=1, source_target_pairs={{0,240},{16,0},{32,16},{48,32},{64,48},{80,64},{96,80},{112,96},{1... | collective-permute-start | bytes 294920 | tf_op jit(solution)/shard_map/ppermute | solution.py:578
  17.2 0.0 copy-done.4
  17.2 0.0 copy-done.2
  17.2 0.0 copy-start
  17.2 0.0 copy-start.1
  17.2 2.3 %bands.1 = (bf16[2304,256]{1,0:T(8,128)(2,1)S(1)}, bf16[1024,256]{1,0:T(8,128)(2,1)S(1)}, bf16[2304,256]{1,0:T(8,128)(2,1)S(1)}, bf16[1024,256]{1,0:T(8,128)(2,1)S(1)}, bf16[2304,256]{1,0:T(8,128)(2,1)S(1)}) custom-call(bf16[864,32]{1,0:T(8,128)(2,1)S(1)} %bitcast.19, bf16[4,64,64]{2,1,0:T(8,128)(2,1)S(1)} %bitcast.21, bf16[1728,64]{1,0:T(8,128)(2,1)S(1)} %bitcast.18, ...), custom_call_target="tpu_custom_call" | custom-call | flops 2000000000 | bytes 8000000 | tf_op jit(solution)/shard_map/bands/pallas_call | solution.py:101
  19.5 0.0 collective-permute-done.4.clo
  19.5 0.4 collective-permute-done.5.chi
  19.9 0.0 collective-permute-done.xlo
  19.9 0.0 collective-permute-done.1.xhi
  19.9 14.8 %network.1 = (bf16[1792,128]{1,0:T(8,128)(2,1)S(1)}, bf16[18,48,256]{2,1,0:T(8,128)(2,1)S(1)}, bf16[18,48,256]{2,1,0:T(8,128)(2,1)S(1)}) custom-call(bf16[16,32,256]{2,1,0:T(8,128)(2,1)S(1)} %copy-done, bf16[16,32,256]{2,1,0:T(8,128)(2,1)S(1)} %copy-done.1, bf16[12,32,256]{2,1,0:T(8,128)(2,1)S(1)} %collective-permute-done.xlo, ...), custom_call_target="tpu_custom_call" | custom-call | flops 10000000000 | bytes 10000000 | tf_op jit(solution)/shard_map/network/pallas_call | solution.py:443
  34.7 0.0 copy-start.7
  34.7 0.0 copy-start.9
  34.7 21.7 %all_to_all.15 = bf16[32,56,128]{2,1,0:T(8,128)(2,1)S(1)} all-to-all(bf16[32,56,128]{2,1,0:T(8,128)(2,1)S(1)} %bitcast.17), channel_id=1, replica_groups={{0,1,16,17,32,33,48,49,64,65,80,81,96,97,112,113,128,129,144,145,160,16..., dimensions={0} | all-to-all | bytes 917504 | tf_op jit(solution)/shard_map/all_to_all | solution.py:600
  56.5 0.1 convert_reduce_fusion
  56.6 13.1 %all_to_all.16 = bf16[8,56,128]{2,1,0:T(8,128)(2,1)S(1)} all-to-all(bf16[8,56,128]{2,1,0:T(8,128)(2,1)S(1)} %broadcast_in_dim.6), channel_id=1, replica_groups={{0,2,4,6,8,10,12,14},{1,3,5,7,9,11,13,15},{16,18,20,22,24,26,28,30},{17..., dimensions={0} | all-to-all | bytes 229376 | tf_op jit(solution)/shard_map/all_to_all | solution.py:605
  69.7 0.8 broadcast_in_dim.7
  70.5 6.4 %all-to-all-start.2 = ((bf16[32,56,128]{2,1,0:T(8,128)(2,1)}), bf16[32,56,128]{2,1,0:T(8,128)(2,1)S(1)}, u32[]{:S(2)}, u32[]{:S(2)}) async-start(bf16[32,56,128]{2,1,0:T(8,128)(2,1)} %broadcast_in_dim.7), calls=%async_computation.2 | async-start | bytes 917504 | tf_op jit(solution)/shard_map/all_to_all | solution.py:607
  76.9 0.0 copy-start.8
  76.9 1.0 %copy-done.8 = bf16[18,48,256]{2,1,0:T(8,128)(2,1)S(1)} copy-done((bf16[18,48,256]{2,1,0:T(8,128)(2,1)S(1)}, bf16[18,48,256]{2,1,0:T(8,128)(2,1)}, u32[]{:S(2)}) %copy-start.8) | copy-done | bytes 442392
  77.9 1.0 %copy-done.10 = bf16[18,48,256]{2,1,0:T(8,128)(2,1)S(1)} copy-done((bf16[18,48,256]{2,1,0:T(8,128)(2,1)S(1)}, bf16[18,48,256]{2,1,0:T(8,128)(2,1)}, u32[]{:S(2)}) %copy-start.10) | copy-done | bytes 442392
  79.0 3.7 %finish.1 = (bf16[16,32,256]{2,1,0:T(8,128)(2,1)}, bf16[16,32,256]{2,1,0:T(8,128)(2,1)}) custom-call(bf16[16,32,256]{2,1,0:T(8,128)(2,1)S(1)} %copy-done, bf16[16,32,256]{2,1,0:T(8,128)(2,1)S(1)} %copy-done.1, bf16[18,48,256]{2,1,0:T(8,128)(2,1)S(1)} %copy-done.8, bf16[18,48,256]{2,1,0:T(8,128)(2,1)S(1)} %copy-done.10, ...), custom_call_target="tpu_custom_call" | custom-call | flops 3000000000 | bytes 10000000 | tf_op jit(solution)/shard_map/finish/pallas_call | solution.py:428
  82.7 4.6 %all-to-all-done.2 = bf16[32,56,128]{2,1,0:T(8,128)(2,1)S(1)} async-done(((bf16[32,56,128]{2,1,0:T(8,128)(2,1)}), bf16[32,56,128]{2,1,0:T(8,128)(2,1)S(1)}, u32[]{:S(2)}, u32[]{:S(2)}) %all-to-all-start.2) | async-done | bytes 458784 | tf_op jit(solution)/shard_map/all_to_all | solution.py:607
  87.3 1.4 %unpack.1 = (f32[27,32,32]{2,1,0:T(8,128)}, f32[4,64,64]{2,1,0:T(8,128)}, f32[27,64,64]{2,1,0:T(8,128)}, f32[4,64,64]{2,1,0:T(8,128)}, f32[27,32,32]{2,1,0:T(8,128)}) custom-call(bf16[1792,128]{1,0:T(8,128)(2,1)S(1)} %bitcast.16), custom_call_target="tpu_custom_call" | custom-call | tf_op jit(solution)/shard_map/unpack/pallas_call | solution.py:506
  (21 shorter events, 0.1 us)
Async XLA Ops:
  0.6 16.5 %copy-start.4 = (bf16[3,3,3,32,32]{4,3,2,1,0:T(8,128)(2,1)S(1)}, bf16[3,3,3,32,32]{4,3,2,1,0:T(8,128)(2,1)}, u32[]{:S(2)}) copy-start(bf16[3,3,3,32,32]{4,3,2,1,0:T(8,128)(2,1)} %param.12) | copy-start | bytes 165892
  0.6 16.5 %copy-start.6 = (bf16[2,2,2,64,32]{3,4,2,1,0:T(8,128)(2,1)S(1)}, bf16[2,2,2,64,32]{3,4,2,1,0:T(8,128)(2,1)}, u32[]{:S(2)}) copy-start(bf16[2,2,2,64,32]{3,4,2,1,0:T(8,128)(2,1)} %param.11) | copy-start | bytes 98308
  0.7 16.5 %copy-start.2 = (bf16[3,3,3,64,64]{4,3,2,1,0:T(8,128)(2,1)S(1)}, bf16[3,3,3,64,64]{4,3,2,1,0:T(8,128)(2,1)}, u32[]{:S(2)}) copy-start(bf16[3,3,3,64,64]{4,3,2,1,0:T(8,128)(2,1)} %param.10) | copy-start | bytes 663556
  0.7 16.5 %copy-start.5 = (bf16[2,2,2,32,64]{4,3,2,1,0:T(8,128)(2,1)S(1)}, bf16[2,2,2,32,64]{4,3,2,1,0:T(8,128)(2,1)}, u32[]{:S(2)}) copy-start(bf16[2,2,2,32,64]{4,3,2,1,0:T(8,128)(2,1)} %param.9) | copy-start | bytes 98308
  0.7 16.5 %copy-start.3 = (bf16[3,3,3,32,32]{4,3,2,1,0:T(8,128)(2,1)S(1)}, bf16[3,3,3,32,32]{4,3,2,1,0:T(8,128)(2,1)}, u32[]{:S(2)}) copy-start(bf16[3,3,3,32,32]{4,3,2,1,0:T(8,128)(2,1)} %param.8) | copy-start | bytes 165892
  2.9 10.1 %collective-permute-start.2 = (bf16[12,16,256]{2,1,0:T(8,128)(2,1)}, bf16[12,16,256]{2,1,0:T(8,128)(2,1)S(1)}, u32[]{:S(2)}, u32[]{:S(2)}) collective-permute-start(bf16[12,16,256]{2,1,0:T(8,128)(2,1)} %get-tuple-element.28), channel_id=1, source_target_pairs={{0,1},{1,2},{2,3},{3,4},{4,5},{5,6},{6,7},{7,8},{8,9},{9,10},{10,1... | collective-permute-start | bytes 294920 | tf_op jit(solution)/shard_map/ppermute | solution.py:571
  5.0 8.0 %collective-permute-start.3 = (bf16[12,16,256]{2,1,0:T(8,128)(2,1)}, bf16[12,16,256]{2,1,0:T(8,128)(2,1)S(1)}, u32[]{:S(2)}, u32[]{:S(2)}) collective-permute-start(bf16[12,16,256]{2,1,0:T(8,128)(2,1)} %get-tuple-element.29), channel_id=1, source_target_pairs={{0,15},{1,0},{2,1},{3,2},{4,3},{5,4},{6,5},{7,6},{8,7},{9,8},{10,9... | collective-permute-start | bytes 294920 | tf_op jit(solution)/shard_map/ppermute | solution.py:572
  10.4 9.5 %collective-permute-start = (bf16[12,32,256]{2,1,0:T(8,128)(2,1)}, bf16[12,32,256]{2,1,0:T(8,128)(2,1)S(1)}, u32[]{:S(2)}, u32[]{:S(2)}) collective-permute-start(bf16[12,32,256]{2,1,0:T(8,128)(2,1)} %get-tuple-element.26), channel_id=1, source_target_pairs={{0,16},{16,32},{32,48},{48,64},{64,80},{80,96},{96,112},{112,128},... | collective-permute-start | bytes 589832 | tf_op jit(solution)/shard_map/ppermute | solution.py:573
  12.5 7.4 %collective-permute-start.1 = (bf16[12,32,256]{2,1,0:T(8,128)(2,1)}, bf16[12,32,256]{2,1,0:T(8,128)(2,1)S(1)}, u32[]{:S(2)}, u32[]{:S(2)}) collective-permute-start(bf16[12,32,256]{2,1,0:T(8,128)(2,1)} %get-tuple-element.27), channel_id=1, source_target_pairs={{0,240},{16,0},{32,16},{48,32},{64,48},{80,64},{96,80},{112,96},{1... | collective-permute-start | bytes 589832 | tf_op jit(solution)/shard_map/ppermute | solution.py:574
  13.1 6.4 %collective-permute-start.4 = (bf16[24,8,256]{2,1,0:T(8,128)(2,1)S(1)}, bf16[24,8,256]{2,1,0:T(8,128)(2,1)S(1)}, u32[]{:S(2)}, u32[]{:S(2)}) collective-permute-start(bf16[24,8,256]{2,1,0:T(8,128)(2,1)S(1)} %pad_maximum_fusion), channel_id=1, source_target_pairs={{0,16},{16,32},{32,48},{48,64},{64,80},{80,96},{96,112},{112,128},... | collective-permute-start | bytes 294920 | tf_op jit(solution)/shard_map/ppermute | solution.py:577
  15.6 4.3 %collective-permute-start.5 = (bf16[24,8,256]{2,1,0:T(8,128)(2,1)S(1)}, bf16[24,8,256]{2,1,0:T(8,128)(2,1)S(1)}, u32[]{:S(2)}, u32[]{:S(2)}) collective-permute-start(bf16[24,8,256]{2,1,0:T(8,128)(2,1)S(1)} %pad_maximum_fusion.1), channel_id=1, source_target_pairs={{0,240},{16,0},{32,16},{48,32},{64,48},{80,64},{96,80},{112,96},{1... | collective-permute-start | bytes 294920 | tf_op jit(solution)/shard_map/ppermute | solution.py:578
  17.2 2.7 %copy-start = (bf16[16,32,256]{2,1,0:T(8,128)(2,1)S(1)}, bf16[16,32,256]{2,1,0:T(8,128)(2,1)}, u32[]{:S(2)}) copy-start(bf16[16,32,256]{2,1,0:T(8,128)(2,1)} %fc.5) | copy-start | bytes 786436
  17.2 2.7 %copy-start.1 = (bf16[16,32,256]{2,1,0:T(8,128)(2,1)S(1)}, bf16[16,32,256]{2,1,0:T(8,128)(2,1)}, u32[]{:S(2)}) copy-start(bf16[16,32,256]{2,1,0:T(8,128)(2,1)} %cc.5) | copy-start | bytes 786436
  34.7 21.7 %copy-start.7 = (bf16[18,48,256]{2,1,0:T(8,128)(2,1)}, bf16[18,48,256]{2,1,0:T(8,128)(2,1)S(1)}, u32[]{:S(2)}) copy-start(bf16[18,48,256]{2,1,0:T(8,128)(2,1)S(1)} %get-tuple-element.35.skip_rows) | copy-start | bytes 1327108
  34.7 21.8 %copy-start.9 = (bf16[18,48,256]{2,1,0:T(8,128)(2,1)}, bf16[18,48,256]{2,1,0:T(8,128)(2,1)S(1)}, u32[]{:S(2)}) copy-start(bf16[18,48,256]{2,1,0:T(8,128)(2,1)S(1)} %get-tuple-element.36.down_rows) | copy-start | bytes 1327108
  70.5 16.8 %all-to-all-start.2 = ((bf16[32,56,128]{2,1,0:T(8,128)(2,1)}), bf16[32,56,128]{2,1,0:T(8,128)(2,1)S(1)}, u32[]{:S(2)}, u32[]{:S(2)}) async-start(bf16[32,56,128]{2,1,0:T(8,128)(2,1)} %broadcast_in_dim.7), calls=%async_computation.2 | async-start | bytes 917504 | tf_op jit(solution)/shard_map/all_to_all | solution.py:607
  76.9 1.0 %copy-start.8 = (bf16[18,48,256]{2,1,0:T(8,128)(2,1)S(1)}, bf16[18,48,256]{2,1,0:T(8,128)(2,1)}, u32[]{:S(2)}) copy-start(bf16[18,48,256]{2,1,0:T(8,128)(2,1)} %copy-done.7) | copy-start | bytes 1327108
  77.9 1.0 %copy-start.10 = (bf16[18,48,256]{2,1,0:T(8,128)(2,1)S(1)}, bf16[18,48,256]{2,1,0:T(8,128)(2,1)}, u32[]{:S(2)}) copy-start(bf16[18,48,256]{2,1,0:T(8,128)(2,1)} %copy-done.9) | copy-start | bytes 1327108

commit v5 on v4

--- a/solution.py
+++ b/solution.py
@@ -31,7 +31,8 @@
     return v.astype(BF).astype(F32)
 
 
-MOST = 6
+DOWN, D_UP, UP = 7, 6, 3
+MOST = 64
 
 
 def loop(n, body, most=None):
@@ -77,7 +78,7 @@
                     rows = jnp.where(group == p - 1, t2, rows)
                 out[pl.ds(pl.multiple_of(t * W + p * ch, ch), ch), :] = rows.astype(BF)
 
-        loop(9, tap, 3)
+        loop(9, tap)
 
     band(wd, bd, wide, 32)
     band(wup, bu, wide, 32)
@@ -214,9 +215,9 @@
 def main_kernel(
     fc, cc, xlo, xhi, ylo, yhi, clo, chi, bd, pm, bm, um, bu,
     terms, skip_rows, down_rows,
-    fe, ce, hid, ds_down, skp, ds_up, dup, ddn,
+    fe, ce, hid, ds_down, skp, dup, ddn,
     v3f, v3c, v3fl, v3s,
-    parts, co, mid, ds_pool, ds_mid, dmid, v3m, v3dm, v3ml, local,
+    parts, d_parts, co, mid, ds_pool, ds_mid, dmid, v3m, v3dm, v3ml,
     hi, lo, him, lom, dsc,
 ):
     def gather(dst, count, center, off):
@@ -255,13 +256,21 @@
     put_rows(hid, slice(30, 32), zero)
 
     def down(i):
-        pre = conv_rows(v3f, 14 * i, 14, bd)
+        pre = conv_rows(v3f, DOWN * i, DOWN, bd)
         sig = jax.nn.sigmoid(pre)
-        at = pl.ds(2 + 14 * i, 14)
-        put_rows(hid, at, rounded(pre * sig).reshape(14, EY, W))
-        put_rows(ds_down, at, (sig * (1.0 + pre * (1.0 - sig))).reshape(14, EY, W))
-
-    loop(2, down, 1)
+        at = pl.ds(2 + DOWN * i, DOWN)
+        put_rows(hid, at, rounded(pre * sig).reshape(DOWN, EY, W))
+        put_rows(ds_down, at, (sig * (1.0 + pre * (1.0 - sig))).reshape(DOWN, EY, W))
+
+    loop(28 // DOWN, down)
+
+    loop(26, lambda i: taps_to_lanes(ce, 3 + i, v3c, i, 0, EY))
+
+    def d_up(i):
+        total = conv_t_rows(v3c, D_UP * i, D_UP, bu)
+        put_rows(dup, pl.ds(4 + D_UP * i, D_UP), total.reshape(D_UP, EY, W))
+
+    loop(24 // D_UP, d_up)
 
     pad = jnp.zeros((CY - EY // 2, W), F32)
 
@@ -283,7 +292,7 @@
         co[pl.ds(8 * i, 8)] = rounded(pre * sig).reshape(8, CY, W)
         ds_pool[pl.ds(8 * i, 8)] = (sig * (1.0 + pre * (1.0 - sig))).reshape(8, CY, W)
 
-    loop(2, pool, 1)
+    loop(2, pool)
 
     loop(14, lambda i: taps_to_lanes(co, 1 + i, v3m, i, 0, CY))
 
@@ -294,32 +303,25 @@
     ds_mid[2:14] = (sig_mid * (1.0 + pre_mid * (1.0 - sig_mid))).reshape(12, CY, W)
 
     def up(x):
-        m = mid[pl.ds(2 + 6 * x, 6)].reshape(6 * CY, W)
+        m = mid[pl.ds(2 + UP * x, UP)].reshape(UP * CY, W)
         for i in range(2):
             for j in range(2):
                 q = 2 * i + j
                 lifted = dot(m, um[q * W : (q + 1) * W, :])
-                for r in range(6):
-                    row = 2 * (2 + 6 * x + r) + i
-                    own = get_every_second(hid, row, j, EY // 2)
+                for r in range(UP):
+                    at = 2 + UP * x + r
+                    own = parts[q, at].astype(F32)[0 : EY // 2]
                     pre = own + lifted[r * CY : r * CY + EY // 2]
                     sig = jax.nn.sigmoid(pre)
-                    put_every_second(skp, row, j, rounded(pre * sig))
-                    put_every_second(ds_up, row, j, sig * (1.0 + pre * (1.0 - sig)))
-
-    loop(2, up, 1)
+                    put_every_second(skp, 2 * at + i, j, rounded(pre * sig))
+                    raw = get_every_second(dup, 2 * at + i, j, EY // 2)
+                    d_up = raw * (sig * (1.0 + pre * (1.0 - sig)))
+                    d_parts[q, at] = jnp.concatenate([d_up, pad], axis=0).astype(BF)
+
+    loop(12 // UP, up)
 
     loop(18, lambda i: taps_to_lanes(skp, 7 + i, v3s, i, 8, BY))
     loop(18, lambda i: put_row(skip_rows, i, get_row(skp, 7 + i)))
-
-    loop(26, lambda i: taps_to_lanes(ce, 3 + i, v3c, i, 0, EY))
-
-    def d_up(i):
-        total = conv_t_rows(v3c, 12 * i, 12, bu)
-        at = pl.ds(4 + 12 * i, 12)
-        put_rows(dup, at, rounded(total.reshape(12, EY, W) * get_rows(ds_up, at)))
-
-    loop(2, d_up, 1)
 
     cot_t = cc[...].reshape(BX * BY, W).astype(F32).T.astype(BF)
     fold = repeat_matrix(32, W, 32, 0)
@@ -335,13 +337,9 @@
     conv_weight_terms(cot_t, v3s, BX, 32, hi, lo, dsc)
     fold_to(fold, hi, lo, 7, 7)
 
-    def own_parts(src, x):
-        for i in range(2):
-            for j in range(2):
-                half = get_every_second(src, 8 + 2 * x + i, 8 + j, BY // 2)
-                local[2 * i + j, x] = half.astype(BF)
-
-    loop(8, lambda x: own_parts(dup, x))
+    def own_parts(src, q):
+        return src[q, 4:12].astype(F32)[:, 4:20].reshape(128, W).astype(BF)
+
     mid_t = mid[4:12].astype(F32)[:, 0:24][:, 4:20].reshape(128, W).T.astype(BF)
 
     def fold_four(tile):
@@ -350,8 +348,8 @@
             rows = slice(tile * 32 + t * 64, tile * 32 + (t + 1) * 64)
             terms[rows, :] = total[:, t * 128 : (t + 1) * 128].astype(BF)
 
-    def plain_terms(left, q, row):
-        d = dot(left, local[q].reshape(128, W))
+    def plain_terms(left, src, q, row):
+        d = dot(left, own_parts(src, q))
         for t in range(2):
             group = lax.broadcasted_iota(jnp.int32, (64, 128), 1) // 64
             low = d[(2 * t) * 64 : (2 * t + 1) * 64, t * 128 : (t + 1) * 128]
@@ -359,14 +357,12 @@
             put_split(jnp.where(group == 0, low, high), him, lom, row, t * 128)
 
     for q in range(4):
-        plain_terms(mid_t, q, 64 * q)
+        plain_terms(mid_t, d_parts, q, 64 * q)
     fold_four(46)
-
-    loop(12, lambda x: to_parts(dup, 2 + x))
 
     d_middle = None
     for q in range(4):
-        part = dot(parts[q, 2:14].reshape(12 * CY, W), um[q * W : (q + 1) * W, :], NT)
+        part = dot(d_parts[q, 2:14].reshape(12 * CY, W), um[q * W : (q + 1) * W, :], NT)
         d_middle = part if d_middle is None else d_middle + part
     dmid[2:14] = rounded(d_middle * ds_mid[2:14].reshape(12 * CY, W)).reshape(12, CY, W)
     ds_mid[2:14] = d_middle.reshape(12, CY, W)
@@ -393,7 +389,7 @@
             back = dot(dp, pm[q * W : (q + 1) * W, :], NT)
             for r in range(10):
                 row = 2 * (3 + r) + i
-                own = get_every_second(dup, row, j, EY // 2)
+                own = d_parts[q, 3 + r].astype(F32)[0 : EY // 2]
                 d_hidden = own + back[r * CY : r * CY + EY // 2]
                 slope = get_every_second(ds_down, row, j, EY // 2)
                 put_every_second(ddn, row, j, rounded(d_hidden * slope))
@@ -404,10 +400,9 @@
     conv_weight_terms(down_t, v3fl, BX, 32, hi, lo, dsc)
     fold_to(fold, hi, lo, 0, 7)
 
-    loop(8, lambda x: own_parts(hid, x))
     pool_t = ds_pool[4:12][:, 4:20].reshape(128, W).T.astype(BF)
     for q in range(4):
-        plain_terms(pool_t, q, 64 * q)
+        plain_terms(pool_t, parts, q, 64 * q)
     fold_four(42)
     rest = terms.shape[0] - TILES * 32
     if rest > 0:
@@ -444,12 +439,13 @@
         main_kernel,
         out_shape=(jax.ShapeDtypeStruct((term_rows, 128), BF), some, some),
         scratch_shapes=[flat] * 2
-        + [split] * 6
+        + [split] * 5
         + [
             pltpu.VMEM((30, EY, 3 * W), BF),
             pltpu.VMEM((26, EY, 3 * W), BF),
             pltpu.VMEM((18, BY, 3 * W), BF),
             pltpu.VMEM((18, BY, 3 * W), BF),
+            pltpu.VMEM((4, CX, CY, W), BF),
             pltpu.VMEM((4, CX, CY, W), BF),
             coarse,
             pltpu.VMEM((CX, CY, W), BF),
@@ -459,7 +455,6 @@
             pltpu.VMEM((14, CY, 3 * W), BF),
             pltpu.VMEM((12, CY, 3 * W), BF),
             pltpu.VMEM((10, 16, 3 * W), BF),
-            pltpu.VMEM((4, 8, 16, W), BF),
             pltpu.VMEM((28 * 32, W), BF),
             pltpu.VMEM((28 * 32, W), BF),
             pltpu.VMEM((28 * 64, W), BF),

time: 89.2 us -> 85.6 us (0.960)
  Pallas kernels: 24.4 us -> 18.4 us
  waiting for transfers between devices: 5.49 us -> 7.89 us
    pallas_call x1, Pallas kernels: 14.8 us -> 11.1 us  [main_call(): pl.pallas_call(main_kernel, out_shape=(jax.ShapeDtypeStruct((term_rows, 1...]
    pallas_call x1, Pallas kernels: 3.72 us -> 2.17 us  [finish_call(): pl.pallas_call(finish_kernel, out_shape=(block, block), scratch_shapes=[p...]
    all_to_all x1, waiting for transfers between devices: 4.6 us -> 6.15 us  [per_device(): swap(jnp.broadcast_to(part, (n1, rows, 128)), axis_index_groups=near)]
  transfers between devices with their start and end apart: 7 -> 7, of which waited for: 3 -> 3; matrix products, arithmetic and copies ran while one was open for 0% -> 0% of each run, Pallas kernels for 7% -> 4%
where the time goes in v5:
time: 85.6 us; the launch traced here: 85.2 us
  blocking collectives  34.8 us (41%)
  starting transfers between devices  20.1 us (23%)
  Pallas kernels  18.4 us (21%)
  waiting for transfers between devices  7.89 us (9%)
  local copies, waits for them, and re-layouts  2.93 us (3%)
  between operations  1.01 us (1%)
    all_to_all x1, blocking collectives, per_device(): part = swap(terms.reshape(n1, rows, 128), axis_index_groups=near)  21.7 us
    all_to_all x1, blocking collectives, per_device(): swap(jnp.broadcast_to(part, (n2, rows, 128)), axis_index_groups=far)  13.1 us
    pallas_call x1, Pallas kernels, main_call(): pl.pallas_call(main_kernel, out_shape=(jax.ShapeDtypeStruct((term_rows, 1...  11.1 us
    all_to_all x1, starting transfers between devices, per_device(): swap(jnp.broadcast_to(part, (n1, rows, 128)), axis_index_groups=near)  6.4 us
    all_to_all x1, waiting for transfers between devices, per_device(): swap(jnp.broadcast_to(part, (n1, rows, 128)), axis_index_groups=near)  6.15 us
    ppermute x1, starting transfers between devices, exchange(): yhi = lax.ppermute(first_y, 'gy', ring('gy', -1))  5.38 us
    ppermute x1, starting transfers between devices, exchange(): clo = lax.ppermute(last_c, 'gx', ring('gx', 1))  2.49 us
    pallas_call x1, Pallas kernels, pack(): pl.pallas_call(pack_kernel, out_shape=(rows, rows, columns, columns), in_...  2.22 us
  transfers between devices with their start and end apart: 7, of which 3 were waited for; matrix products, arithmetic and copies ran while one was open for 0% of the time, Pallas kernels for 4%

profile of v5, /device:TPU:1, one launch (start us, length us, event | category | flops | bytes accessed | tf_op | source)
XLA Modules:
  0.0 85.2 jit_solution(10536163143607719100)
XLA Ops:
  0.7 2.2 %pack.1 = (bf16[12,32,256]{2,1,0:T(8,128)(2,1)}, bf16[12,32,256]{2,1,0:T(8,128)(2,1)}, bf16[12,16,256]{2,1,0:T(8,128)(2,1)}, bf16[12,16,256]{2,1,0:T(8,128)(2,1)}) custom-call(bf16[16,32,256]{2,1,0:T(8,128)(2,1)} %fc.5, bf16[16,32,256]{2,1,0:T(8,128)(2,1)} %cc.5), custom_call_target="tpu_custom_call" | custom-call | tf_op jit(solution)/shard_map/pack/pallas_call | solution.py:550
  2.9 2.1 %collective-permute-start.2 = (bf16[12,16,256]{2,1,0:T(8,128)(2,1)}, bf16[12,16,256]{2,1,0:T(8,128)(2,1)S(1)}, u32[]{:S(2)}, u32[]{:S(2)}) collective-permute-start(bf16[12,16,256]{2,1,0:T(8,128)(2,1)} %get-tuple-element.28), channel_id=1, source_target_pairs={{0,1},{1,2},{2,3},{3,4},{4,5},{5,6},{6,7},{7,8},{8,9},{9,10},{10,1... | collective-permute-start | bytes 294920 | tf_op jit(solution)/shard_map/ppermute | solution.py:566
  5.0 5.4 %collective-permute-start.3 = (bf16[12,16,256]{2,1,0:T(8,128)(2,1)}, bf16[12,16,256]{2,1,0:T(8,128)(2,1)S(1)}, u32[]{:S(2)}, u32[]{:S(2)}) collective-permute-start(bf16[12,16,256]{2,1,0:T(8,128)(2,1)} %get-tuple-element.29), channel_id=1, source_target_pairs={{0,15},{1,0},{2,1},{3,2},{4,3},{5,4},{6,5},{7,6},{8,7},{9,8},{10,9... | collective-permute-start | bytes 294920 | tf_op jit(solution)/shard_map/ppermute | solution.py:567
  10.4 2.1 %collective-permute-start = (bf16[12,32,256]{2,1,0:T(8,128)(2,1)}, bf16[12,32,256]{2,1,0:T(8,128)(2,1)S(1)}, u32[]{:S(2)}, u32[]{:S(2)}) collective-permute-start(bf16[12,32,256]{2,1,0:T(8,128)(2,1)} %get-tuple-element.26), channel_id=1, source_target_pairs={{0,16},{16,32},{32,48},{48,64},{64,80},{80,96},{96,112},{112,128},... | collective-permute-start | bytes 589832 | tf_op jit(solution)/shard_map/ppermute | solution.py:568
  12.5 0.0 collective-permute-start.1
  12.5 0.5 collective-permute-done.2.ylo
  13.1 0.0 collective-permute-done.3.yhi
  13.1 2.5 %collective-permute-start.4 = (bf16[24,8,256]{2,1,0:T(8,128)(2,1)S(1)}, bf16[24,8,256]{2,1,0:T(8,128)(2,1)S(1)}, u32[]{:S(2)}, u32[]{:S(2)}) collective-permute-start(bf16[24,8,256]{2,1,0:T(8,128)(2,1)S(1)} %pad_maximum_fusion), channel_id=1, source_target_pairs={{0,16},{16,32},{32,48},{48,64},{64,80},{80,96},{96,112},{112,128},... | collective-permute-start | bytes 294920 | tf_op jit(solution)/shard_map/ppermute | solution.py:572
  15.6 1.5 %collective-permute-start.5 = (bf16[24,8,256]{2,1,0:T(8,128)(2,1)S(1)}, bf16[24,8,256]{2,1,0:T(8,128)(2,1)S(1)}, u32[]{:S(2)}, u32[]{:S(2)}) collective-permute-start(bf16[24,8,256]{2,1,0:T(8,128)(2,1)S(1)} %pad_maximum_fusion.1), channel_id=1, source_target_pairs={{0,240},{16,0},{32,16},{48,32},{64,48},{80,64},{96,80},{112,96},{1... | collective-permute-start | bytes 294920 | tf_op jit(solution)/shard_map/ppermute | solution.py:573
  17.2 0.0 copy-done.4
  17.2 0.0 copy-done.2
  17.2 0.0 copy-start
  17.2 0.0 copy-start.1
  17.2 1.5 %bands.1 = (bf16[2304,256]{1,0:T(8,128)(2,1)S(1)}, bf16[1024,256]{1,0:T(8,128)(2,1)S(1)}, bf16[2304,256]{1,0:T(8,128)(2,1)S(1)}, bf16[1024,256]{1,0:T(8,128)(2,1)S(1)}, bf16[2304,256]{1,0:T(8,128)(2,1)S(1)}) custom-call(bf16[864,32]{1,0:T(8,128)(2,1)S(1)} %bitcast.19, bf16[4,64,64]{2,1,0:T(8,128)(2,1)S(1)} %bitcast.21, bf16[1728,64]{1,0:T(8,128)(2,1)S(1)} %bitcast.18, ...), custom_call_target="tpu_custom_call" | custom-call | flops 2000000000 | bytes 8000000 | tf_op jit(solution)/shard_map/bands/pallas_call | solution.py:102
  18.7 0.0 collective-permute-done.4.clo
  18.7 1.2 %collective-permute-done.5.chi = bf16[24,8,256]{2,1,0:T(8,128)(2,1)S(1)} collective-permute-done((bf16[24,8,256]{2,1,0:T(8,128)(2,1)S(1)}, bf16[24,8,256]{2,1,0:T(8,128)(2,1)S(1)}, u32[]{:S(2)}, u32[]{:S(2)}) %collective-permute-start.5) | collective-permute-done | bytes 98336 | tf_op jit(solution)/shard_map/ppermute | solution.py:573
  19.9 0.0 collective-permute-done.xlo
  19.9 0.0 collective-permute-done.1.xhi
  19.9 11.1 %network.1 = (bf16[1792,128]{1,0:T(8,128)(2,1)S(1)}, bf16[18,48,256]{2,1,0:T(8,128)(2,1)S(1)}, bf16[18,48,256]{2,1,0:T(8,128)(2,1)S(1)}) custom-call(bf16[16,32,256]{2,1,0:T(8,128)(2,1)S(1)} %copy-done, bf16[16,32,256]{2,1,0:T(8,128)(2,1)S(1)} %copy-done.1, bf16[12,32,256]{2,1,0:T(8,128)(2,1)S(1)} %collective-permute-done.xlo, ...), custom_call_target="tpu_custom_call" | custom-call | flops 10000000000 | bytes 10000000 | tf_op jit(solution)/shard_map/network/pallas_call | solution.py:438
  31.0 0.0 copy-start.7
  31.1 0.0 copy-start.9
  31.1 21.7 %all_to_all.15 = bf16[32,56,128]{2,1,0:T(8,128)(2,1)S(1)} all-to-all(bf16[32,56,128]{2,1,0:T(8,128)(2,1)S(1)} %bitcast.17), channel_id=1, replica_groups={{0,1,16,17,32,33,48,49,64,65,80,81,96,97,112,113,128,129,144,145,160,16..., dimensions={0} | all-to-all | bytes 917504 | tf_op jit(solution)/shard_map/all_to_all | solution.py:595
  52.8 0.1 convert_reduce_fusion
  52.9 13.1 %all_to_all.16 = bf16[8,56,128]{2,1,0:T(8,128)(2,1)S(1)} all-to-all(bf16[8,56,128]{2,1,0:T(8,128)(2,1)S(1)} %broadcast_in_dim.6), channel_id=1, replica_groups={{0,2,4,6,8,10,12,14},{1,3,5,7,9,11,13,15},{16,18,20,22,24,26,28,30},{17..., dimensions={0} | all-to-all | bytes 229376 | tf_op jit(solution)/shard_map/all_to_all | solution.py:600
  66.0 0.8 broadcast_in_dim.7
  66.8 6.4 %all-to-all-start.2 = ((bf16[32,56,128]{2,1,0:T(8,128)(2,1)}), bf16[32,56,128]{2,1,0:T(8,128)(2,1)S(1)}, u32[]{:S(2)}, u32[]{:S(2)}) async-start(bf16[32,56,128]{2,1,0:T(8,128)(2,1)} %broadcast_in_dim.7), calls=%async_computation.2 | async-start | bytes 917504 | tf_op jit(solution)/shard_map/all_to_all | solution.py:602
  73.2 0.0 copy-start.8
  73.3 1.0 %copy-done.8 = bf16[18,48,256]{2,1,0:T(8,128)(2,1)S(1)} copy-done((bf16[18,48,256]{2,1,0:T(8,128)(2,1)S(1)}, bf16[18,48,256]{2,1,0:T(8,128)(2,1)}, u32[]{:S(2)}) %copy-start.8) | copy-done | bytes 442392
  74.3 1.0 %copy-done.10 = bf16[18,48,256]{2,1,0:T(8,128)(2,1)S(1)} copy-done((bf16[18,48,256]{2,1,0:T(8,128)(2,1)S(1)}, bf16[18,48,256]{2,1,0:T(8,128)(2,1)}, u32[]{:S(2)}) %copy-start.10) | copy-done | bytes 442392
  75.3 2.2 %finish.1 = (bf16[16,32,256]{2,1,0:T(8,128)(2,1)}, bf16[16,32,256]{2,1,0:T(8,128)(2,1)}) custom-call(bf16[16,32,256]{2,1,0:T(8,128)(2,1)S(1)} %copy-done, bf16[16,32,256]{2,1,0:T(8,128)(2,1)S(1)} %copy-done.1, bf16[18,48,256]{2,1,0:T(8,128)(2,1)S(1)} %copy-done.8, bf16[18,48,256]{2,1,0:T(8,128)(2,1)S(1)} %copy-done.10, ...), custom_call_target="tpu_custom_call" | custom-call | flops 3000000000 | bytes 10000000 | tf_op jit(solution)/shard_map/finish/pallas_call | solution.py:423
  77.5 6.2 %all-to-all-done.2 = bf16[32,56,128]{2,1,0:T(8,128)(2,1)S(1)} async-done(((bf16[32,56,128]{2,1,0:T(8,128)(2,1)}), bf16[32,56,128]{2,1,0:T(8,128)(2,1)S(1)}, u32[]{:S(2)}, u32[]{:S(2)}) %all-to-all-start.2) | async-done | bytes 458784 | tf_op jit(solution)/shard_map/all_to_all | solution.py:602
  83.6 1.4 %unpack.1 = (f32[27,32,32]{2,1,0:T(8,128)}, f32[4,64,64]{2,1,0:T(8,128)}, f32[27,64,64]{2,1,0:T(8,128)}, f32[4,64,64]{2,1,0:T(8,128)}, f32[27,32,32]{2,1,0:T(8,128)}) custom-call(bf16[1792,128]{1,0:T(8,128)(2,1)S(1)} %bitcast.16), custom_call_target="tpu_custom_call" | custom-call | tf_op jit(solution)/shard_map/unpack/pallas_call | solution.py:501
  (21 shorter events, 0.1 us)
Async XLA Ops:
  0.6 16.5 %copy-start.4 = (bf16[3,3,3,32,32]{4,3,2,1,0:T(8,128)(2,1)S(1)}, bf16[3,3,3,32,32]{4,3,2,1,0:T(8,128)(2,1)}, u32[]{:S(2)}) copy-start(bf16[3,3,3,32,32]{4,3,2,1,0:T(8,128)(2,1)} %param.12) | copy-start | bytes 165892
  0.6 16.5 %copy-start.6 = (bf16[2,2,2,64,32]{3,4,2,1,0:T(8,128)(2,1)S(1)}, bf16[2,2,2,64,32]{3,4,2,1,0:T(8,128)(2,1)}, u32[]{:S(2)}) copy-start(bf16[2,2,2,64,32]{3,4,2,1,0:T(8,128)(2,1)} %param.11) | copy-start | bytes 98308
  0.7 16.5 %copy-start.2 = (bf16[3,3,3,64,64]{4,3,2,1,0:T(8,128)(2,1)S(1)}, bf16[3,3,3,64,64]{4,3,2,1,0:T(8,128)(2,1)}, u32[]{:S(2)}) copy-start(bf16[3,3,3,64,64]{4,3,2,1,0:T(8,128)(2,1)} %param.10) | copy-start | bytes 663556
  0.7 16.5 %copy-start.5 = (bf16[2,2,2,32,64]{4,3,2,1,0:T(8,128)(2,1)S(1)}, bf16[2,2,2,32,64]{4,3,2,1,0:T(8,128)(2,1)}, u32[]{:S(2)}) copy-start(bf16[2,2,2,32,64]{4,3,2,1,0:T(8,128)(2,1)} %param.9) | copy-start | bytes 98308
  0.7 16.5 %copy-start.3 = (bf16[3,3,3,32,32]{4,3,2,1,0:T(8,128)(2,1)S(1)}, bf16[3,3,3,32,32]{4,3,2,1,0:T(8,128)(2,1)}, u32[]{:S(2)}) copy-start(bf16[3,3,3,32,32]{4,3,2,1,0:T(8,128)(2,1)} %param.8) | copy-start | bytes 165892
  2.9 10.1 %collective-permute-start.2 = (bf16[12,16,256]{2,1,0:T(8,128)(2,1)}, bf16[12,16,256]{2,1,0:T(8,128)(2,1)S(1)}, u32[]{:S(2)}, u32[]{:S(2)}) collective-permute-start(bf16[12,16,256]{2,1,0:T(8,128)(2,1)} %get-tuple-element.28), channel_id=1, source_target_pairs={{0,1},{1,2},{2,3},{3,4},{4,5},{5,6},{6,7},{7,8},{8,9},{9,10},{10,1... | collective-permute-start | bytes 294920 | tf_op jit(solution)/shard_map/ppermute | solution.py:566
  5.0 8.0 %collective-permute-start.3 = (bf16[12,16,256]{2,1,0:T(8,128)(2,1)}, bf16[12,16,256]{2,1,0:T(8,128)(2,1)S(1)}, u32[]{:S(2)}, u32[]{:S(2)}) collective-permute-start(bf16[12,16,256]{2,1,0:T(8,128)(2,1)} %get-tuple-element.29), channel_id=1, source_target_pairs={{0,15},{1,0},{2,1},{3,2},{4,3},{5,4},{6,5},{7,6},{8,7},{9,8},{10,9... | collective-permute-start | bytes 294920 | tf_op jit(solution)/shard_map/ppermute | solution.py:567
  10.4 9.5 %collective-permute-start = (bf16[12,32,256]{2,1,0:T(8,128)(2,1)}, bf16[12,32,256]{2,1,0:T(8,128)(2,1)S(1)}, u32[]{:S(2)}, u32[]{:S(2)}) collective-permute-start(bf16[12,32,256]{2,1,0:T(8,128)(2,1)} %get-tuple-element.26), channel_id=1, source_target_pairs={{0,16},{16,32},{32,48},{48,64},{64,80},{80,96},{96,112},{112,128},... | collective-permute-start | bytes 589832 | tf_op jit(solution)/shard_map/ppermute | solution.py:568
  12.5 7.4 %collective-permute-start.1 = (bf16[12,32,256]{2,1,0:T(8,128)(2,1)}, bf16[12,32,256]{2,1,0:T(8,128)(2,1)S(1)}, u32[]{:S(2)}, u32[]{:S(2)}) collective-permute-start(bf16[12,32,256]{2,1,0:T(8,128)(2,1)} %get-tuple-element.27), channel_id=1, source_target_pairs={{0,240},{16,0},{32,16},{48,32},{64,48},{80,64},{96,80},{112,96},{1... | collective-permute-start | bytes 589832 | tf_op jit(solution)/shard_map/ppermute | solution.py:569
  13.1 5.6 %collective-permute-start.4 = (bf16[24,8,256]{2,1,0:T(8,128)(2,1)S(1)}, bf16[24,8,256]{2,1,0:T(8,128)(2,1)S(1)}, u32[]{:S(2)}, u32[]{:S(2)}) collective-permute-start(bf16[24,8,256]{2,1,0:T(8,128)(2,1)S(1)} %pad_maximum_fusion), channel_id=1, source_target_pairs={{0,16},{16,32},{32,48},{48,64},{64,80},{80,96},{96,112},{112,128},... | collective-permute-start | bytes 294920 | tf_op jit(solution)/shard_map/ppermute | solution.py:572
  15.6 4.3 %collective-permute-start.5 = (bf16[24,8,256]{2,1,0:T(8,128)(2,1)S(1)}, bf16[24,8,256]{2,1,0:T(8,128)(2,1)S(1)}, u32[]{:S(2)}, u32[]{:S(2)}) collective-permute-start(bf16[24,8,256]{2,1,0:T(8,128)(2,1)S(1)} %pad_maximum_fusion.1), channel_id=1, source_target_pairs={{0,240},{16,0},{32,16},{48,32},{64,48},{80,64},{96,80},{112,96},{1... | collective-permute-start | bytes 294920 | tf_op jit(solution)/shard_map/ppermute | solution.py:573
  17.2 2.7 %copy-start = (bf16[16,32,256]{2,1,0:T(8,128)(2,1)S(1)}, bf16[16,32,256]{2,1,0:T(8,128)(2,1)}, u32[]{:S(2)}) copy-start(bf16[16,32,256]{2,1,0:T(8,128)(2,1)} %fc.5) | copy-start | bytes 786436
  17.2 2.7 %copy-start.1 = (bf16[16,32,256]{2,1,0:T(8,128)(2,1)S(1)}, bf16[16,32,256]{2,1,0:T(8,128)(2,1)}, u32[]{:S(2)}) copy-start(bf16[16,32,256]{2,1,0:T(8,128)(2,1)} %cc.5) | copy-start | bytes 786436
  31.0 21.7 %copy-start.7 = (bf16[18,48,256]{2,1,0:T(8,128)(2,1)}, bf16[18,48,256]{2,1,0:T(8,128)(2,1)S(1)}, u32[]{:S(2)}) copy-start(bf16[18,48,256]{2,1,0:T(8,128)(2,1)S(1)} %get-tuple-element.35.skip_rows) | copy-start | bytes 1327108
  31.1 21.8 %copy-start.9 = (bf16[18,48,256]{2,1,0:T(8,128)(2,1)}, bf16[18,48,256]{2,1,0:T(8,128)(2,1)S(1)}, u32[]{:S(2)}) copy-start(bf16[18,48,256]{2,1,0:T(8,128)(2,1)S(1)} %get-tuple-element.36.down_rows) | copy-start | bytes 1327108
  66.8 16.8 %all-to-all-start.2 = ((bf16[32,56,128]{2,1,0:T(8,128)(2,1)}), bf16[32,56,128]{2,1,0:T(8,128)(2,1)S(1)}, u32[]{:S(2)}, u32[]{:S(2)}) async-start(bf16[32,56,128]{2,1,0:T(8,128)(2,1)} %broadcast_in_dim.7), calls=%async_computation.2 | async-start | bytes 917504 | tf_op jit(solution)/shard_map/all_to_all | solution.py:602
  73.2 1.0 %copy-start.8 = (bf16[18,48,256]{2,1,0:T(8,128)(2,1)S(1)}, bf16[18,48,256]{2,1,0:T(8,128)(2,1)}, u32[]{:S(2)}) copy-start(bf16[18,48,256]{2,1,0:T(8,128)(2,1)} %copy-done.7) | copy-start | bytes 1327108
  74.3 1.0 %copy-start.10 = (bf16[18,48,256]{2,1,0:T(8,128)(2,1)S(1)}, bf16[18,48,256]{2,1,0:T(8,128)(2,1)}, u32[]{:S(2)}) copy-start(bf16[18,48,256]{2,1,0:T(8,128)(2,1)} %copy-done.9) | copy-start | bytes 1327108

commit v6 on v5

--- a/solution.py
+++ b/solution.py
@@ -213,12 +213,12 @@
 
 
 def main_kernel(
-    fc, cc, xlo, xhi, ylo, yhi, clo, chi, bd, pm, bm, um, bu,
-    terms, skip_rows, down_rows,
+    core, fc, cc, xlo, xhi, ylo, yhi, clo, chi, bd, pm, bm, um, bu,
+    mine, other, skip_rows, down_rows,
     fe, ce, hid, ds_down, skp, dup, ddn,
     v3f, v3c, v3fl, v3s,
     parts, d_parts, co, mid, ds_pool, ds_mid, dmid, v3m, v3dm, v3ml,
-    hi, lo, him, lom, dsc,
+    hi, lo, him, lom, dsc, terms,
 ):
     def gather(dst, count, center, off):
         def put(row, value):
@@ -407,6 +407,17 @@
     rest = terms.shape[0] - TILES * 32
     if rest > 0:
         terms[TILES * 32 :, :] = jnp.zeros((rest, 128), BF)
+    half = terms.shape[0] // 2
+
+    @pl.when(core[0] == 0)
+    def _():
+        mine[...] = terms[0:half, :]
+        other[...] = terms[half:, :]
+
+    @pl.when(core[0] != 0)
+    def _():
+        mine[...] = terms[half:, :]
+        other[...] = terms[0:half, :]
 
 
 def finish_kernel(fc, cc, skip_rows, down_rows, bd, bu, out, gf, v3):
@@ -430,14 +441,17 @@
     )(fields, cot, skip_rows, down_rows, bands[0], bands[4])
 
 
-def main_call(fields, cot, halos, bands, term_rows):
+def main_call(core, fields, cot, halos, bands, term_rows):
+    half = jax.ShapeDtypeStruct((term_rows // 2, 128), BF)
     some = jax.ShapeDtypeStruct((18, EY, W), BF)
     flat = pltpu.VMEM((2, EX * EY, 128), F32)
     split = pltpu.VMEM((2, EX, EY, 128), F32)
     coarse = pltpu.VMEM((CX, CY, W), F32)
     return pl.pallas_call(
         main_kernel,
-        out_shape=(jax.ShapeDtypeStruct((term_rows, 128), BF), some, some),
+        out_shape=(half, half, some, some),
+        in_specs=[pl.BlockSpec(memory_space=pltpu.SMEM)]
+        + [pl.BlockSpec(memory_space=pltpu.VMEM)] * 13,
         scratch_shapes=[flat] * 2
         + [split] * 5
         + [
@@ -460,16 +474,30 @@
             pltpu.VMEM((28 * 64, W), BF),
             pltpu.VMEM((28 * 64, W), BF),
             pltpu.VMEM((W, 3 * W), F32),
+            pltpu.VMEM((term_rows, 128), BF),
         ],
         compiler_params=pltpu.CompilerParams(vmem_limit_bytes=36 * 1024 * 1024),
         cost_estimate=pl.CostEstimate(flops=10**10, bytes_accessed=10**7, transcendentals=10**6),
         name="network",
-    )(fields, cot, *halos, *bands)
+    )(core, fields, cot, *halos, *bands)
 
 
 def unpack_kernel(
-    terms, down, pool, mid, unpool, up, down_v, pool_v, mid_v, unpool_v, up_v, sems
+    core, mine, other, down, pool, mid, unpool, up,
+    down_v, pool_v, mid_v, unpool_v, up_v, terms, sems,
 ):
+    half = mine.shape[0]
+
+    @pl.when(core[0] == 0)
+    def _():
+        terms[0:half, :] = mine[...]
+        terms[half:, :] = other[...]
+
+    @pl.when(core[0] != 0)
+    def _():
+        terms[0:half, :] = other[...]
+        terms[half:, :] = mine[...]
+
     def send(k, src, dst):
         copy = pltpu.make_async_copy(src, dst, sems.at[k])
         copy.start()
@@ -496,17 +524,19 @@
         copy.wait()
 
 
-def unpack(terms):
+def unpack(core, mine, other):
     shapes = ((27, 32, 32), (4, 64, 64), (27, 64, 64), (4, 64, 64), (27, 32, 32))
     return pl.pallas_call(
         unpack_kernel,
         out_shape=tuple(jax.ShapeDtypeStruct(s, F32) for s in shapes),
-        in_specs=[pl.BlockSpec(memory_space=pltpu.VMEM)],
+        in_specs=[pl.BlockSpec(memory_space=pltpu.SMEM)]
+        + [pl.BlockSpec(memory_space=pltpu.VMEM)] * 2,
         out_specs=tuple(pl.BlockSpec(memory_space=pl.ANY) for _ in shapes),
-        scratch_shapes=[pltpu.VMEM(s, F32) for s in shapes] + [pltpu.SemaphoreType.DMA((7,))],
+        scratch_shapes=[pltpu.VMEM(s, F32) for s in shapes]
+        + [pltpu.VMEM((2 * mine.shape[0], 128), BF), pltpu.SemaphoreType.DMA((7,))],
         compiler_params=pltpu.CompilerParams(vmem_limit_bytes=8 * 1024 * 1024),
         name="unpack",
-    )(terms)
+    )(core, mine, other)
 
 
 def ring(axis, step):
@@ -514,7 +544,7 @@
     return [(i, (i + step) % n) for i in range(n)]
 
 
-def pack_kernel(fc, cc, first_x, last_x, first_y, last_y, side, wide, sems):
+def pack_kernel(fc, cc, first_x, last_x, first_y, last_y, side, wide, columns, sems):
     copies = []
 
     def fetch(src, dst):
@@ -531,7 +561,7 @@
     for copy in copies[:4]:
         copy.wait()
     for k, (count, at) in enumerate(((HF, 0), (HC, HF))):
-        for e, (out, first) in enumerate(((first_y, 0), (last_y, 16 - count))):
+        for e, (out, first) in enumerate(((0, 0), (1, 16 - count))):
             for h in range(2):
                 lanes = slice(h * 128, h * 128 + 128)
                 wide[h] = side[2 * k + e, :, :, lanes].reshape(BX * 16, 128).astype(F32)
@@ -539,7 +569,9 @@
                 for h in range(2):
                     lanes = slice(h * 128, h * 128 + 128)
                     column = wide[h, pl.ds(first + c, BX, stride=16), :]
-                    out[at + c, :, lanes] = column.astype(BF)
+                    columns[out, at + c, :, lanes] = column.astype(BF)
+    fetch(columns.at[0], first_y)
+    fetch(columns.at[1], last_y)
     for copy in copies[4:]:
         copy.wait()
 
@@ -551,10 +583,12 @@
         pack_kernel,
         out_shape=(rows, rows, columns, columns),
         in_specs=[pl.BlockSpec(memory_space=pl.ANY)] * 2,
+        out_specs=(pl.BlockSpec(memory_space=pl.ANY),) * 4,
         scratch_shapes=[
             pltpu.VMEM((4, BX, 16, W), BF),
             pltpu.VMEM((2, BX * 16, 128), F32),
-            pltpu.SemaphoreType.DMA((8,)),
+            pltpu.VMEM((2, HF + HC, BX, W), BF),
+            pltpu.SemaphoreType.DMA((10,)),
         ],
         compiler_params=pltpu.CompilerParams(vmem_limit_bytes=56 * 1024 * 1024),
         name="pack",
@@ -576,7 +610,11 @@
 
 def reduce_groups(nx, ny):
     flat = lambda x, y: x * ny + y
-    near = [[flat(x, 2 * z + e) for x in range(nx) for e in range(2)] for z in range(ny // 2)]
+    near = [
+        [flat(x, 2 * z + e) for x in range(c, nx, 2) for e in range(2)]
+        for c in range(2)
+        for z in range(ny // 2)
+    ]
     far = [[flat(x, 2 * z + e) for z in range(ny // 2)] for x in range(nx) for e in range(2)]
     return near, far
 
@@ -585,22 +623,28 @@
     nx, ny = lax.axis_size("gx"), lax.axis_size("gy")
     near, far = reduce_groups(nx, ny)
     n1, n2 = len(near[0]), len(far[0])
-    rows = -(-TILES * 32 // (8 * n1)) * 8
+    rows = -(-TILES * 32 // (16 * n1)) * 8
+    core = (lax.axis_index("gx") % 2).astype(jnp.int32).reshape(1)
+    pairs = [(i, i + 1 - 2 * (i % 2)) for i in range(nx)]
     bands = build_bands(w_down, w_pool, w_mid, w_unpool, w_up)
     halos = exchange(fields, cotangent)
-    terms, skip_rows, down_rows = main_call(fields, cotangent, halos, bands, n1 * rows)
+    mine, other, skip_rows, down_rows = main_call(
+        core, fields, cotangent, halos, bands, 2 * n1 * rows
+    )
     swap = functools.partial(
         lax.all_to_all, axis_name=("gx", "gy"), split_axis=0, concat_axis=0, tiled=True
     )
-    part = swap(terms.reshape(n1, rows, 128), axis_index_groups=near)
-    output, grad_fields = finish_call(fields, cotangent, skip_rows, down_rows, bands)
     cells = fields.shape[0] * fields.shape[1] * 8 * nx * ny
     root = 1.0 / math.sqrt(math.sqrt(cells))
+    part = mine.astype(F32) + lax.ppermute(other, "gx", pairs).astype(F32)
+    part = swap(part.astype(BF).reshape(n1, rows, 128), axis_index_groups=near)
+    output, grad_fields = finish_call(fields, cotangent, skip_rows, down_rows, bands)
     part = (jnp.sum(part.astype(F32), axis=0) * root).astype(BF)
     part = swap(jnp.broadcast_to(part, (n2, rows, 128)), axis_index_groups=far).astype(F32)
     part = (jnp.sum(part, axis=0) * root).astype(BF)
-    whole = swap(jnp.broadcast_to(part, (n1, rows, 128)), axis_index_groups=near)
-    down, pool, mid, unpool, up = unpack(whole.reshape(n1 * rows, 128))
+    part = swap(jnp.broadcast_to(part, (n1, rows, 128)), axis_index_groups=near)
+    part = part.reshape(n1 * rows, 128)
+    down, pool, mid, unpool, up = unpack(core, part, lax.ppermute(part, "gx", pairs))
     return (
         output,
         grad_fields,

time: 85.6 us -> 94 us (1.098)
  Pallas kernels: 18.4 us -> 29.3 us
  waiting for transfers between devices: 7.89 us -> 2.86 us
  blocking collectives: 34.8 us -> 37.8 us
  local copies, waits for them, and re-layouts: 2.93 us -> 0.1 us
  starting transfers between devices: 20.1 us -> 22.6 us
    pallas_call x1, Pallas kernels: 2.22 us -> 13.1 us  [pack(): pl.pallas_call(pack_kernel, out_shape=(rows, rows, columns, columns), in_...]
    ppermute x0 -> x2, starting transfers between devices: none -> 8.89 us  [the longest x1 4.87 us: per_device(): part = mine.astype(F32) + lax.ppermute(other, 'gx', pairs).astype(F32)]
    all_to_all x1 -> x0, starting transfers between devices: 6.4 us -> none  [per_device(): swap(jnp.broadcast_to(part, (n1, rows, 128)), axis_index_groups=near)]
    all_to_all x1 -> x0, waiting for transfers between devices: 6.15 us -> none  [per_device(): swap(jnp.broadcast_to(part, (n1, rows, 128)), axis_index_groups=near)]
    all_to_all x1 -> x2, blocking collectives: 21.7 us -> 24.8 us  [the longest x1 14.5 us: per_device(): part = swap(part.astype(BF).reshape(n1, rows, 128), axis_index_groups=near)]
    unnamed x22 -> x14, local copies, waits for them, and re-layouts: 2.07 us -> 0.03 us
    ppermute x0 -> x2, waiting for transfers between devices: none -> 1.12 us  [the longest x1 1.12 us: per_device(): part = mine.astype(F32) + lax.ppermute(other, 'gx', pairs).astype(F32)]
  transfers between devices with their start and end apart: 7 -> 8, of which waited for: 3 -> 3; matrix products, arithmetic and copies ran while one was open for 0% -> 0% of each run, Pallas kernels for 4% -> 4%
where the time goes in v6:
time: 94 us; the launch traced here: 93.8 us
  blocking collectives  37.8 us (40%)
  Pallas kernels  29.3 us (31%)
  starting transfers between devices  22.6 us (24%)
  waiting for transfers between devices  2.86 us (3%)
  between operations  0.98 us (1%)
    all_to_all x1, blocking collectives, per_device(): part = swap(part.astype(BF).reshape(n1, rows, 128), axis_index_groups=near)  14.5 us
    pallas_call x1, Pallas kernels, pack(): pl.pallas_call(pack_kernel, out_shape=(rows, rows, columns, columns), in_...  13.1 us
    all_to_all x1, blocking collectives, per_device(): swap(jnp.broadcast_to(part, (n2, rows, 128)), axis_index_groups=far)  13.1 us
    pallas_call x1, Pallas kernels, main_call(): pl.pallas_call(main_kernel, out_shape=(half, half, some, some), in_specs=...  11.1 us
    all_to_all x1, blocking collectives, per_device(): part = swap(jnp.broadcast_to(part, (n1, rows, 128)), axis_index_groups=near)  10.3 us
    ppermute x1, starting transfers between devices, exchange(): yhi = lax.ppermute(first_y, 'gy', ring('gy', -1))  5.38 us
    ppermute x1, starting transfers between devices, per_device(): part = mine.astype(F32) + lax.ppermute(other, 'gx', pairs).astype(F32)  4.87 us
    ppermute x1, starting transfers between devices, per_device(): lax.ppermute(part, 'gx', pairs)  4.02 us
  transfers between devices with their start and end apart: 8, of which 3 were waited for; matrix products, arithmetic and copies ran while one was open for 0% of the time, Pallas kernels for 4%

profile of v6, /device:TPU:1, one launch (start us, length us, event | category | flops | bytes accessed | tf_op | source)
XLA Modules:
  0.0 93.8 jit_solution(4462989739330672893)
XLA Ops:
  0.6 0.0 copy-start.4
  0.6 0.0 copy-start.6
  0.7 0.0 copy-start.2
  0.7 0.0 copy-start.5
  0.7 13.1 %pack.1 = (bf16[12,32,256]{2,1,0:T(8,128)(2,1)}, bf16[12,32,256]{2,1,0:T(8,128)(2,1)}, bf16[12,16,256]{2,1,0:T(8,128)(2,1)}, bf16[12,16,256]{2,1,0:T(8,128)(2,1)}) custom-call(bf16[16,32,256]{2,1,0:T(8,128)(2,1)} %fc.5, bf16[16,32,256]{2,1,0:T(8,128)(2,1)} %cc.5), custom_call_target="tpu_custom_call" | custom-call | tf_op jit(solution)/shard_map/pack/pallas_call | solution.py:582
  13.8 2.1 %collective-permute-start.2 = (bf16[12,16,256]{2,1,0:T(8,128)(2,1)}, bf16[12,16,256]{2,1,0:T(8,128)(2,1)S(1)}, u32[]{:S(2)}, u32[]{:S(2)}) collective-permute-start(bf16[12,16,256]{2,1,0:T(8,128)(2,1)} %get-tuple-element.29), channel_id=1, source_target_pairs={{0,1},{1,2},{2,3},{3,4},{4,5},{5,6},{6,7},{7,8},{8,9},{9,10},{10,1... | collective-permute-start | bytes 294920 | tf_op jit(solution)/shard_map/ppermute | solution.py:600
  15.9 5.4 %collective-permute-start.3 = (bf16[12,16,256]{2,1,0:T(8,128)(2,1)}, bf16[12,16,256]{2,1,0:T(8,128)(2,1)S(1)}, u32[]{:S(2)}, u32[]{:S(2)}) collective-permute-start(bf16[12,16,256]{2,1,0:T(8,128)(2,1)} %get-tuple-element.30), channel_id=1, source_target_pairs={{0,15},{1,0},{2,1},{3,2},{4,3},{5,4},{6,5},{7,6},{8,7},{9,8},{10,9... | collective-permute-start | bytes 294920 | tf_op jit(solution)/shard_map/ppermute | solution.py:601
  21.3 2.1 %collective-permute-start = (bf16[12,32,256]{2,1,0:T(8,128)(2,1)}, bf16[12,32,256]{2,1,0:T(8,128)(2,1)S(1)}, u32[]{:S(2)}, u32[]{:S(2)}) collective-permute-start(bf16[12,32,256]{2,1,0:T(8,128)(2,1)} %get-tuple-element.27), channel_id=1, source_target_pairs={{0,16},{16,32},{32,48},{48,64},{64,80},{80,96},{96,112},{112,128},... | collective-permute-start | bytes 589832 | tf_op jit(solution)/shard_map/ppermute | solution.py:602
  23.4 0.0 collective-permute-start.1
  23.4 0.5 collective-permute-done.2.ylo
  24.0 0.0 collective-permute-done.3.yhi
  24.0 2.5 %collective-permute-start.4 = (bf16[24,8,256]{2,1,0:T(8,128)(2,1)S(1)}, bf16[24,8,256]{2,1,0:T(8,128)(2,1)S(1)}, u32[]{:S(2)}, u32[]{:S(2)}) collective-permute-start(bf16[24,8,256]{2,1,0:T(8,128)(2,1)S(1)} %pad_maximum_fusion), channel_id=1, source_target_pairs={{0,16},{16,32},{32,48},{48,64},{64,80},{80,96},{96,112},{112,128},... | collective-permute-start | bytes 294920 | tf_op jit(solution)/shard_map/ppermute | solution.py:606
  26.5 1.5 %collective-permute-start.5 = (bf16[24,8,256]{2,1,0:T(8,128)(2,1)S(1)}, bf16[24,8,256]{2,1,0:T(8,128)(2,1)S(1)}, u32[]{:S(2)}, u32[]{:S(2)}) collective-permute-start(bf16[24,8,256]{2,1,0:T(8,128)(2,1)S(1)} %pad_maximum_fusion.1), channel_id=1, source_target_pairs={{0,240},{16,0},{32,16},{48,32},{64,48},{80,64},{96,80},{112,96},{1... | collective-permute-start | bytes 294920 | tf_op jit(solution)/shard_map/ppermute | solution.py:607
  28.1 0.0 copy-done.5
  28.1 0.0 copy-start
  28.1 0.0 copy-start.1
  28.1 1.5 %bands.1 = (bf16[2304,256]{1,0:T(8,128)(2,1)S(1)}, bf16[1024,256]{1,0:T(8,128)(2,1)S(1)}, bf16[2304,256]{1,0:T(8,128)(2,1)S(1)}, bf16[1024,256]{1,0:T(8,128)(2,1)S(1)}, bf16[2304,256]{1,0:T(8,128)(2,1)S(1)}) custom-call(bf16[864,32]{1,0:T(8,128)(2,1)S(1)} %bitcast.20, bf16[4,64,64]{2,1,0:T(8,128)(2,1)S(1)} %bitcast.22, bf16[1728,64]{1,0:T(8,128)(2,1)S(1)} %bitcast.19, ...), custom_call_target="tpu_custom_call" | custom-call | flops 2000000000 | bytes 8000000 | tf_op jit(solution)/shard_map/bands/pallas_call | solution.py:102
  29.6 0.0 collective-permute-done.4.clo
  29.6 1.2 %collective-permute-done.5.chi = bf16[24,8,256]{2,1,0:T(8,128)(2,1)S(1)} collective-permute-done((bf16[24,8,256]{2,1,0:T(8,128)(2,1)S(1)}, bf16[24,8,256]{2,1,0:T(8,128)(2,1)S(1)}, u32[]{:S(2)}, u32[]{:S(2)}) %collective-permute-start.5) | collective-permute-done | bytes 98336 | tf_op jit(solution)/shard_map/ppermute | solution.py:607
  30.8 0.0 collective-permute-done.xlo
  30.8 0.0 collective-permute-done.1.xhi
  30.8 11.1 %network.1 = (bf16[896,128]{1,0:T(8,128)(2,1)S(1)}, bf16[896,128]{1,0:T(8,128)(2,1)S(1)}, bf16[18,48,256]{2,1,0:T(8,128)(2,1)S(1)}, bf16[18,48,256]{2,1,0:T(8,128)(2,1)S(1)}) custom-call(s32[1]{0:T(128)} %bitcast.core, bf16[16,32,256]{2,1,0:T(8,128)(2,1)S(1)} %copy-done, bf16[16,32,256]{2,1,0:T(8,128)(2,1)S(1)} %copy-done.1, ...), custom_call_target="tpu_custom_call" | custom-call | flops 10000000000 | bytes 10000000 | tf_op jit(solution)/shard_map/network/pallas_call | solution.py:450
  42.0 4.9 %collective-permute-start.6 = (bf16[896,128]{1,0:T(8,128)(2,1)S(1)}, bf16[896,128]{1,0:T(8,128)(2,1)S(1)}, u32[]{:S(2)}, u32[]{:S(2)}) collective-permute-start(bf16[896,128]{1,0:T(8,128)(2,1)S(1)} %get-tuple-element.41), channel_id=1, source_target_pairs={{0,16},{16,0},{32,48},{48,32},{64,80},{80,64},{96,112},{112,96},{1... | collective-permute-start | bytes 688136 | tf_op jit(solution)/shard_map/ppermute | solution.py:639
  46.8 1.1 %collective-permute-done.6 = bf16[896,128]{1,0:T(8,128)(2,1)S(1)} collective-permute-done((bf16[896,128]{1,0:T(8,128)(2,1)S(1)}, bf16[896,128]{1,0:T(8,128)(2,1)S(1)}, u32[]{:S(2)}, u32[]{:S(2)}) %collective-permute-start.6) | collective-permute-done | bytes 229408 | tf_op jit(solution)/shard_map/ppermute | solution.py:639
  48.0 0.1 add_convert_fusion
  48.0 14.5 %all_to_all.15 = bf16[16,56,128]{2,1,0:T(8,128)(2,1)S(1)} all-to-all(bf16[16,56,128]{2,1,0:T(8,128)(2,1)S(1)} %bitcast.24), channel_id=1, replica_groups={{0,1,32,33,64,65,96,97,128,129,160,161,192,193,224,225},{2,3,34,35,66,6..., dimensions={0} | all-to-all | bytes 458752 | tf_op jit(solution)/shard_map/all_to_all | solution.py:640
  62.6 13.1 %all_to_all.16 = bf16[8,56,128]{2,1,0:T(8,128)(2,1)S(1)} all-to-all(bf16[8,56,128]{2,1,0:T(8,128)(2,1)S(1)} %broadcast_in_dim.6), channel_id=1, replica_groups={{0,2,4,6,8,10,12,14},{1,3,5,7,9,11,13,15},{16,18,20,22,24,26,28,30},{17..., dimensions={0} | all-to-all | bytes 229376 | tf_op jit(solution)/shard_map/all_to_all | solution.py:643
  75.7 10.3 %all_to_all.17 = bf16[16,56,128]{2,1,0:T(8,128)(2,1)S(1)} all-to-all(bf16[16,56,128]{2,1,0:T(8,128)(2,1)S(1)} %broadcast_in_dim.7), channel_id=1, replica_groups={{0,1,32,33,64,65,96,97,128,129,160,161,192,193,224,225},{2,3,34,35,66,6..., dimensions={0} | all-to-all | bytes 458752 | tf_op jit(solution)/shard_map/all_to_all | solution.py:645
  86.0 4.0 %collective-permute-start.7 = (bf16[896,128]{1,0:T(8,128)(2,1)S(1)}, bf16[896,128]{1,0:T(8,128)(2,1)S(1)}, u32[]{:S(2)}, u32[]{:S(2)}) collective-permute-start(bf16[896,128]{1,0:T(8,128)(2,1)S(1)} %bitcast.17), channel_id=1, source_target_pairs={{0,16},{16,0},{32,48},{48,32},{64,80},{80,64},{96,112},{112,96},{1... | collective-permute-start | bytes 688136 | tf_op jit(solution)/shard_map/ppermute | solution.py:647
  90.0 2.2 %finish.1 = (bf16[16,32,256]{2,1,0:T(8,128)(2,1)}, bf16[16,32,256]{2,1,0:T(8,128)(2,1)}) custom-call(bf16[16,32,256]{2,1,0:T(8,128)(2,1)S(1)} %copy-done, bf16[16,32,256]{2,1,0:T(8,128)(2,1)S(1)} %copy-done.1, bf16[18,48,256]{2,1,0:T(8,128)(2,1)S(1)} %get-tuple-element.36.skip_rows, bf16[18,48,256]{2,1,0:T(8,128)(2,1)S(1)} %get-tuple-element.37.down_rows, ...), custom_call_target="tpu_custom_call" | custom-call | flops 3000000000 | bytes 10000000 | tf_op jit(solution)/shard_map/finish/pallas_call | solution.py:434
  92.2 0.0 collective-permute-done.7.other
  92.2 1.5 %unpack.1 = (f32[27,32,32]{2,1,0:T(8,128)}, f32[4,64,64]{2,1,0:T(8,128)}, f32[27,64,64]{2,1,0:T(8,128)}, f32[4,64,64]{2,1,0:T(8,128)}, f32[27,32,32]{2,1,0:T(8,128)}) custom-call(s32[1]{0:T(128)} %bitcast.core, bf16[896,128]{1,0:T(8,128)(2,1)S(1)} %bitcast.18, bf16[896,128]{1,0:T(8,128)(2,1)S(1)} %collective-permute-done.7.other), custom_call_target="tpu_custom_call" | custom-call | tf_op jit(solution)/shard_map/unpack/pallas_call | solution.py:529
  (17 shorter events, 0.2 us)
Async XLA Ops:
  0.6 27.4 %copy-start.4 = (bf16[3,3,3,32,32]{4,3,2,1,0:T(8,128)(2,1)S(1)}, bf16[3,3,3,32,32]{4,3,2,1,0:T(8,128)(2,1)}, u32[]{:S(2)}) copy-start(bf16[3,3,3,32,32]{4,3,2,1,0:T(8,128)(2,1)} %param.12) | copy-start | bytes 165892
  0.6 27.4 %copy-start.6 = (bf16[2,2,2,64,32]{3,4,2,1,0:T(8,128)(2,1)S(1)}, bf16[2,2,2,64,32]{3,4,2,1,0:T(8,128)(2,1)}, u32[]{:S(2)}) copy-start(bf16[2,2,2,64,32]{3,4,2,1,0:T(8,128)(2,1)} %param.11) | copy-start | bytes 98308
  0.7 27.4 %copy-start.2 = (bf16[3,3,3,64,64]{4,3,2,1,0:T(8,128)(2,1)S(1)}, bf16[3,3,3,64,64]{4,3,2,1,0:T(8,128)(2,1)}, u32[]{:S(2)}) copy-start(bf16[3,3,3,64,64]{4,3,2,1,0:T(8,128)(2,1)} %param.10) | copy-start | bytes 663556
  0.7 27.4 %copy-start.5 = (bf16[2,2,2,32,64]{4,3,2,1,0:T(8,128)(2,1)S(1)}, bf16[2,2,2,32,64]{4,3,2,1,0:T(8,128)(2,1)}, u32[]{:S(2)}) copy-start(bf16[2,2,2,32,64]{4,3,2,1,0:T(8,128)(2,1)} %param.9) | copy-start | bytes 98308
  0.7 27.4 %copy-start.3 = (bf16[3,3,3,32,32]{4,3,2,1,0:T(8,128)(2,1)S(1)}, bf16[3,3,3,32,32]{4,3,2,1,0:T(8,128)(2,1)}, u32[]{:S(2)}) copy-start(bf16[3,3,3,32,32]{4,3,2,1,0:T(8,128)(2,1)} %param.8) | copy-start | bytes 165892
  13.8 10.1 %collective-permute-start.2 = (bf16[12,16,256]{2,1,0:T(8,128)(2,1)}, bf16[12,16,256]{2,1,0:T(8,128)(2,1)S(1)}, u32[]{:S(2)}, u32[]{:S(2)}) collective-permute-start(bf16[12,16,256]{2,1,0:T(8,128)(2,1)} %get-tuple-element.29), channel_id=1, source_target_pairs={{0,1},{1,2},{2,3},{3,4},{4,5},{5,6},{6,7},{7,8},{8,9},{9,10},{10,1... | collective-permute-start | bytes 294920 | tf_op jit(solution)/shard_map/ppermute | solution.py:600
  15.9 8.0 %collective-permute-start.3 = (bf16[12,16,256]{2,1,0:T(8,128)(2,1)}, bf16[12,16,256]{2,1,0:T(8,128)(2,1)S(1)}, u32[]{:S(2)}, u32[]{:S(2)}) collective-permute-start(bf16[12,16,256]{2,1,0:T(8,128)(2,1)} %get-tuple-element.30), channel_id=1, source_target_pairs={{0,15},{1,0},{2,1},{3,2},{4,3},{5,4},{6,5},{7,6},{8,7},{9,8},{10,9... | collective-permute-start | bytes 294920 | tf_op jit(solution)/shard_map/ppermute | solution.py:601
  21.3 9.5 %collective-permute-start = (bf16[12,32,256]{2,1,0:T(8,128)(2,1)}, bf16[12,32,256]{2,1,0:T(8,128)(2,1)S(1)}, u32[]{:S(2)}, u32[]{:S(2)}) collective-permute-start(bf16[12,32,256]{2,1,0:T(8,128)(2,1)} %get-tuple-element.27), channel_id=1, source_target_pairs={{0,16},{16,32},{32,48},{48,64},{64,80},{80,96},{96,112},{112,128},... | collective-permute-start | bytes 589832 | tf_op jit(solution)/shard_map/ppermute | solution.py:602
  23.4 7.4 %collective-permute-start.1 = (bf16[12,32,256]{2,1,0:T(8,128)(2,1)}, bf16[12,32,256]{2,1,0:T(8,128)(2,1)S(1)}, u32[]{:S(2)}, u32[]{:S(2)}) collective-permute-start(bf16[12,32,256]{2,1,0:T(8,128)(2,1)} %get-tuple-element.28), channel_id=1, source_target_pairs={{0,240},{16,0},{32,16},{48,32},{64,48},{80,64},{96,80},{112,96},{1... | collective-permute-start | bytes 589832 | tf_op jit(solution)/shard_map/ppermute | solution.py:603
  24.0 5.6 %collective-permute-start.4 = (bf16[24,8,256]{2,1,0:T(8,128)(2,1)S(1)}, bf16[24,8,256]{2,1,0:T(8,128)(2,1)S(1)}, u32[]{:S(2)}, u32[]{:S(2)}) collective-permute-start(bf16[24,8,256]{2,1,0:T(8,128)(2,1)S(1)} %pad_maximum_fusion), channel_id=1, source_target_pairs={{0,16},{16,32},{32,48},{48,64},{64,80},{80,96},{96,112},{112,128},... | collective-permute-start | bytes 294920 | tf_op jit(solution)/shard_map/ppermute | solution.py:606
  26.5 4.3 %collective-permute-start.5 = (bf16[24,8,256]{2,1,0:T(8,128)(2,1)S(1)}, bf16[24,8,256]{2,1,0:T(8,128)(2,1)S(1)}, u32[]{:S(2)}, u32[]{:S(2)}) collective-permute-start(bf16[24,8,256]{2,1,0:T(8,128)(2,1)S(1)} %pad_maximum_fusion.1), channel_id=1, source_target_pairs={{0,240},{16,0},{32,16},{48,32},{64,48},{80,64},{96,80},{112,96},{1... | collective-permute-start | bytes 294920 | tf_op jit(solution)/shard_map/ppermute | solution.py:607
  28.1 2.7 %copy-start = (bf16[16,32,256]{2,1,0:T(8,128)(2,1)S(1)}, bf16[16,32,256]{2,1,0:T(8,128)(2,1)}, u32[]{:S(2)}) copy-start(bf16[16,32,256]{2,1,0:T(8,128)(2,1)} %fc.5) | copy-start | bytes 786436
  28.1 2.7 %copy-start.1 = (bf16[16,32,256]{2,1,0:T(8,128)(2,1)S(1)}, bf16[16,32,256]{2,1,0:T(8,128)(2,1)}, u32[]{:S(2)}) copy-start(bf16[16,32,256]{2,1,0:T(8,128)(2,1)} %cc.5) | copy-start | bytes 786436
  42.0 6.0 %collective-permute-start.6 = (bf16[896,128]{1,0:T(8,128)(2,1)S(1)}, bf16[896,128]{1,0:T(8,128)(2,1)S(1)}, u32[]{:S(2)}, u32[]{:S(2)}) collective-permute-start(bf16[896,128]{1,0:T(8,128)(2,1)S(1)} %get-tuple-element.41), channel_id=1, source_target_pairs={{0,16},{16,0},{32,48},{48,32},{64,80},{80,64},{96,112},{112,96},{1... | collective-permute-start | bytes 688136 | tf_op jit(solution)/shard_map/ppermute | solution.py:639
  86.0 6.2 %collective-permute-start.7 = (bf16[896,128]{1,0:T(8,128)(2,1)S(1)}, bf16[896,128]{1,0:T(8,128)(2,1)S(1)}, u32[]{:S(2)}, u32[]{:S(2)}) collective-permute-start(bf16[896,128]{1,0:T(8,128)(2,1)S(1)} %bitcast.17), channel_id=1, source_target_pairs={{0,16},{16,0},{32,48},{48,32},{64,80},{80,64},{96,112},{112,96},{1... | collective-permute-start | bytes 688136 | tf_op jit(solution)/shard_map/ppermute | solution.py:647

commit v7 on v6

--- a/solution.py
+++ b/solution.py
@@ -420,25 +420,21 @@
         other[...] = terms[0:half, :]
 
 
-def finish_kernel(fc, cc, skip_rows, down_rows, bd, bu, out, gf, v3):
-    loop(18, lambda i: taps_to_lanes(skip_rows, i, v3, i, 8, BY))
-    total = conv_rows(v3, 0, BX, bu).reshape(BX, BY, W)
-    out[...] = (fc[...].astype(F32) + total).astype(BF)
-    loop(18, lambda i: taps_to_lanes(down_rows, i, v3, i, 8, BY))
-    total = conv_t_rows(v3, 0, BX, bd).reshape(BX, BY, W)
-    gf[...] = (cc[...].astype(F32) + total).astype(BF)
-
-
-def finish_call(fields, cot, skip_rows, down_rows, bands):
-    block = jax.ShapeDtypeStruct((BX, BY, W), BF)
+def finish_kernel(conv, base, rows, band, out, v3):
+    loop(18, lambda i: taps_to_lanes(rows, i, v3, i, 8, BY))
+    total = conv(v3, 0, BX, band).reshape(BX, BY, W)
+    out[...] = (base[...].astype(F32) + total).astype(BF)
+
+
+def finish_call(conv, base, rows, band):
     return pl.pallas_call(
-        finish_kernel,
-        out_shape=(block, block),
+        functools.partial(finish_kernel, conv),
+        out_shape=jax.ShapeDtypeStruct((BX, BY, W), BF),
         scratch_shapes=[pltpu.VMEM((18, BY, 3 * W), BF)],
         compiler_params=pltpu.CompilerParams(vmem_limit_bytes=16 * 1024 * 1024),
-        cost_estimate=pl.CostEstimate(flops=3 * 10**9, bytes_accessed=10**7, transcendentals=0),
+        cost_estimate=pl.CostEstimate(flops=10**9, bytes_accessed=10**6, transcendentals=0),
         name="finish",
-    )(fields, cot, skip_rows, down_rows, bands[0], bands[4])
+    )(base, rows, band)
 
 
 def main_call(core, fields, cot, halos, bands, term_rows):
@@ -544,7 +540,7 @@
     return [(i, (i + step) % n) for i in range(n)]
 
 
-def pack_kernel(fc, cc, first_x, last_x, first_y, last_y, side, wide, columns, sems):
+def pack_kernel(fc, cc, first_x, last_x, first_y, last_y, side, wide, rows, columns, sems):
     copies = []
 
     def fetch(src, dst):
@@ -556,10 +552,12 @@
         fetch(src.at[:, 0:16], side.at[2 * k])
         fetch(src.at[:, BY - 16 : BY], side.at[2 * k + 1])
     for src, count, at in ((fc, HF, 0), (cc, HC, HF)):
-        fetch(src.at[0:count], first_x.at[at : at + count])
-        fetch(src.at[BX - count : BX], last_x.at[at : at + count])
-    for copy in copies[:4]:
+        fetch(src.at[0:count], rows.at[0, at : at + count])
+        fetch(src.at[BX - count : BX], rows.at[1, at : at + count])
+    for copy in copies:
         copy.wait()
+    fetch(rows.at[0], first_x)
+    fetch(rows.at[1], last_x)
     for k, (count, at) in enumerate(((HF, 0), (HC, HF))):
         for e, (out, first) in enumerate(((0, 0), (1, 16 - count))):
             for h in range(2):
@@ -572,7 +570,7 @@
                     columns[out, at + c, :, lanes] = column.astype(BF)
     fetch(columns.at[0], first_y)
     fetch(columns.at[1], last_y)
-    for copy in copies[4:]:
+    for copy in copies[8:]:
         copy.wait()
 
 
@@ -587,8 +585,9 @@
         scratch_shapes=[
             pltpu.VMEM((4, BX, 16, W), BF),
             pltpu.VMEM((2, BX * 16, 128), F32),
+            pltpu.VMEM((2, HF + HC, BY, W), BF),
             pltpu.VMEM((2, HF + HC, BX, W), BF),
-            pltpu.SemaphoreType.DMA((10,)),
+            pltpu.SemaphoreType.DMA((12,)),
         ],
         compiler_params=pltpu.CompilerParams(vmem_limit_bytes=56 * 1024 * 1024),
         name="pack",
@@ -636,15 +635,19 @@
     )
     cells = fields.shape[0] * fields.shape[1] * 8 * nx * ny
     root = 1.0 / math.sqrt(math.sqrt(cells))
-    part = mine.astype(F32) + lax.ppermute(other, "gx", pairs).astype(F32)
+    theirs = lax.ppermute(other, "gx", pairs)
+    output = finish_call(conv_rows, fields, skip_rows, bands[4])
+    theirs, output = lax.optimization_barrier((theirs, output))
+    part = mine.astype(F32) + theirs.astype(F32)
     part = swap(part.astype(BF).reshape(n1, rows, 128), axis_index_groups=near)
-    output, grad_fields = finish_call(fields, cotangent, skip_rows, down_rows, bands)
     part = (jnp.sum(part.astype(F32), axis=0) * root).astype(BF)
     part = swap(jnp.broadcast_to(part, (n2, rows, 128)), axis_index_groups=far).astype(F32)
     part = (jnp.sum(part, axis=0) * root).astype(BF)
     part = swap(jnp.broadcast_to(part, (n1, rows, 128)), axis_index_groups=near)
     part = part.reshape(n1 * rows, 128)
-    down, pool, mid, unpool, up = unpack(core, part, lax.ppermute(part, "gx", pairs))
+    theirs = lax.ppermute(part, "gx", pairs)
+    grad_fields = finish_call(conv_t_rows, cotangent, down_rows, bands[0])
+    down, pool, mid, unpool, up = unpack(core, part, theirs)
     return (
         output,
         grad_fields,

time: 94 us -> 82.6 us (0.88)
  Pallas kernels: 29.3 us -> 19.3 us
  waiting for transfers between devices: 2.86 us -> 1.74 us
    pallas_call x1, Pallas kernels: 13.1 us -> 2.26 us  [pack(): pl.pallas_call(pack_kernel, out_shape=(rows, rows, columns, columns), in_...]
    ppermute x2, waiting for transfers between devices: 1.12 us -> 0.01 us  [the longest x1 0.01 us: per_device(): theirs = lax.ppermute(other, 'gx', pairs)]
    pallas_call x1 -> x2, Pallas kernels: 2.18 us -> 3.01 us  [finish_call(): pl.pallas_call(functools.partial(finish_kernel, conv), out_shape=jax.Shap...]
  transfers between devices with their start and end apart: 8 -> 8, of which waited for: 3 -> 2; matrix products, arithmetic and copies ran while one was open for 0% -> 0% of each run, Pallas kernels for 4% -> 5%
where the time goes in v7:
time: 82.6 us; the launch traced here: 82.3 us
  blocking collectives  37.1 us (45%)
  starting transfers between devices  23 us (28%)
  Pallas kernels  19.3 us (23%)
  waiting for transfers between devices  1.74 us (2%)
  between operations  0.98 us (1%)
    all_to_all x1, blocking collectives, per_device(): part = swap(part.astype(BF).reshape(n1, rows, 128), axis_index_groups=near)  13.7 us
    all_to_all x1, blocking collectives, per_device(): swap(jnp.broadcast_to(part, (n2, rows, 128)), axis_index_groups=far)  13.2 us
    pallas_call x1, Pallas kernels, main_call(): pl.pallas_call(main_kernel, out_shape=(half, half, some, some), in_specs=...  11.1 us
    all_to_all x1, blocking collectives, per_device(): part = swap(jnp.broadcast_to(part, (n1, rows, 128)), axis_index_groups=near)  10.2 us
    ppermute x1, starting transfers between devices, exchange(): yhi = lax.ppermute(first_y, 'gy', ring('gy', -1))  5.38 us
    ppermute x1, starting transfers between devices, per_device(): theirs = lax.ppermute(other, 'gx', pairs)  4.89 us
    ppermute x1, starting transfers between devices, per_device(): theirs = lax.ppermute(part, 'gx', pairs)  4.39 us
    pallas_call x2, Pallas kernels, finish_call(): pl.pallas_call(functools.partial(finish_kernel, conv), out_shape=jax.Shap...  3.01 us
  transfers between devices with their start and end apart: 8, of which 2 were waited for; matrix products, arithmetic and copies ran while one was open for 0% of the time, Pallas kernels for 5%

profile of v7, /device:TPU:1, one launch (start us, length us, event | category | flops | bytes accessed | tf_op | source)
XLA Modules:
  0.0 82.3 jit_solution(2586472008480095252)
XLA Ops:
  0.6 0.0 copy-start.4
  0.6 0.0 copy-start.6
  0.7 2.3 %pack.1 = (bf16[12,32,256]{2,1,0:T(8,128)(2,1)}, bf16[12,32,256]{2,1,0:T(8,128)(2,1)}, bf16[12,16,256]{2,1,0:T(8,128)(2,1)}, bf16[12,16,256]{2,1,0:T(8,128)(2,1)}) custom-call(bf16[16,32,256]{2,1,0:T(8,128)(2,1)} %base.2, bf16[16,32,256]{2,1,0:T(8,128)(2,1)} %base.3), custom_call_target="tpu_custom_call" | custom-call | tf_op jit(solution)/shard_map/pack/pallas_call | solution.py:580
  2.9 2.1 %collective-permute-start.2 = (bf16[12,16,256]{2,1,0:T(8,128)(2,1)}, bf16[12,16,256]{2,1,0:T(8,128)(2,1)S(1)}, u32[]{:S(2)}, u32[]{:S(2)}) collective-permute-start(bf16[12,16,256]{2,1,0:T(8,128)(2,1)} %get-tuple-element.29), channel_id=1, source_target_pairs={{0,1},{1,2},{2,3},{3,4},{4,5},{5,6},{6,7},{7,8},{8,9},{9,10},{10,1... | collective-permute-start | bytes 294920 | tf_op jit(solution)/shard_map/ppermute | solution.py:599
  5.1 5.4 %collective-permute-start.3 = (bf16[12,16,256]{2,1,0:T(8,128)(2,1)}, bf16[12,16,256]{2,1,0:T(8,128)(2,1)S(1)}, u32[]{:S(2)}, u32[]{:S(2)}) collective-permute-start(bf16[12,16,256]{2,1,0:T(8,128)(2,1)} %get-tuple-element.30), channel_id=1, source_target_pairs={{0,15},{1,0},{2,1},{3,2},{4,3},{5,4},{6,5},{7,6},{8,7},{9,8},{10,9... | collective-permute-start | bytes 294920 | tf_op jit(solution)/shard_map/ppermute | solution.py:600
  10.4 2.1 %collective-permute-start = (bf16[12,32,256]{2,1,0:T(8,128)(2,1)}, bf16[12,32,256]{2,1,0:T(8,128)(2,1)S(1)}, u32[]{:S(2)}, u32[]{:S(2)}) collective-permute-start(bf16[12,32,256]{2,1,0:T(8,128)(2,1)} %get-tuple-element.27), channel_id=1, source_target_pairs={{0,16},{16,32},{32,48},{48,64},{64,80},{80,96},{96,112},{112,128},... | collective-permute-start | bytes 589832 | tf_op jit(solution)/shard_map/ppermute | solution.py:601
  12.6 0.0 collective-permute-start.1
  12.6 0.5 collective-permute-done.2.ylo
  13.1 0.0 collective-permute-done.3.yhi
  13.1 2.5 %collective-permute-start.4 = (bf16[24,8,256]{2,1,0:T(8,128)(2,1)S(1)}, bf16[24,8,256]{2,1,0:T(8,128)(2,1)S(1)}, u32[]{:S(2)}, u32[]{:S(2)}) collective-permute-start(bf16[24,8,256]{2,1,0:T(8,128)(2,1)S(1)} %pad_maximum_fusion), channel_id=1, source_target_pairs={{0,16},{16,32},{32,48},{48,64},{64,80},{80,96},{96,112},{112,128},... | collective-permute-start | bytes 294920 | tf_op jit(solution)/shard_map/ppermute | solution.py:605
  15.6 1.5 %collective-permute-start.5 = (bf16[24,8,256]{2,1,0:T(8,128)(2,1)S(1)}, bf16[24,8,256]{2,1,0:T(8,128)(2,1)S(1)}, u32[]{:S(2)}, u32[]{:S(2)}) collective-permute-start(bf16[24,8,256]{2,1,0:T(8,128)(2,1)S(1)} %pad_maximum_fusion.1), channel_id=1, source_target_pairs={{0,240},{16,0},{32,16},{48,32},{64,48},{80,64},{96,80},{112,96},{1... | collective-permute-start | bytes 294920 | tf_op jit(solution)/shard_map/ppermute | solution.py:606
  17.2 0.0 copy-done.6
  17.2 0.0 copy-start
  17.2 0.0 copy-start.1
  17.2 1.5 %bands.1 = (bf16[2304,256]{1,0:T(8,128)(2,1)S(1)}, bf16[1024,256]{1,0:T(8,128)(2,1)S(1)}, bf16[2304,256]{1,0:T(8,128)(2,1)S(1)}, bf16[1024,256]{1,0:T(8,128)(2,1)S(1)}, bf16[2304,256]{1,0:T(8,128)(2,1)S(1)}) custom-call(bf16[864,32]{1,0:T(8,128)(2,1)S(1)} %bitcast.20, bf16[4,64,64]{2,1,0:T(8,128)(2,1)S(1)} %bitcast.22, bf16[1728,64]{1,0:T(8,128)(2,1)S(1)} %bitcast.19, ...), custom_call_target="tpu_custom_call" | custom-call | flops 2000000000 | bytes 8000000 | tf_op jit(solution)/shard_map/bands/pallas_call | solution.py:102
  18.7 0.0 collective-permute-done.4.clo
  18.7 1.2 %collective-permute-done.5.chi = bf16[24,8,256]{2,1,0:T(8,128)(2,1)S(1)} collective-permute-done((bf16[24,8,256]{2,1,0:T(8,128)(2,1)S(1)}, bf16[24,8,256]{2,1,0:T(8,128)(2,1)S(1)}, u32[]{:S(2)}, u32[]{:S(2)}) %collective-permute-start.5) | collective-permute-done | bytes 98336 | tf_op jit(solution)/shard_map/ppermute | solution.py:606
  19.9 0.0 collective-permute-done.xlo
  20.0 0.0 collective-permute-done.1.xhi
  20.0 0.0 copy-done.1
  20.0 11.1 %network.1 = (bf16[896,128]{1,0:T(8,128)(2,1)S(1)}, bf16[896,128]{1,0:T(8,128)(2,1)S(1)}, bf16[18,48,256]{2,1,0:T(8,128)(2,1)S(1)}, bf16[18,48,256]{2,1,0:T(8,128)(2,1)S(1)}) custom-call(s32[1]{0:T(128)} %bitcast.core, bf16[16,32,256]{2,1,0:T(8,128)(2,1)S(1)} %copy-done, bf16[16,32,256]{2,1,0:T(8,128)(2,1)S(1)} %copy-done.1, ...), custom_call_target="tpu_custom_call" | custom-call | flops 10000000000 | bytes 10000000 | tf_op jit(solution)/shard_map/network/pallas_call | solution.py:446
  31.1 4.9 %collective-permute-start.6 = (bf16[896,128]{1,0:T(8,128)(2,1)S(1)}, bf16[896,128]{1,0:T(8,128)(2,1)S(1)}, u32[]{:S(2)}, u32[]{:S(2)}) collective-permute-start(bf16[896,128]{1,0:T(8,128)(2,1)S(1)} %get-tuple-element.36), channel_id=1, source_target_pairs={{0,16},{16,0},{32,48},{48,32},{64,80},{80,64},{96,112},{112,96},{1... | collective-permute-start | bytes 688136 | tf_op jit(solution)/shard_map/ppermute | solution.py:638
  36.0 1.5 %finish.2 = bf16[16,32,256]{2,1,0:T(8,128)(2,1)} custom-call(bf16[16,32,256]{2,1,0:T(8,128)(2,1)S(1)} %copy-done, bf16[18,48,256]{2,1,0:T(8,128)(2,1)S(1)} %get-tuple-element.37.rows, bf16[2304,256]{1,0:T(8,128)(2,1)S(1)} %get-tuple-element.35.bu.band), custom_call_target="tpu_custom_call" | custom-call | flops 1000000000 | bytes 1000000 | tf_op jit(solution)/shard_map/finish/pallas_call | solution.py:430
  37.5 0.0 collective-permute-done.6
  37.5 0.1 add_convert_fusion
  37.6 13.7 %all_to_all.15 = bf16[16,56,128]{2,1,0:T(8,128)(2,1)S(1)} all-to-all(bf16[16,56,128]{2,1,0:T(8,128)(2,1)S(1)} %bitcast.24), channel_id=1, replica_groups={{0,1,32,33,64,65,96,97,128,129,160,161,192,193,224,225},{2,3,34,35,66,6..., dimensions={0} | all-to-all | bytes 458752 | tf_op jit(solution)/shard_map/all_to_all | solution.py:642
  51.3 13.2 %all_to_all.16 = bf16[8,56,128]{2,1,0:T(8,128)(2,1)S(1)} all-to-all(bf16[8,56,128]{2,1,0:T(8,128)(2,1)S(1)} %broadcast_in_dim.6), channel_id=1, replica_groups={{0,2,4,6,8,10,12,14},{1,3,5,7,9,11,13,15},{16,18,20,22,24,26,28,30},{17..., dimensions={0} | all-to-all | bytes 229376 | tf_op jit(solution)/shard_map/all_to_all | solution.py:644
  64.6 10.2 %all_to_all.17 = bf16[16,56,128]{2,1,0:T(8,128)(2,1)S(1)} all-to-all(bf16[16,56,128]{2,1,0:T(8,128)(2,1)S(1)} %broadcast_in_dim.7), channel_id=1, replica_groups={{0,1,32,33,64,65,96,97,128,129,160,161,192,193,224,225},{2,3,34,35,66,6..., dimensions={0} | all-to-all | bytes 458752 | tf_op jit(solution)/shard_map/all_to_all | solution.py:646
  74.8 4.4 %collective-permute-start.7 = (bf16[896,128]{1,0:T(8,128)(2,1)S(1)}, bf16[896,128]{1,0:T(8,128)(2,1)S(1)}, u32[]{:S(2)}, u32[]{:S(2)}) collective-permute-start(bf16[896,128]{1,0:T(8,128)(2,1)S(1)} %bitcast.17), channel_id=1, source_target_pairs={{0,16},{16,0},{32,48},{48,32},{64,80},{80,64},{96,112},{112,96},{1... | collective-permute-start | bytes 688136 | tf_op jit(solution)/shard_map/ppermute | solution.py:648
  79.2 1.5 %finish.3 = bf16[16,32,256]{2,1,0:T(8,128)(2,1)} custom-call(bf16[16,32,256]{2,1,0:T(8,128)(2,1)S(1)} %copy-done.1, bf16[18,48,256]{2,1,0:T(8,128)(2,1)S(1)} %get-tuple-element.39.rows, bf16[2304,256]{1,0:T(8,128)(2,1)S(1)} %get-tuple-element.31.bd.band), custom_call_target="tpu_custom_call" | custom-call | flops 1000000000 | bytes 1000000 | tf_op jit(solution)/shard_map/finish/pallas_call | solution.py:430
  80.7 0.0 collective-permute-done.7.other
  80.7 1.5 %unpack.1 = (f32[27,32,32]{2,1,0:T(8,128)}, f32[4,64,64]{2,1,0:T(8,128)}, f32[27,64,64]{2,1,0:T(8,128)}, f32[4,64,64]{2,1,0:T(8,128)}, f32[27,32,32]{2,1,0:T(8,128)}) custom-call(s32[1]{0:T(128)} %bitcast.core, bf16[896,128]{1,0:T(8,128)(2,1)S(1)} %bitcast.18, bf16[896,128]{1,0:T(8,128)(2,1)S(1)} %collective-permute-done.7.other), custom_call_target="tpu_custom_call" | custom-call | tf_op jit(solution)/shard_map/unpack/pallas_call | solution.py:525
  (18 shorter events, 0.2 us)
Async XLA Ops:
  0.6 16.6 %copy-start.4 = (bf16[3,3,3,32,32]{4,3,2,1,0:T(8,128)(2,1)S(1)}, bf16[3,3,3,32,32]{4,3,2,1,0:T(8,128)(2,1)}, u32[]{:S(2)}) copy-start(bf16[3,3,3,32,32]{4,3,2,1,0:T(8,128)(2,1)} %param.12) | copy-start | bytes 165892
  0.6 16.6 %copy-start.6 = (bf16[2,2,2,64,32]{3,4,2,1,0:T(8,128)(2,1)S(1)}, bf16[2,2,2,64,32]{3,4,2,1,0:T(8,128)(2,1)}, u32[]{:S(2)}) copy-start(bf16[2,2,2,64,32]{3,4,2,1,0:T(8,128)(2,1)} %param.11) | copy-start | bytes 98308
  0.7 16.5 %copy-start.2 = (bf16[3,3,3,64,64]{4,3,2,1,0:T(8,128)(2,1)S(1)}, bf16[3,3,3,64,64]{4,3,2,1,0:T(8,128)(2,1)}, u32[]{:S(2)}) copy-start(bf16[3,3,3,64,64]{4,3,2,1,0:T(8,128)(2,1)} %param.10) | copy-start | bytes 663556
  0.7 16.5 %copy-start.5 = (bf16[2,2,2,32,64]{4,3,2,1,0:T(8,128)(2,1)S(1)}, bf16[2,2,2,32,64]{4,3,2,1,0:T(8,128)(2,1)}, u32[]{:S(2)}) copy-start(bf16[2,2,2,32,64]{4,3,2,1,0:T(8,128)(2,1)} %param.9) | copy-start | bytes 98308
  0.7 16.5 %copy-start.3 = (bf16[3,3,3,32,32]{4,3,2,1,0:T(8,128)(2,1)S(1)}, bf16[3,3,3,32,32]{4,3,2,1,0:T(8,128)(2,1)}, u32[]{:S(2)}) copy-start(bf16[3,3,3,32,32]{4,3,2,1,0:T(8,128)(2,1)} %param.8) | copy-start | bytes 165892
  2.9 10.1 %collective-permute-start.2 = (bf16[12,16,256]{2,1,0:T(8,128)(2,1)}, bf16[12,16,256]{2,1,0:T(8,128)(2,1)S(1)}, u32[]{:S(2)}, u32[]{:S(2)}) collective-permute-start(bf16[12,16,256]{2,1,0:T(8,128)(2,1)} %get-tuple-element.29), channel_id=1, source_target_pairs={{0,1},{1,2},{2,3},{3,4},{4,5},{5,6},{6,7},{7,8},{8,9},{9,10},{10,1... | collective-permute-start | bytes 294920 | tf_op jit(solution)/shard_map/ppermute | solution.py:599
  5.1 8.0 %collective-permute-start.3 = (bf16[12,16,256]{2,1,0:T(8,128)(2,1)}, bf16[12,16,256]{2,1,0:T(8,128)(2,1)S(1)}, u32[]{:S(2)}, u32[]{:S(2)}) collective-permute-start(bf16[12,16,256]{2,1,0:T(8,128)(2,1)} %get-tuple-element.30), channel_id=1, source_target_pairs={{0,15},{1,0},{2,1},{3,2},{4,3},{5,4},{6,5},{7,6},{8,7},{9,8},{10,9... | collective-permute-start | bytes 294920 | tf_op jit(solution)/shard_map/ppermute | solution.py:600
  10.4 9.5 %collective-permute-start = (bf16[12,32,256]{2,1,0:T(8,128)(2,1)}, bf16[12,32,256]{2,1,0:T(8,128)(2,1)S(1)}, u32[]{:S(2)}, u32[]{:S(2)}) collective-permute-start(bf16[12,32,256]{2,1,0:T(8,128)(2,1)} %get-tuple-element.27), channel_id=1, source_target_pairs={{0,16},{16,32},{32,48},{48,64},{64,80},{80,96},{96,112},{112,128},... | collective-permute-start | bytes 589832 | tf_op jit(solution)/shard_map/ppermute | solution.py:601
  12.6 7.4 %collective-permute-start.1 = (bf16[12,32,256]{2,1,0:T(8,128)(2,1)}, bf16[12,32,256]{2,1,0:T(8,128)(2,1)S(1)}, u32[]{:S(2)}, u32[]{:S(2)}) collective-permute-start(bf16[12,32,256]{2,1,0:T(8,128)(2,1)} %get-tuple-element.28), channel_id=1, source_target_pairs={{0,240},{16,0},{32,16},{48,32},{64,48},{80,64},{96,80},{112,96},{1... | collective-permute-start | bytes 589832 | tf_op jit(solution)/shard_map/ppermute | solution.py:602
  13.1 5.6 %collective-permute-start.4 = (bf16[24,8,256]{2,1,0:T(8,128)(2,1)S(1)}, bf16[24,8,256]{2,1,0:T(8,128)(2,1)S(1)}, u32[]{:S(2)}, u32[]{:S(2)}) collective-permute-start(bf16[24,8,256]{2,1,0:T(8,128)(2,1)S(1)} %pad_maximum_fusion), channel_id=1, source_target_pairs={{0,16},{16,32},{32,48},{48,64},{64,80},{80,96},{96,112},{112,128},... | collective-permute-start | bytes 294920 | tf_op jit(solution)/shard_map/ppermute | solution.py:605
  15.6 4.3 %collective-permute-start.5 = (bf16[24,8,256]{2,1,0:T(8,128)(2,1)S(1)}, bf16[24,8,256]{2,1,0:T(8,128)(2,1)S(1)}, u32[]{:S(2)}, u32[]{:S(2)}) collective-permute-start(bf16[24,8,256]{2,1,0:T(8,128)(2,1)S(1)} %pad_maximum_fusion.1), channel_id=1, source_target_pairs={{0,240},{16,0},{32,16},{48,32},{64,48},{80,64},{96,80},{112,96},{1... | collective-permute-start | bytes 294920 | tf_op jit(solution)/shard_map/ppermute | solution.py:606
  17.2 2.7 %copy-start = (bf16[16,32,256]{2,1,0:T(8,128)(2,1)S(1)}, bf16[16,32,256]{2,1,0:T(8,128)(2,1)}, u32[]{:S(2)}) copy-start(bf16[16,32,256]{2,1,0:T(8,128)(2,1)} %base.2) | copy-start | bytes 786436
  17.2 2.7 %copy-start.1 = (bf16[16,32,256]{2,1,0:T(8,128)(2,1)S(1)}, bf16[16,32,256]{2,1,0:T(8,128)(2,1)}, u32[]{:S(2)}) copy-start(bf16[16,32,256]{2,1,0:T(8,128)(2,1)} %base.3) | copy-start | bytes 786436
  31.1 6.4 %collective-permute-start.6 = (bf16[896,128]{1,0:T(8,128)(2,1)S(1)}, bf16[896,128]{1,0:T(8,128)(2,1)S(1)}, u32[]{:S(2)}, u32[]{:S(2)}) collective-permute-start(bf16[896,128]{1,0:T(8,128)(2,1)S(1)} %get-tuple-element.36), channel_id=1, source_target_pairs={{0,16},{16,0},{32,48},{48,32},{64,80},{80,64},{96,112},{112,96},{1... | collective-permute-start | bytes 688136 | tf_op jit(solution)/shard_map/ppermute | solution.py:638
  74.8 5.9 %collective-permute-start.7 = (bf16[896,128]{1,0:T(8,128)(2,1)S(1)}, bf16[896,128]{1,0:T(8,128)(2,1)S(1)}, u32[]{:S(2)}, u32[]{:S(2)}) collective-permute-start(bf16[896,128]{1,0:T(8,128)(2,1)S(1)} %bitcast.17), channel_id=1, source_target_pairs={{0,16},{16,0},{32,48},{48,32},{64,80},{80,64},{96,112},{112,96},{1... | collective-permute-start | bytes 688136 | tf_op jit(solution)/shard_map/ppermute | solution.py:648

commit v8 on v7

--- a/solution.py
+++ b/solution.py
@@ -156,26 +156,19 @@
     out[at, :, 2 * W : 3 * W] = pltpu.roll(v, n - 1, 0)[lo : lo + size].astype(BF)
 
 
+def three_rows(v3, first, rows):
+    pieces = [v3[pl.ds(first + a, rows)] for a in range(3)]
+    pieces = [piece.reshape(rows * piece.shape[1], 3 * W) for piece in pieces]
+    return jnp.concatenate(pieces, axis=1)
+
+
 def conv_rows(v3, first, rows, band):
-    total = None
-    for a in range(3):
-        piece = v3[pl.ds(first + a, rows)]
-        piece = piece.reshape(rows * piece.shape[1], 3 * W)
-        part = dot(piece, band[a * 3 * W : (a + 1) * 3 * W, :])
-        total = part if total is None else total + part
-    return total
+    return dot(three_rows(v3, first, rows), band[...])
 
 
 def conv_t_rows(v3, first, rows, band):
-    total = None
-    for a in range(3):
-        piece = v3[pl.ds(first + a, rows)]
-        piece = piece.reshape(rows * piece.shape[1], 3 * W)
-        for b in range(3):
-            tap = (2 - a) * 3 + (2 - b)
-            part = dot(piece[:, b * W : (b + 1) * W], band[tap * W : (tap + 1) * W, :], NT)
-            total = part if total is None else total + part
-    return total
+    taps = [band[tap * W : (tap + 1) * W, :] for tap in range(8, -1, -1)]
+    return dot(three_rows(v3, first, rows), jnp.concatenate(taps, axis=1), NT)
 
 
 def pick(d, lanes, shift, ch, width):
@@ -283,11 +276,8 @@
     loop(CX, lambda x: to_parts(hid, x))
 
     def pool(i):
-        pre = None
-        for q in range(4):
-            piece = parts[q, pl.ds(8 * i, 8)].reshape(8 * CY, W)
-            part = dot(piece, pm[q * W : (q + 1) * W, :])
-            pre = part if pre is None else pre + part
+        pieces = [parts[q, pl.ds(8 * i, 8)].reshape(8 * CY, W) for q in range(4)]
+        pre = dot(jnp.concatenate(pieces, axis=1), pm[...])
         sig = jax.nn.sigmoid(pre)
         co[pl.ds(8 * i, 8)] = rounded(pre * sig).reshape(8, CY, W)
         ds_pool[pl.ds(8 * i, 8)] = (sig * (1.0 + pre * (1.0 - sig))).reshape(8, CY, W)
@@ -360,10 +350,9 @@
         plain_terms(mid_t, d_parts, q, 64 * q)
     fold_four(46)
 
-    d_middle = None
-    for q in range(4):
-        part = dot(d_parts[q, 2:14].reshape(12 * CY, W), um[q * W : (q + 1) * W, :], NT)
-        d_middle = part if d_middle is None else d_middle + part
+    pieces = [d_parts[q, 2:14].reshape(12 * CY, W) for q in range(4)]
+    lanes = [um[q * W : (q + 1) * W, :] for q in range(4)]
+    d_middle = dot(jnp.concatenate(pieces, axis=1), jnp.concatenate(lanes, axis=1), NT)
     dmid[2:14] = rounded(d_middle * ds_mid[2:14].reshape(12 * CY, W)).reshape(12, CY, W)
     ds_mid[2:14] = d_middle.reshape(12, CY, W)
 
@@ -540,7 +529,7 @@
     return [(i, (i + step) % n) for i in range(n)]
 
 
-def pack_kernel(fc, cc, first_x, last_x, first_y, last_y, side, wide, rows, columns, sems):
+def pack_kernel(fc, cc, first_x, last_x, first_y, last_y, side, wide, sems):
     copies = []
 
     def fetch(src, dst):
@@ -552,14 +541,12 @@
         fetch(src.at[:, 0:16], side.at[2 * k])
         fetch(src.at[:, BY - 16 : BY], side.at[2 * k + 1])
     for src, count, at in ((fc, HF, 0), (cc, HC, HF)):
-        fetch(src.at[0:count], rows.at[0, at : at + count])
-        fetch(src.at[BX - count : BX], rows.at[1, at : at + count])
-    for copy in copies:
+        fetch(src.at[0:count], first_x.at[at : at + count])
+        fetch(src.at[BX - count : BX], last_x.at[at : at + count])
+    for copy in copies[:4]:
         copy.wait()
-    fetch(rows.at[0], first_x)
-    fetch(rows.at[1], last_x)
     for k, (count, at) in enumerate(((HF, 0), (HC, HF))):
-        for e, (out, first) in enumerate(((0, 0), (1, 16 - count))):
+        for e, (out, first) in enumerate(((first_y, 0), (last_y, 16 - count))):
             for h in range(2):
                 lanes = slice(h * 128, h * 128 + 128)
                 wide[h] = side[2 * k + e, :, :, lanes].reshape(BX * 16, 128).astype(F32)
@@ -567,10 +554,8 @@
                 for h in range(2):
                     lanes = slice(h * 128, h * 128 + 128)
                     column = wide[h, pl.ds(first + c, BX, stride=16), :]
-                    columns[out, at + c, :, lanes] = column.astype(BF)
-    fetch(columns.at[0], first_y)
-    fetch(columns.at[1], last_y)
-    for copy in copies[8:]:
+                    out[at + c, :, lanes] = column.astype(BF)
+    for copy in copies[4:]:
         copy.wait()
 
 
@@ -581,15 +566,12 @@
         pack_kernel,
         out_shape=(rows, rows, columns, columns),
         in_specs=[pl.BlockSpec(memory_space=pl.ANY)] * 2,
-        out_specs=(pl.BlockSpec(memory_space=pl.ANY),) * 4,
         scratch_shapes=[
             pltpu.VMEM((4, BX, 16, W), BF),
             pltpu.VMEM((2, BX * 16, 128), F32),
-            pltpu.VMEM((2, HF + HC, BY, W), BF),
-            pltpu.VMEM((2, HF + HC, BX, W), BF),
-            pltpu.SemaphoreType.DMA((12,)),
+            pltpu.SemaphoreType.DMA((8,)),
         ],
-        compiler_params=pltpu.CompilerParams(vmem_limit_bytes=56 * 1024 * 1024),
+        compiler_params=pltpu.CompilerParams(vmem_limit_bytes=54592 * 1024),
         name="pack",
     )(fields, cot)
 

time: 82.6 us -> 81.6 us (0.988)
  Pallas kernels: 19.3 us -> 18.4 us
    pallas_call x1, Pallas kernels: 2.26 us -> 1.42 us  [pack(): pl.pallas_call(pack_kernel, out_shape=(rows, rows, columns, columns), in_...]
where the time goes in v8:
time: 81.6 us; the launch traced here: 81.4 us
  blocking collectives  37.1 us (45%)
  starting transfers between devices  23.3 us (29%)
  Pallas kernels  18.4 us (23%)
  waiting for transfers between devices  1.32 us (2%)
  between operations  0.98 us (1%)
    all_to_all x1, blocking collectives, per_device(): part = swap(part.astype(BF).reshape(n1, rows, 128), axis_index_groups=near)  13.7 us
    all_to_all x1, blocking collectives, per_device(): swap(jnp.broadcast_to(part, (n2, rows, 128)), axis_index_groups=far)  13.2 us
    pallas_call x1, Pallas kernels, main_call(): pl.pallas_call(main_kernel, out_shape=(half, half, some, some), in_specs=...  11 us
    all_to_all x1, blocking collectives, per_device(): part = swap(jnp.broadcast_to(part, (n1, rows, 128)), axis_index_groups=near)  10.3 us
    ppermute x1, starting transfers between devices, exchange(): yhi = lax.ppermute(first_y, 'gy', ring('gy', -1))  5.38 us
    ppermute x1, starting transfers between devices, per_device(): theirs = lax.ppermute(other, 'gx', pairs)  5.08 us
    ppermute x1, starting transfers between devices, per_device(): theirs = lax.ppermute(part, 'gx', pairs)  4.39 us
    pallas_call x2, Pallas kernels, finish_call(): pl.pallas_call(functools.partial(finish_kernel, conv), out_shape=jax.Shap...  3.01 us
  transfers between devices with their start and end apart: 8, of which 2 were waited for; matrix products, arithmetic and copies ran while one was open for 0% of the time, Pallas kernels for 5%

profile of v8, /device:TPU:1, one launch (start us, length us, event | category | flops | bytes accessed | tf_op | source)
XLA Modules:
  0.0 81.4 jit_solution(16564395400492041749)
XLA Ops:
  0.6 0.0 copy-start.4
  0.6 0.0 copy-start.6
  0.7 1.4 %pack.1 = (bf16[12,32,256]{2,1,0:T(8,128)(2,1)S(1)}, bf16[12,32,256]{2,1,0:T(8,128)(2,1)S(1)}, bf16[12,16,256]{2,1,0:T(8,128)(2,1)S(1)}, bf16[12,16,256]{2,1,0:T(8,128)(2,1)S(1)}) custom-call(bf16[16,32,256]{2,1,0:T(8,128)(2,1)} %base.2, bf16[16,32,256]{2,1,0:T(8,128)(2,1)} %base.3), custom_call_target="tpu_custom_call" | custom-call | tf_op jit(solution)/shard_map/pack/pallas_call | solution.py:565
  2.1 2.1 %collective-permute-start.2 = (bf16[12,16,256]{2,1,0:T(8,128)(2,1)S(1)}, bf16[12,16,256]{2,1,0:T(8,128)(2,1)S(1)}, u32[]{:S(2)}, u32[]{:S(2)}) collective-permute-start(bf16[12,16,256]{2,1,0:T(8,128)(2,1)S(1)} %get-tuple-element.29), channel_id=1, source_target_pairs={{0,1},{1,2},{2,3},{3,4},{4,5},{5,6},{6,7},{7,8},{8,9},{9,10},{10,1... | collective-permute-start | bytes 294920 | tf_op jit(solution)/shard_map/ppermute | solution.py:581
  4.2 5.4 %collective-permute-start.3 = (bf16[12,16,256]{2,1,0:T(8,128)(2,1)S(1)}, bf16[12,16,256]{2,1,0:T(8,128)(2,1)S(1)}, u32[]{:S(2)}, u32[]{:S(2)}) collective-permute-start(bf16[12,16,256]{2,1,0:T(8,128)(2,1)S(1)} %get-tuple-element.30), channel_id=1, source_target_pairs={{0,15},{1,0},{2,1},{3,2},{4,3},{5,4},{6,5},{7,6},{8,7},{9,8},{10,9... | collective-permute-start | bytes 294920 | tf_op jit(solution)/shard_map/ppermute | solution.py:582
  9.6 2.1 %collective-permute-start = (bf16[12,32,256]{2,1,0:T(8,128)(2,1)S(1)}, bf16[12,32,256]{2,1,0:T(8,128)(2,1)S(1)}, u32[]{:S(2)}, u32[]{:S(2)}) collective-permute-start(bf16[12,32,256]{2,1,0:T(8,128)(2,1)S(1)} %get-tuple-element.27), channel_id=1, source_target_pairs={{0,16},{16,32},{32,48},{48,64},{64,80},{80,96},{96,112},{112,128},... | collective-permute-start | bytes 589832 | tf_op jit(solution)/shard_map/ppermute | solution.py:583
  11.7 0.0 collective-permute-start.1
  11.7 0.3 collective-permute-done.2.ylo
  12.1 0.0 collective-permute-done.3.yhi
  12.1 2.5 %collective-permute-start.4 = (bf16[24,8,256]{2,1,0:T(8,128)(2,1)S(1)}, bf16[24,8,256]{2,1,0:T(8,128)(2,1)S(1)}, u32[]{:S(2)}, u32[]{:S(2)}) collective-permute-start(bf16[24,8,256]{2,1,0:T(8,128)(2,1)S(1)} %pad_maximum_fusion), channel_id=1, source_target_pairs={{0,16},{16,32},{32,48},{48,64},{64,80},{80,96},{96,112},{112,128},... | collective-permute-start | bytes 294920 | tf_op jit(solution)/shard_map/ppermute | solution.py:587
  14.6 1.8 %collective-permute-start.5 = (bf16[24,8,256]{2,1,0:T(8,128)(2,1)S(1)}, bf16[24,8,256]{2,1,0:T(8,128)(2,1)S(1)}, u32[]{:S(2)}, u32[]{:S(2)}) collective-permute-start(bf16[24,8,256]{2,1,0:T(8,128)(2,1)S(1)} %pad_maximum_fusion.1), channel_id=1, source_target_pairs={{0,240},{16,0},{32,16},{48,32},{64,48},{80,64},{96,80},{112,96},{1... | collective-permute-start | bytes 294920 | tf_op jit(solution)/shard_map/ppermute | solution.py:588
  16.4 0.0 copy-done.4
  16.4 0.0 copy-done.3
  16.4 0.0 copy-start
  16.4 0.0 copy-start.1
  16.4 1.5 %bands.1 = (bf16[2304,256]{1,0:T(8,128)(2,1)S(1)}, bf16[1024,256]{1,0:T(8,128)(2,1)S(1)}, bf16[2304,256]{1,0:T(8,128)(2,1)S(1)}, bf16[1024,256]{1,0:T(8,128)(2,1)S(1)}, bf16[2304,256]{1,0:T(8,128)(2,1)S(1)}) custom-call(bf16[864,32]{1,0:T(8,128)(2,1)S(1)} %bitcast.20, bf16[4,64,64]{2,1,0:T(8,128)(2,1)S(1)} %bitcast.22, bf16[1728,64]{1,0:T(8,128)(2,1)S(1)} %bitcast.19, ...), custom_call_target="tpu_custom_call" | custom-call | flops 2000000000 | bytes 8000000 | tf_op jit(solution)/shard_map/bands/pallas_call | solution.py:102
  17.9 0.0 collective-permute-done.4.clo
  17.9 1.0 %collective-permute-done.5.chi = bf16[24,8,256]{2,1,0:T(8,128)(2,1)S(1)} collective-permute-done((bf16[24,8,256]{2,1,0:T(8,128)(2,1)S(1)}, bf16[24,8,256]{2,1,0:T(8,128)(2,1)S(1)}, u32[]{:S(2)}, u32[]{:S(2)}) %collective-permute-start.5) | collective-permute-done | bytes 98336 | tf_op jit(solution)/shard_map/ppermute | solution.py:588
  18.9 0.0 collective-permute-done.xlo
  18.9 0.0 collective-permute-done.1.xhi
  18.9 11.0 %network.1 = (bf16[896,128]{1,0:T(8,128)(2,1)S(1)}, bf16[896,128]{1,0:T(8,128)(2,1)S(1)}, bf16[18,48,256]{2,1,0:T(8,128)(2,1)S(1)}, bf16[18,48,256]{2,1,0:T(8,128)(2,1)S(1)}) custom-call(s32[1]{0:T(128)} %bitcast.core, bf16[16,32,256]{2,1,0:T(8,128)(2,1)S(1)} %copy-done, bf16[16,32,256]{2,1,0:T(8,128)(2,1)S(1)} %copy-done.1, ...), custom_call_target="tpu_custom_call" | custom-call | flops 10000000000 | bytes 10000000 | tf_op jit(solution)/shard_map/network/pallas_call | solution.py:435
  30.0 5.1 %collective-permute-start.6 = (bf16[896,128]{1,0:T(8,128)(2,1)S(1)}, bf16[896,128]{1,0:T(8,128)(2,1)S(1)}, u32[]{:S(2)}, u32[]{:S(2)}) collective-permute-start(bf16[896,128]{1,0:T(8,128)(2,1)S(1)} %get-tuple-element.36), channel_id=1, source_target_pairs={{0,16},{16,0},{32,48},{48,32},{64,80},{80,64},{96,112},{112,96},{1... | collective-permute-start | bytes 688136 | tf_op jit(solution)/shard_map/ppermute | solution.py:620
  35.1 1.5 %finish.2 = bf16[16,32,256]{2,1,0:T(8,128)(2,1)} custom-call(bf16[16,32,256]{2,1,0:T(8,128)(2,1)S(1)} %copy-done, bf16[18,48,256]{2,1,0:T(8,128)(2,1)S(1)} %get-tuple-element.37.rows, bf16[2304,256]{1,0:T(8,128)(2,1)S(1)} %get-tuple-element.35.bu.band), custom_call_target="tpu_custom_call" | custom-call | flops 1000000000 | bytes 1000000 | tf_op jit(solution)/shard_map/finish/pallas_call | solution.py:419
  36.5 0.0 collective-permute-done.6
  36.5 0.1 add_convert_fusion
  36.6 13.7 %all_to_all.15 = bf16[16,56,128]{2,1,0:T(8,128)(2,1)S(1)} all-to-all(bf16[16,56,128]{2,1,0:T(8,128)(2,1)S(1)} %bitcast.24), channel_id=1, replica_groups={{0,1,32,33,64,65,96,97,128,129,160,161,192,193,224,225},{2,3,34,35,66,6..., dimensions={0} | all-to-all | bytes 458752 | tf_op jit(solution)/shard_map/all_to_all | solution.py:624
  50.4 13.2 %all_to_all.16 = bf16[8,56,128]{2,1,0:T(8,128)(2,1)S(1)} all-to-all(bf16[8,56,128]{2,1,0:T(8,128)(2,1)S(1)} %broadcast_in_dim.6), channel_id=1, replica_groups={{0,2,4,6,8,10,12,14},{1,3,5,7,9,11,13,15},{16,18,20,22,24,26,28,30},{17..., dimensions={0} | all-to-all | bytes 229376 | tf_op jit(solution)/shard_map/all_to_all | solution.py:626
  63.6 10.3 %all_to_all.17 = bf16[16,56,128]{2,1,0:T(8,128)(2,1)S(1)} all-to-all(bf16[16,56,128]{2,1,0:T(8,128)(2,1)S(1)} %broadcast_in_dim.7), channel_id=1, replica_groups={{0,1,32,33,64,65,96,97,128,129,160,161,192,193,224,225},{2,3,34,35,66,6..., dimensions={0} | all-to-all | bytes 458752 | tf_op jit(solution)/shard_map/all_to_all | solution.py:628
  73.9 4.4 %collective-permute-start.7 = (bf16[896,128]{1,0:T(8,128)(2,1)S(1)}, bf16[896,128]{1,0:T(8,128)(2,1)S(1)}, u32[]{:S(2)}, u32[]{:S(2)}) collective-permute-start(bf16[896,128]{1,0:T(8,128)(2,1)S(1)} %bitcast.17), channel_id=1, source_target_pairs={{0,16},{16,0},{32,48},{48,32},{64,80},{80,64},{96,112},{112,96},{1... | collective-permute-start | bytes 688136 | tf_op jit(solution)/shard_map/ppermute | solution.py:630
  78.3 1.5 %finish.3 = bf16[16,32,256]{2,1,0:T(8,128)(2,1)} custom-call(bf16[16,32,256]{2,1,0:T(8,128)(2,1)S(1)} %copy-done.1, bf16[18,48,256]{2,1,0:T(8,128)(2,1)S(1)} %get-tuple-element.39.rows, bf16[2304,256]{1,0:T(8,128)(2,1)S(1)} %get-tuple-element.31.bd.band), custom_call_target="tpu_custom_call" | custom-call | flops 1000000000 | bytes 1000000 | tf_op jit(solution)/shard_map/finish/pallas_call | solution.py:419
  79.8 0.0 collective-permute-done.7.other
  79.8 1.5 %unpack.1 = (f32[27,32,32]{2,1,0:T(8,128)}, f32[4,64,64]{2,1,0:T(8,128)}, f32[27,64,64]{2,1,0:T(8,128)}, f32[4,64,64]{2,1,0:T(8,128)}, f32[27,32,32]{2,1,0:T(8,128)}) custom-call(s32[1]{0:T(128)} %bitcast.core, bf16[896,128]{1,0:T(8,128)(2,1)S(1)} %bitcast.18, bf16[896,128]{1,0:T(8,128)(2,1)S(1)} %collective-permute-done.7.other), custom_call_target="tpu_custom_call" | custom-call | tf_op jit(solution)/shard_map/unpack/pallas_call | solution.py:514
  (18 shorter events, 0.2 us)
Async XLA Ops:
  0.6 15.7 %copy-start.4 = (bf16[3,3,3,32,32]{4,3,2,1,0:T(8,128)(2,1)S(1)}, bf16[3,3,3,32,32]{4,3,2,1,0:T(8,128)(2,1)}, u32[]{:S(2)}) copy-start(bf16[3,3,3,32,32]{4,3,2,1,0:T(8,128)(2,1)} %param.12) | copy-start | bytes 165892
  0.6 15.7 %copy-start.6 = (bf16[2,2,2,64,32]{3,4,2,1,0:T(8,128)(2,1)S(1)}, bf16[2,2,2,64,32]{3,4,2,1,0:T(8,128)(2,1)}, u32[]{:S(2)}) copy-start(bf16[2,2,2,64,32]{3,4,2,1,0:T(8,128)(2,1)} %param.11) | copy-start | bytes 98308
  0.7 15.7 %copy-start.2 = (bf16[3,3,3,64,64]{4,3,2,1,0:T(8,128)(2,1)S(1)}, bf16[3,3,3,64,64]{4,3,2,1,0:T(8,128)(2,1)}, u32[]{:S(2)}) copy-start(bf16[3,3,3,64,64]{4,3,2,1,0:T(8,128)(2,1)} %param.10) | copy-start | bytes 663556
  0.7 15.7 %copy-start.5 = (bf16[2,2,2,32,64]{4,3,2,1,0:T(8,128)(2,1)S(1)}, bf16[2,2,2,32,64]{4,3,2,1,0:T(8,128)(2,1)}, u32[]{:S(2)}) copy-start(bf16[2,2,2,32,64]{4,3,2,1,0:T(8,128)(2,1)} %param.9) | copy-start | bytes 98308
  0.7 15.7 %copy-start.3 = (bf16[3,3,3,32,32]{4,3,2,1,0:T(8,128)(2,1)S(1)}, bf16[3,3,3,32,32]{4,3,2,1,0:T(8,128)(2,1)}, u32[]{:S(2)}) copy-start(bf16[3,3,3,32,32]{4,3,2,1,0:T(8,128)(2,1)} %param.8) | copy-start | bytes 165892
  2.1 9.9 %collective-permute-start.2 = (bf16[12,16,256]{2,1,0:T(8,128)(2,1)S(1)}, bf16[12,16,256]{2,1,0:T(8,128)(2,1)S(1)}, u32[]{:S(2)}, u32[]{:S(2)}) collective-permute-start(bf16[12,16,256]{2,1,0:T(8,128)(2,1)S(1)} %get-tuple-element.29), channel_id=1, source_target_pairs={{0,1},{1,2},{2,3},{3,4},{4,5},{5,6},{6,7},{7,8},{8,9},{9,10},{10,1... | collective-permute-start | bytes 294920 | tf_op jit(solution)/shard_map/ppermute | solution.py:581
  4.2 7.8 %collective-permute-start.3 = (bf16[12,16,256]{2,1,0:T(8,128)(2,1)S(1)}, bf16[12,16,256]{2,1,0:T(8,128)(2,1)S(1)}, u32[]{:S(2)}, u32[]{:S(2)}) collective-permute-start(bf16[12,16,256]{2,1,0:T(8,128)(2,1)S(1)} %get-tuple-element.30), channel_id=1, source_target_pairs={{0,15},{1,0},{2,1},{3,2},{4,3},{5,4},{6,5},{7,6},{8,7},{9,8},{10,9... | collective-permute-start | bytes 294920 | tf_op jit(solution)/shard_map/ppermute | solution.py:582
  9.6 9.3 %collective-permute-start = (bf16[12,32,256]{2,1,0:T(8,128)(2,1)S(1)}, bf16[12,32,256]{2,1,0:T(8,128)(2,1)S(1)}, u32[]{:S(2)}, u32[]{:S(2)}) collective-permute-start(bf16[12,32,256]{2,1,0:T(8,128)(2,1)S(1)} %get-tuple-element.27), channel_id=1, source_target_pairs={{0,16},{16,32},{32,48},{48,64},{64,80},{80,96},{96,112},{112,128},... | collective-permute-start | bytes 589832 | tf_op jit(solution)/shard_map/ppermute | solution.py:583
  11.7 7.2 %collective-permute-start.1 = (bf16[12,32,256]{2,1,0:T(8,128)(2,1)S(1)}, bf16[12,32,256]{2,1,0:T(8,128)(2,1)S(1)}, u32[]{:S(2)}, u32[]{:S(2)}) collective-permute-start(bf16[12,32,256]{2,1,0:T(8,128)(2,1)S(1)} %get-tuple-element.28), channel_id=1, source_target_pairs={{0,240},{16,0},{32,16},{48,32},{64,48},{80,64},{96,80},{112,96},{1... | collective-permute-start | bytes 589832 | tf_op jit(solution)/shard_map/ppermute | solution.py:584
  12.1 5.8 %collective-permute-start.4 = (bf16[24,8,256]{2,1,0:T(8,128)(2,1)S(1)}, bf16[24,8,256]{2,1,0:T(8,128)(2,1)S(1)}, u32[]{:S(2)}, u32[]{:S(2)}) collective-permute-start(bf16[24,8,256]{2,1,0:T(8,128)(2,1)S(1)} %pad_maximum_fusion), channel_id=1, source_target_pairs={{0,16},{16,32},{32,48},{48,64},{64,80},{80,96},{96,112},{112,128},... | collective-permute-start | bytes 294920 | tf_op jit(solution)/shard_map/ppermute | solution.py:587
  14.6 4.3 %collective-permute-start.5 = (bf16[24,8,256]{2,1,0:T(8,128)(2,1)S(1)}, bf16[24,8,256]{2,1,0:T(8,128)(2,1)S(1)}, u32[]{:S(2)}, u32[]{:S(2)}) collective-permute-start(bf16[24,8,256]{2,1,0:T(8,128)(2,1)S(1)} %pad_maximum_fusion.1), channel_id=1, source_target_pairs={{0,240},{16,0},{32,16},{48,32},{64,48},{80,64},{96,80},{112,96},{1... | collective-permute-start | bytes 294920 | tf_op jit(solution)/shard_map/ppermute | solution.py:588
  16.4 2.5 %copy-start = (bf16[16,32,256]{2,1,0:T(8,128)(2,1)S(1)}, bf16[16,32,256]{2,1,0:T(8,128)(2,1)}, u32[]{:S(2)}) copy-start(bf16[16,32,256]{2,1,0:T(8,128)(2,1)} %base.2) | copy-start | bytes 786436
  16.4 2.5 %copy-start.1 = (bf16[16,32,256]{2,1,0:T(8,128)(2,1)S(1)}, bf16[16,32,256]{2,1,0:T(8,128)(2,1)}, u32[]{:S(2)}) copy-start(bf16[16,32,256]{2,1,0:T(8,128)(2,1)} %base.3) | copy-start | bytes 786436
  30.0 6.6 %collective-permute-start.6 = (bf16[896,128]{1,0:T(8,128)(2,1)S(1)}, bf16[896,128]{1,0:T(8,128)(2,1)S(1)}, u32[]{:S(2)}, u32[]{:S(2)}) collective-permute-start(bf16[896,128]{1,0:T(8,128)(2,1)S(1)} %get-tuple-element.36), channel_id=1, source_target_pairs={{0,16},{16,0},{32,48},{48,32},{64,80},{80,64},{96,112},{112,96},{1... | collective-permute-start | bytes 688136 | tf_op jit(solution)/shard_map/ppermute | solution.py:620
  73.9 5.9 %collective-permute-start.7 = (bf16[896,128]{1,0:T(8,128)(2,1)S(1)}, bf16[896,128]{1,0:T(8,128)(2,1)S(1)}, u32[]{:S(2)}, u32[]{:S(2)}) collective-permute-start(bf16[896,128]{1,0:T(8,128)(2,1)S(1)} %bitcast.17), channel_id=1, source_target_pairs={{0,16},{16,0},{32,48},{48,32},{64,80},{80,64},{96,112},{112,96},{1... | collective-permute-start | bytes 688136 | tf_op jit(solution)/shard_map/ppermute | solution.py:630

commit v9 on v8

--- a/solution.py
+++ b/solution.py
@@ -31,7 +31,7 @@
     return v.astype(BF).astype(F32)
 
 
-DOWN, D_UP, UP = 7, 6, 3
+DOWN, D_UP, UP = 14, 24, 6
 MOST = 64
 
 

time: 81.6 us -> 80.9 us (level)
  transfers between devices with their start and end apart: 8 -> 8, of which waited for: 2 -> 2; matrix products, arithmetic and copies ran while one was open for 0% -> 0% of each run, Pallas kernels for 5% -> 6%
where the time goes in v9:
time: 80.9 us; the launch traced here: 80.7 us
  blocking collectives  37.1 us (46%)
  starting transfers between devices  23.4 us (29%)
  Pallas kernels  17.7 us (22%)
  waiting for transfers between devices  1.32 us (2%)
  between operations  0.98 us (1%)
    all_to_all x1, blocking collectives, per_device(): part = swap(part.astype(BF).reshape(n1, rows, 128), axis_index_groups=near)  13.7 us
    all_to_all x1, blocking collectives, per_device(): swap(jnp.broadcast_to(part, (n2, rows, 128)), axis_index_groups=far)  13.2 us
    pallas_call x1, Pallas kernels, main_call(): pl.pallas_call(main_kernel, out_shape=(half, half, some, some), in_specs=...  10.3 us
    all_to_all x1, blocking collectives, per_device(): part = swap(jnp.broadcast_to(part, (n1, rows, 128)), axis_index_groups=near)  10.2 us
    ppermute x1, starting transfers between devices, exchange(): yhi = lax.ppermute(first_y, 'gy', ring('gy', -1))  5.38 us
    ppermute x1, starting transfers between devices, per_device(): theirs = lax.ppermute(other, 'gx', pairs)  5.08 us
    ppermute x1, starting transfers between devices, per_device(): theirs = lax.ppermute(part, 'gx', pairs)  4.39 us
    pallas_call x2, Pallas kernels, finish_call(): pl.pallas_call(functools.partial(finish_kernel, conv), out_shape=jax.Shap...  3.01 us
  transfers between devices with their start and end apart: 8, of which 2 were waited for; matrix products, arithmetic and copies ran while one was open for 0% of the time, Pallas kernels for 6%

profile of v9, /device:TPU:1, one launch (start us, length us, event | category | flops | bytes accessed | tf_op | source)
XLA Modules:
  0.0 80.7 jit_solution(14154559636844439418)
XLA Ops:
  0.6 0.0 copy-start.4
  0.6 0.0 copy-start.6
  0.7 1.4 %pack.1 = (bf16[12,32,256]{2,1,0:T(8,128)(2,1)S(1)}, bf16[12,32,256]{2,1,0:T(8,128)(2,1)S(1)}, bf16[12,16,256]{2,1,0:T(8,128)(2,1)S(1)}, bf16[12,16,256]{2,1,0:T(8,128)(2,1)S(1)}) custom-call(bf16[16,32,256]{2,1,0:T(8,128)(2,1)} %base.2, bf16[16,32,256]{2,1,0:T(8,128)(2,1)} %base.3), custom_call_target="tpu_custom_call" | custom-call | tf_op jit(solution)/shard_map/pack/pallas_call | solution.py:565
  2.1 2.1 %collective-permute-start.2 = (bf16[12,16,256]{2,1,0:T(8,128)(2,1)S(1)}, bf16[12,16,256]{2,1,0:T(8,128)(2,1)S(1)}, u32[]{:S(2)}, u32[]{:S(2)}) collective-permute-start(bf16[12,16,256]{2,1,0:T(8,128)(2,1)S(1)} %get-tuple-element.29), channel_id=1, source_target_pairs={{0,1},{1,2},{2,3},{3,4},{4,5},{5,6},{6,7},{7,8},{8,9},{9,10},{10,1... | collective-permute-start | bytes 294920 | tf_op jit(solution)/shard_map/ppermute | solution.py:581
  4.2 5.4 %collective-permute-start.3 = (bf16[12,16,256]{2,1,0:T(8,128)(2,1)S(1)}, bf16[12,16,256]{2,1,0:T(8,128)(2,1)S(1)}, u32[]{:S(2)}, u32[]{:S(2)}) collective-permute-start(bf16[12,16,256]{2,1,0:T(8,128)(2,1)S(1)} %get-tuple-element.30), channel_id=1, source_target_pairs={{0,15},{1,0},{2,1},{3,2},{4,3},{5,4},{6,5},{7,6},{8,7},{9,8},{10,9... | collective-permute-start | bytes 294920 | tf_op jit(solution)/shard_map/ppermute | solution.py:582
  9.6 2.1 %collective-permute-start = (bf16[12,32,256]{2,1,0:T(8,128)(2,1)S(1)}, bf16[12,32,256]{2,1,0:T(8,128)(2,1)S(1)}, u32[]{:S(2)}, u32[]{:S(2)}) collective-permute-start(bf16[12,32,256]{2,1,0:T(8,128)(2,1)S(1)} %get-tuple-element.27), channel_id=1, source_target_pairs={{0,16},{16,32},{32,48},{48,64},{64,80},{80,96},{96,112},{112,128},... | collective-permute-start | bytes 589832 | tf_op jit(solution)/shard_map/ppermute | solution.py:583
  11.7 0.0 collective-permute-start.1
  11.7 0.3 collective-permute-done.2.ylo
  12.1 0.0 collective-permute-done.3.yhi
  12.1 2.5 %collective-permute-start.4 = (bf16[24,8,256]{2,1,0:T(8,128)(2,1)S(1)}, bf16[24,8,256]{2,1,0:T(8,128)(2,1)S(1)}, u32[]{:S(2)}, u32[]{:S(2)}) collective-permute-start(bf16[24,8,256]{2,1,0:T(8,128)(2,1)S(1)} %pad_maximum_fusion), channel_id=1, source_target_pairs={{0,16},{16,32},{32,48},{48,64},{64,80},{80,96},{96,112},{112,128},... | collective-permute-start | bytes 294920 | tf_op jit(solution)/shard_map/ppermute | solution.py:587
  14.6 1.8 %collective-permute-start.5 = (bf16[24,8,256]{2,1,0:T(8,128)(2,1)S(1)}, bf16[24,8,256]{2,1,0:T(8,128)(2,1)S(1)}, u32[]{:S(2)}, u32[]{:S(2)}) collective-permute-start(bf16[24,8,256]{2,1,0:T(8,128)(2,1)S(1)} %pad_maximum_fusion.1), channel_id=1, source_target_pairs={{0,240},{16,0},{32,16},{48,32},{64,48},{80,64},{96,80},{112,96},{1... | collective-permute-start | bytes 294920 | tf_op jit(solution)/shard_map/ppermute | solution.py:588
  16.4 0.0 copy-done.4
  16.4 0.0 copy-done.3
  16.4 0.0 copy-start
  16.4 0.0 copy-start.1
  16.4 1.5 %bands.1 = (bf16[2304,256]{1,0:T(8,128)(2,1)S(1)}, bf16[1024,256]{1,0:T(8,128)(2,1)S(1)}, bf16[2304,256]{1,0:T(8,128)(2,1)S(1)}, bf16[1024,256]{1,0:T(8,128)(2,1)S(1)}, bf16[2304,256]{1,0:T(8,128)(2,1)S(1)}) custom-call(bf16[864,32]{1,0:T(8,128)(2,1)S(1)} %bitcast.20, bf16[4,64,64]{2,1,0:T(8,128)(2,1)S(1)} %bitcast.22, bf16[1728,64]{1,0:T(8,128)(2,1)S(1)} %bitcast.19, ...), custom_call_target="tpu_custom_call" | custom-call | flops 2000000000 | bytes 8000000 | tf_op jit(solution)/shard_map/bands/pallas_call | solution.py:102
  17.9 0.0 collective-permute-done.4.clo
  17.9 1.0 %collective-permute-done.5.chi = bf16[24,8,256]{2,1,0:T(8,128)(2,1)S(1)} collective-permute-done((bf16[24,8,256]{2,1,0:T(8,128)(2,1)S(1)}, bf16[24,8,256]{2,1,0:T(8,128)(2,1)S(1)}, u32[]{:S(2)}, u32[]{:S(2)}) %collective-permute-start.5) | collective-permute-done | bytes 98336 | tf_op jit(solution)/shard_map/ppermute | solution.py:588
  18.9 0.0 collective-permute-done.xlo
  18.9 0.0 collective-permute-done.1.xhi
  18.9 10.3 %network.1 = (bf16[896,128]{1,0:T(8,128)(2,1)S(1)}, bf16[896,128]{1,0:T(8,128)(2,1)S(1)}, bf16[18,48,256]{2,1,0:T(8,128)(2,1)S(1)}, bf16[18,48,256]{2,1,0:T(8,128)(2,1)S(1)}) custom-call(s32[1]{0:T(128)} %bitcast.core, bf16[16,32,256]{2,1,0:T(8,128)(2,1)S(1)} %copy-done, bf16[16,32,256]{2,1,0:T(8,128)(2,1)S(1)} %copy-done.1, ...), custom_call_target="tpu_custom_call" | custom-call | flops 10000000000 | bytes 10000000 | tf_op jit(solution)/shard_map/network/pallas_call | solution.py:435
  29.3 5.1 %collective-permute-start.6 = (bf16[896,128]{1,0:T(8,128)(2,1)S(1)}, bf16[896,128]{1,0:T(8,128)(2,1)S(1)}, u32[]{:S(2)}, u32[]{:S(2)}) collective-permute-start(bf16[896,128]{1,0:T(8,128)(2,1)S(1)} %get-tuple-element.36), channel_id=1, source_target_pairs={{0,16},{16,0},{32,48},{48,32},{64,80},{80,64},{96,112},{112,96},{1... | collective-permute-start | bytes 688136 | tf_op jit(solution)/shard_map/ppermute | solution.py:620
  34.3 1.5 %finish.2 = bf16[16,32,256]{2,1,0:T(8,128)(2,1)} custom-call(bf16[16,32,256]{2,1,0:T(8,128)(2,1)S(1)} %copy-done, bf16[18,48,256]{2,1,0:T(8,128)(2,1)S(1)} %get-tuple-element.37.rows, bf16[2304,256]{1,0:T(8,128)(2,1)S(1)} %get-tuple-element.35.bu.band), custom_call_target="tpu_custom_call" | custom-call | flops 1000000000 | bytes 1000000 | tf_op jit(solution)/shard_map/finish/pallas_call | solution.py:419
  35.8 0.0 collective-permute-done.6
  35.8 0.1 add_convert_fusion
  35.9 13.7 %all_to_all.15 = bf16[16,56,128]{2,1,0:T(8,128)(2,1)S(1)} all-to-all(bf16[16,56,128]{2,1,0:T(8,128)(2,1)S(1)} %bitcast.24), channel_id=1, replica_groups={{0,1,32,33,64,65,96,97,128,129,160,161,192,193,224,225},{2,3,34,35,66,6..., dimensions={0} | all-to-all | bytes 458752 | tf_op jit(solution)/shard_map/all_to_all | solution.py:624
  49.7 13.2 %all_to_all.16 = bf16[8,56,128]{2,1,0:T(8,128)(2,1)S(1)} all-to-all(bf16[8,56,128]{2,1,0:T(8,128)(2,1)S(1)} %broadcast_in_dim.6), channel_id=1, replica_groups={{0,2,4,6,8,10,12,14},{1,3,5,7,9,11,13,15},{16,18,20,22,24,26,28,30},{17..., dimensions={0} | all-to-all | bytes 229376 | tf_op jit(solution)/shard_map/all_to_all | solution.py:626
  62.9 10.2 %all_to_all.17 = bf16[16,56,128]{2,1,0:T(8,128)(2,1)S(1)} all-to-all(bf16[16,56,128]{2,1,0:T(8,128)(2,1)S(1)} %broadcast_in_dim.7), channel_id=1, replica_groups={{0,1,32,33,64,65,96,97,128,129,160,161,192,193,224,225},{2,3,34,35,66,6..., dimensions={0} | all-to-all | bytes 458752 | tf_op jit(solution)/shard_map/all_to_all | solution.py:628
  73.2 4.4 %collective-permute-start.7 = (bf16[896,128]{1,0:T(8,128)(2,1)S(1)}, bf16[896,128]{1,0:T(8,128)(2,1)S(1)}, u32[]{:S(2)}, u32[]{:S(2)}) collective-permute-start(bf16[896,128]{1,0:T(8,128)(2,1)S(1)} %bitcast.17), channel_id=1, source_target_pairs={{0,16},{16,0},{32,48},{48,32},{64,80},{80,64},{96,112},{112,96},{1... | collective-permute-start | bytes 688136 | tf_op jit(solution)/shard_map/ppermute | solution.py:630
  77.5 1.5 %finish.3 = bf16[16,32,256]{2,1,0:T(8,128)(2,1)} custom-call(bf16[16,32,256]{2,1,0:T(8,128)(2,1)S(1)} %copy-done.1, bf16[18,48,256]{2,1,0:T(8,128)(2,1)S(1)} %get-tuple-element.39.rows, bf16[2304,256]{1,0:T(8,128)(2,1)S(1)} %get-tuple-element.31.bd.band), custom_call_target="tpu_custom_call" | custom-call | flops 1000000000 | bytes 1000000 | tf_op jit(solution)/shard_map/finish/pallas_call | solution.py:419
  79.1 0.0 collective-permute-done.7.other
  79.1 1.5 %unpack.1 = (f32[27,32,32]{2,1,0:T(8,128)}, f32[4,64,64]{2,1,0:T(8,128)}, f32[27,64,64]{2,1,0:T(8,128)}, f32[4,64,64]{2,1,0:T(8,128)}, f32[27,32,32]{2,1,0:T(8,128)}) custom-call(s32[1]{0:T(128)} %bitcast.core, bf16[896,128]{1,0:T(8,128)(2,1)S(1)} %bitcast.18, bf16[896,128]{1,0:T(8,128)(2,1)S(1)} %collective-permute-done.7.other), custom_call_target="tpu_custom_call" | custom-call | tf_op jit(solution)/shard_map/unpack/pallas_call | solution.py:514
  (18 shorter events, 0.2 us)
Async XLA Ops:
  0.6 15.7 %copy-start.4 = (bf16[3,3,3,32,32]{4,3,2,1,0:T(8,128)(2,1)S(1)}, bf16[3,3,3,32,32]{4,3,2,1,0:T(8,128)(2,1)}, u32[]{:S(2)}) copy-start(bf16[3,3,3,32,32]{4,3,2,1,0:T(8,128)(2,1)} %param.12) | copy-start | bytes 165892
  0.6 15.7 %copy-start.6 = (bf16[2,2,2,64,32]{3,4,2,1,0:T(8,128)(2,1)S(1)}, bf16[2,2,2,64,32]{3,4,2,1,0:T(8,128)(2,1)}, u32[]{:S(2)}) copy-start(bf16[2,2,2,64,32]{3,4,2,1,0:T(8,128)(2,1)} %param.11) | copy-start | bytes 98308
  0.7 15.7 %copy-start.2 = (bf16[3,3,3,64,64]{4,3,2,1,0:T(8,128)(2,1)S(1)}, bf16[3,3,3,64,64]{4,3,2,1,0:T(8,128)(2,1)}, u32[]{:S(2)}) copy-start(bf16[3,3,3,64,64]{4,3,2,1,0:T(8,128)(2,1)} %param.10) | copy-start | bytes 663556
  0.7 15.7 %copy-start.5 = (bf16[2,2,2,32,64]{4,3,2,1,0:T(8,128)(2,1)S(1)}, bf16[2,2,2,32,64]{4,3,2,1,0:T(8,128)(2,1)}, u32[]{:S(2)}) copy-start(bf16[2,2,2,32,64]{4,3,2,1,0:T(8,128)(2,1)} %param.9) | copy-start | bytes 98308
  0.7 15.7 %copy-start.3 = (bf16[3,3,3,32,32]{4,3,2,1,0:T(8,128)(2,1)S(1)}, bf16[3,3,3,32,32]{4,3,2,1,0:T(8,128)(2,1)}, u32[]{:S(2)}) copy-start(bf16[3,3,3,32,32]{4,3,2,1,0:T(8,128)(2,1)} %param.8) | copy-start | bytes 165892
  2.1 9.9 %collective-permute-start.2 = (bf16[12,16,256]{2,1,0:T(8,128)(2,1)S(1)}, bf16[12,16,256]{2,1,0:T(8,128)(2,1)S(1)}, u32[]{:S(2)}, u32[]{:S(2)}) collective-permute-start(bf16[12,16,256]{2,1,0:T(8,128)(2,1)S(1)} %get-tuple-element.29), channel_id=1, source_target_pairs={{0,1},{1,2},{2,3},{3,4},{4,5},{5,6},{6,7},{7,8},{8,9},{9,10},{10,1... | collective-permute-start | bytes 294920 | tf_op jit(solution)/shard_map/ppermute | solution.py:581
  4.2 7.8 %collective-permute-start.3 = (bf16[12,16,256]{2,1,0:T(8,128)(2,1)S(1)}, bf16[12,16,256]{2,1,0:T(8,128)(2,1)S(1)}, u32[]{:S(2)}, u32[]{:S(2)}) collective-permute-start(bf16[12,16,256]{2,1,0:T(8,128)(2,1)S(1)} %get-tuple-element.30), channel_id=1, source_target_pairs={{0,15},{1,0},{2,1},{3,2},{4,3},{5,4},{6,5},{7,6},{8,7},{9,8},{10,9... | collective-permute-start | bytes 294920 | tf_op jit(solution)/shard_map/ppermute | solution.py:582
  9.6 9.3 %collective-permute-start = (bf16[12,32,256]{2,1,0:T(8,128)(2,1)S(1)}, bf16[12,32,256]{2,1,0:T(8,128)(2,1)S(1)}, u32[]{:S(2)}, u32[]{:S(2)}) collective-permute-start(bf16[12,32,256]{2,1,0:T(8,128)(2,1)S(1)} %get-tuple-element.27), channel_id=1, source_target_pairs={{0,16},{16,32},{32,48},{48,64},{64,80},{80,96},{96,112},{112,128},... | collective-permute-start | bytes 589832 | tf_op jit(solution)/shard_map/ppermute | solution.py:583
  11.7 7.2 %collective-permute-start.1 = (bf16[12,32,256]{2,1,0:T(8,128)(2,1)S(1)}, bf16[12,32,256]{2,1,0:T(8,128)(2,1)S(1)}, u32[]{:S(2)}, u32[]{:S(2)}) collective-permute-start(bf16[12,32,256]{2,1,0:T(8,128)(2,1)S(1)} %get-tuple-element.28), channel_id=1, source_target_pairs={{0,240},{16,0},{32,16},{48,32},{64,48},{80,64},{96,80},{112,96},{1... | collective-permute-start | bytes 589832 | tf_op jit(solution)/shard_map/ppermute | solution.py:584
  12.1 5.8 %collective-permute-start.4 = (bf16[24,8,256]{2,1,0:T(8,128)(2,1)S(1)}, bf16[24,8,256]{2,1,0:T(8,128)(2,1)S(1)}, u32[]{:S(2)}, u32[]{:S(2)}) collective-permute-start(bf16[24,8,256]{2,1,0:T(8,128)(2,1)S(1)} %pad_maximum_fusion), channel_id=1, source_target_pairs={{0,16},{16,32},{32,48},{48,64},{64,80},{80,96},{96,112},{112,128},... | collective-permute-start | bytes 294920 | tf_op jit(solution)/shard_map/ppermute | solution.py:587
  14.6 4.3 %collective-permute-start.5 = (bf16[24,8,256]{2,1,0:T(8,128)(2,1)S(1)}, bf16[24,8,256]{2,1,0:T(8,128)(2,1)S(1)}, u32[]{:S(2)}, u32[]{:S(2)}) collective-permute-start(bf16[24,8,256]{2,1,0:T(8,128)(2,1)S(1)} %pad_maximum_fusion.1), channel_id=1, source_target_pairs={{0,240},{16,0},{32,16},{48,32},{64,48},{80,64},{96,80},{112,96},{1... | collective-permute-start | bytes 294920 | tf_op jit(solution)/shard_map/ppermute | solution.py:588
  16.4 2.5 %copy-start = (bf16[16,32,256]{2,1,0:T(8,128)(2,1)S(1)}, bf16[16,32,256]{2,1,0:T(8,128)(2,1)}, u32[]{:S(2)}) copy-start(bf16[16,32,256]{2,1,0:T(8,128)(2,1)} %base.2) | copy-start | bytes 786436
  16.4 2.5 %copy-start.1 = (bf16[16,32,256]{2,1,0:T(8,128)(2,1)S(1)}, bf16[16,32,256]{2,1,0:T(8,128)(2,1)}, u32[]{:S(2)}) copy-start(bf16[16,32,256]{2,1,0:T(8,128)(2,1)} %base.3) | copy-start | bytes 786436
  29.3 6.6 %collective-permute-start.6 = (bf16[896,128]{1,0:T(8,128)(2,1)S(1)}, bf16[896,128]{1,0:T(8,128)(2,1)S(1)}, u32[]{:S(2)}, u32[]{:S(2)}) collective-permute-start(bf16[896,128]{1,0:T(8,128)(2,1)S(1)} %get-tuple-element.36), channel_id=1, source_target_pairs={{0,16},{16,0},{32,48},{48,32},{64,80},{80,64},{96,112},{112,96},{1... | collective-permute-start | bytes 688136 | tf_op jit(solution)/shard_map/ppermute | solution.py:620
  73.2 5.9 %collective-permute-start.7 = (bf16[896,128]{1,0:T(8,128)(2,1)S(1)}, bf16[896,128]{1,0:T(8,128)(2,1)S(1)}, u32[]{:S(2)}, u32[]{:S(2)}) collective-permute-start(bf16[896,128]{1,0:T(8,128)(2,1)S(1)} %bitcast.17), channel_id=1, source_target_pairs={{0,16},{16,0},{32,48},{48,32},{64,80},{80,64},{96,112},{112,96},{1... | collective-permute-start | bytes 688136 | tf_op jit(solution)/shard_map/ppermute | solution.py:630
